TPU v7x, 128 devices: a whole 4x4x4 slice. The times are simulated.
128 devices in a mesh: ctx: 16 (over z, y), fsdp: 8 (over x, core).
Axes of the slice: x: 4, y: 4, z: 4, core: 2. Of those that a mesh axis runs over, the one named last changes fastest.
Arguments:
- tokens: bfloat16 [8, 2048, 1536], P('fsdp', 'ctx'), may hold values from -6 to 6
- cotangent: bfloat16 [8, 2048, 1536], P('fsdp', 'ctx'), may hold values from -6 to 6
- lengths: int32 [8], P('fsdp'), may hold values from 512 to 2048, as said below
- block_map: int32 [32], replicated, may hold values from 0 to 31, each once
- norm_gain: bfloat16 [1536], P('fsdp'), may hold values from 0.5 to 1.5
- w_query: bfloat16 [1536, 1536], P('fsdp'), may hold values from -0.15625 to 0.15625
- w_key: bfloat16 [1536, 1536], P('fsdp'), may hold values from -0.15625 to 0.15625
- w_value: bfloat16 [1536, 1536], P('fsdp'), may hold values from -0.15625 to 0.15625
- w_forget: bfloat16 [1536, 24], P('fsdp'), may hold values from -0.15625 to 0.15625
- forget_bias: bfloat16 [24], P('fsdp'), may hold values from 2 to 8
- w_outgate: bfloat16 [1536, 1536], P('fsdp'), may hold values from -0.15625 to 0.15625
- w_output: bfloat16 [1536, 1536], P('fsdp'), may hold values from -0.625 to 0.625
- ffn_gain: bfloat16 [1536], P('fsdp'), may hold values from 0.5 to 1.5
- w_gate: bfloat16 [1536, 4096], P('fsdp'), may hold values from -0.15625 to 0.15625
- w_up: bfloat16 [1536, 4096], P('fsdp'), may hold values from -0.15625 to 0.15625
- w_down: bfloat16 [4096, 1536], P('fsdp'), may hold values from -0.09375 to 0.09375
Outputs:
- mixed: bfloat16 [8, 2048, 1536], P('fsdp', 'ctx')
- tokens_grad: bfloat16 [8, 2048, 1536], P('fsdp', 'ctx')
- norm_gain_grad: float32 [1536], P('fsdp')
- w_query_grad: float32 [1536, 1536], P('fsdp')
- w_key_grad: float32 [1536, 1536], P('fsdp')
- w_value_grad: float32 [1536, 1536], P('fsdp')
- w_forget_grad: float32 [1536, 24], P('fsdp')
- forget_bias_grad: float32 [24], P('fsdp')
- w_outgate_grad: float32 [1536, 1536], P('fsdp')
- w_output_grad: float32 [1536, 1536], P('fsdp')
- ffn_gain_grad: float32 [1536], P('fsdp')
- w_gate_grad: float32 [1536, 4096], P('fsdp')
- w_up_grad: float32 [1536, 4096], P('fsdp')
- w_down_grad: float32 [4096, 1536], P('fsdp')
Inputs may be any that keep to these rules, and one draw needn't show every extreme that they name: `lengths`: each slot's sequence fills its first global positions; some slot is exactly 2048 long and another a quarter of 2048. A permutation: storage block b of every slot holds global block block_map[b].
All inputs are finite; a program needn't handle non-finite values.
Results may differ from a plain program's by a relative error of at most 0.023.
Values may be sent and summed in bfloat16 or wider, within the bound.
No kernel may reach another device: no remote copies, remote signals or barrier semaphores. Data moves between devices by JAX's collectives and lax.ppermute only.
A program may use at most 320 MiB of HBM per device.

v0:
```python
import math

import jax
import jax.numpy as jnp
from jax import lax
from jax.sharding import PartitionSpec as P

H = 24
HD = 64


EPS = 1e-06
NEG = -1e30


def reorder(matrix, fsdp_count, ctx_count):
    height, width = matrix.shape
    shaped = matrix.reshape(height, fsdp_count, ctx_count, width // (fsdp_count * ctx_count))
    return shaped.transpose(0, 2, 1, 3).reshape(height, width)


def outer_sum(left, right):
    return jnp.einsum("tr,tc->rc", left, right, preferred_element_type=jnp.float32)


def project_back(grad, weight):
    return jnp.einsum("tc,rc->tr", grad, weight, preferred_element_type=jnp.float32)


def norm_back(values, inv_root, gain, upstream):
    scaled = upstream * gain[None, :]
    gain_grad = jnp.sum(upstream * values * inv_root[:, None], 0)
    value_grad = inv_root[:, None] * scaled - values * (inv_root**3)[:, None] * jnp.mean(
        scaled * values, -1, keepdims=True
    )
    return (value_grad, gain_grad)


def decay_rows(logs, starts, block_len):
    count = starts.shape[0]
    summed = jnp.cumsum(logs.astype(jnp.float32).reshape(count, block_len, -1), 1)
    return (summed + starts[:, None, :]).reshape(count * block_len, -1)


def per_device(
    tokens,
    cotangent,
    lengths,
    block_map,
    norm_gain,
    w_query,
    w_key,
    w_value,
    w_forget,
    forget_bias,
    w_outgate,
    w_output,
    ffn_gain,
    w_gate,
    w_up,
    w_down,
):
    f32 = jnp.float32
    bf16 = jnp.bfloat16
    ctx_count = lax.axis_size("ctx")
    fsdp_count = lax.axis_size("fsdp")
    ctx_index = lax.axis_index("ctx")
    fsdp_index = lax.axis_index("fsdp")
    inputs = tokens[0].astype(f32)
    height = inputs.shape[0]
    block_len = height // 2
    block_count = block_map.shape[0]
    span = block_count * block_len
    scale = 1.0 / math.sqrt(HD)
    own_blocks = lax.dynamic_slice_in_dim(block_map, 2 * ctx_index, 2)
    offsets = jnp.arange(block_len, dtype=jnp.int32)
    query_pos = (own_blocks[:, None] * block_len + offsets[None, :]).reshape(height)
    key_pos = (block_map[:, None] * block_len + offsets[None, :]).reshape(span)
    live = (query_pos < lengths[0]).astype(f32)
    gain_first, query_w, key_w, value_w, forget_w, forget_b, outgate_w, output_w = (
        lax.all_gather(norm_gain, "fsdp", axis=0, tiled=True),
        lax.all_gather(w_query, "fsdp", axis=0, tiled=True),
        lax.all_gather(w_key, "fsdp", axis=0, tiled=True),
        lax.all_gather(w_value, "fsdp", axis=0, tiled=True),
        lax.all_gather(w_forget, "fsdp", axis=0, tiled=True),
        lax.all_gather(forget_bias, "fsdp", axis=0, tiled=True),
        lax.all_gather(w_outgate, "fsdp", axis=0, tiled=True),
        lax.all_gather(w_output, "fsdp", axis=0, tiled=True),
    )
    gain_first32 = gain_first.astype(f32)
    inv_first = lax.rsqrt(jnp.mean(inputs * inputs, -1) + EPS)
    normed = (inputs * inv_first[:, None] * gain_first32[None, :]).astype(bf16)
    queries = jnp.dot(normed, query_w, preferred_element_type=f32).astype(bf16)
    key_rows = jnp.dot(normed, key_w, preferred_element_type=f32).astype(bf16)
    value_rows = jnp.dot(normed, value_w, preferred_element_type=f32).astype(bf16)
    forget_pre = (
        jnp.dot(normed, forget_w, preferred_element_type=f32) + forget_b.astype(f32)[None, :]
    )
    log_keep = jax.nn.log_sigmoid(forget_pre).astype(bf16)
    gate_logit = jnp.dot(normed, outgate_w, preferred_element_type=f32)
    totals = jnp.sum(log_keep.astype(f32).reshape(2, block_len, -1), 1)
    all_totals = lax.all_gather(totals, "ctx", axis=0, tiled=True)
    earlier = block_map[None, :] < block_map[:, None]
    prefix = jnp.sum(jnp.where(earlier[:, :, None], all_totals[None, :, :], 0.0), 1)
    query_decay = decay_rows(
        log_keep, lax.dynamic_slice_in_dim(prefix, 2 * ctx_index, 2), block_len
    )
    keys, values, key_logs = (
        lax.all_gather(key_rows, "ctx", axis=0, tiled=True),
        lax.all_gather(value_rows, "ctx", axis=0, tiled=True),
        lax.all_gather(log_keep, "ctx", axis=0, tiled=True),
    )
    key_decay = decay_rows(key_logs, prefix, block_len)
    width_keys = math.gcd(span, 512)
    pieces = span // width_keys
    heads = queries.reshape(height, H, HD)
    decay_query_t = query_decay.T

    def scores(key_block, decay_block, pos_block):
        raw = jnp.einsum("qhd,khd->hqk", heads, key_block, preferred_element_type=f32) * scale
        raw = raw + decay_query_t[:, :, None] - decay_block.T[:, None, :]
        return jnp.where((query_pos[:, None] >= pos_block[None, :])[None], raw, NEG)

    decay_blocks = key_decay.reshape(pieces, width_keys, H)
    pos_blocks = key_pos.reshape(pieces, width_keys)

    def sweep_max(running, block):
        top, total = running
        scored = scores(block[0], block[1], block[2])
        new_top = jnp.maximum(top, jnp.max(scored, -1))
        total = total * jnp.exp(top - new_top) + jnp.sum(jnp.exp(scored - new_top[:, :, None]), -1)
        return ((new_top, total), None)

    start = (jnp.full((H, height), NEG, f32), jnp.zeros((H, height), f32))
    (top, total), unused = lax.scan(
        sweep_max, start, (keys.reshape(pieces, width_keys, H, HD), decay_blocks, pos_blocks)
    )
    log_total = top + jnp.log(total)

    def sweep_out(accum, block):
        probs = jnp.exp(scores(block[0], block[1], block[2]) - log_total[:, :, None]).astype(bf16)
        return (
            accum + jnp.einsum("hqk,khd->qhd", probs, block[3], preferred_element_type=f32),
            None,
        )

    attn_sum, unused = lax.scan(
        sweep_out,
        jnp.zeros((height, H, HD), f32),
        (
            keys.reshape(pieces, width_keys, H, HD),
            decay_blocks,
            pos_blocks,
            values.reshape(pieces, width_keys, H, HD),
        ),
    )
    attended = attn_sum.reshape(height, H * HD)
    gate_open = jax.nn.sigmoid(gate_logit)
    mixed_in = (attended * gate_open).astype(bf16)
    residual = inputs + jnp.dot(mixed_in, output_w, preferred_element_type=f32)
    gain_second, gate_w, up_w, down_w = (
        lax.all_gather(ffn_gain, "fsdp", axis=0, tiled=True),
        lax.all_gather(w_gate, "fsdp", axis=0, tiled=True),
        lax.all_gather(w_up, "fsdp", axis=0, tiled=True),
        lax.all_gather(w_down, "fsdp", axis=0, tiled=True),
    )
    gain_second32 = gain_second.astype(f32)
    inv_second = lax.rsqrt(jnp.mean(residual * residual, -1) + EPS)
    normed_two = (residual * inv_second[:, None] * gain_second32[None, :]).astype(bf16)
    gate_pre = jnp.dot(normed_two, gate_w, preferred_element_type=f32)
    up_pre = jnp.dot(normed_two, up_w, preferred_element_type=f32)
    hidden = (jax.nn.silu(gate_pre) * up_pre).astype(bf16)
    ffn_out = jnp.dot(hidden, down_w, preferred_element_type=f32)
    result = (live[:, None] * (residual + ffn_out)).astype(bf16)
    upstream = live[:, None] * cotangent[0].astype(f32)
    down_grad = upstream.astype(bf16)
    hidden_grad = project_back(down_grad, down_w)
    sig_gate = jax.nn.sigmoid(gate_pre)
    gate_grad = (hidden_grad * up_pre * sig_gate * (1.0 + gate_pre * (1.0 - sig_gate))).astype(bf16)
    up_grad = (hidden_grad * gate_pre * sig_gate).astype(bf16)
    left_two = reorder(normed_two, fsdp_count, ctx_count)
    left_hidden = reorder(hidden, fsdp_count, ctx_count)
    ffn_parts = (
        lax.psum_scatter(
            outer_sum(left_two, gate_grad), ("ctx", "fsdp"), scatter_dimension=0, tiled=True
        ),
        lax.psum_scatter(
            outer_sum(left_two, up_grad), ("ctx", "fsdp"), scatter_dimension=0, tiled=True
        ),
        lax.psum_scatter(
            outer_sum(left_hidden, down_grad), ("ctx", "fsdp"), scatter_dimension=0, tiled=True
        ),
    )
    normed_two_grad = project_back(gate_grad, gate_w) + project_back(up_grad, up_w)
    res_norm_grad, gain_second_grad = norm_back(
        residual, inv_second, gain_second32, normed_two_grad
    )
    residual_grad = upstream + res_norm_grad
    branch_grad = residual_grad.astype(bf16)
    mixed_grad = project_back(branch_grad, output_w)
    attended_grad = (mixed_grad * gate_open).astype(bf16)
    logit_grad = (mixed_grad * attended * gate_open * (1.0 - gate_open)).astype(bf16)
    attended_heads = attended_grad.reshape(height, H, HD)
    delta = jnp.sum((attended_grad.astype(f32) * attended).reshape(height, H, HD), -1).T
    keys_again, values_again = (
        lax.all_gather(key_rows, "ctx", axis=0, tiled=True),
        lax.all_gather(value_rows, "ctx", axis=0, tiled=True),
    )

    def sweep_back(running, block):
        query_grad, decay_grad = running
        key_block, value_block, decay_block, pos_block = block
        probs = jnp.exp(scores(key_block, decay_block, pos_block) - log_total[:, :, None])
        value_grad = jnp.einsum(
            "hqk,qhd->khd", probs.astype(bf16), attended_heads, preferred_element_type=f32
        )
        prob_grad = jnp.einsum(
            "qhd,khd->hqk", attended_heads, value_block, preferred_element_type=f32
        )
        score_grad = (probs * (prob_grad - delta[:, :, None])).astype(bf16)
        query_grad = (
            query_grad
            + jnp.einsum("hqk,khd->qhd", score_grad, key_block, preferred_element_type=f32) * scale
        )
        key_grad = jnp.einsum("hqk,qhd->khd", score_grad, heads, preferred_element_type=f32) * scale
        decay_grad = decay_grad + jnp.sum(score_grad, -1, dtype=f32)
        key_decay_grad = -jnp.sum(score_grad, 1, dtype=f32).T
        return ((query_grad, decay_grad), (key_grad, value_grad, key_decay_grad))

    begin = (jnp.zeros((height, H, HD), f32), jnp.zeros((H, height), f32))
    (query_sum, decay_sum), (key_terms, value_terms, key_decay_terms) = lax.scan(
        sweep_back,
        begin,
        (
            keys_again.reshape(pieces, width_keys, H, HD),
            values_again.reshape(pieces, width_keys, H, HD),
            decay_blocks,
            pos_blocks,
        ),
    )
    decay_all = key_decay_terms.reshape(span, H) + lax.dynamic_update_slice_in_dim(
        jnp.zeros((span, H), f32), decay_sum.T, ctx_index * height, 0
    )
    blocked = decay_all.reshape(block_count, block_len, H)
    within = jnp.flip(jnp.cumsum(jnp.flip(blocked, 1), 1), 1)
    later = block_map[None, :] > block_map[:, None]
    beyond = jnp.sum(jnp.where(later[:, :, None], jnp.sum(blocked, 1)[None, :, :], 0.0), 1)
    log_term = (within + beyond[:, None, :]).reshape(span, H)
    key_sum, value_sum, log_grad = (
        lax.psum_scatter(
            key_terms.reshape(span, H * HD).astype(jnp.bfloat16),
            "ctx",
            scatter_dimension=0,
            tiled=True,
        ).astype(jnp.float32),
        lax.psum_scatter(
            value_terms.reshape(span, H * HD).astype(jnp.bfloat16),
            "ctx",
            scatter_dimension=0,
            tiled=True,
        ).astype(jnp.float32),
        lax.psum_scatter(
            log_term.astype(jnp.bfloat16), "ctx", scatter_dimension=0, tiled=True
        ).astype(jnp.float32),
    )
    query_grad16 = query_sum.reshape(height, H * HD).astype(bf16)
    key_grad16 = key_sum.astype(bf16)
    value_grad16 = value_sum.astype(bf16)
    forget_grad = (log_grad * jax.nn.sigmoid(-forget_pre)).astype(bf16)
    left_one = reorder(normed, fsdp_count, ctx_count)
    left_mixed = reorder(mixed_in, fsdp_count, ctx_count)
    attn_parts = (
        lax.psum_scatter(
            outer_sum(left_one, query_grad16), ("ctx", "fsdp"), scatter_dimension=0, tiled=True
        ),
        lax.psum_scatter(
            outer_sum(left_one, key_grad16), ("ctx", "fsdp"), scatter_dimension=0, tiled=True
        ),
        lax.psum_scatter(
            outer_sum(left_one, value_grad16), ("ctx", "fsdp"), scatter_dimension=0, tiled=True
        ),
        lax.psum_scatter(
            outer_sum(left_one, forget_grad), ("ctx", "fsdp"), scatter_dimension=0, tiled=True
        ),
        lax.psum_scatter(
            outer_sum(left_one, logit_grad), ("ctx", "fsdp"), scatter_dimension=0, tiled=True
        ),
        lax.psum_scatter(
            outer_sum(left_mixed, branch_grad), ("ctx", "fsdp"), scatter_dimension=0, tiled=True
        ),
    )
    normed_grad = (
        project_back(query_grad16, query_w)
        + project_back(key_grad16, key_w)
        + project_back(value_grad16, value_w)
    )
    normed_grad = (
        normed_grad + project_back(forget_grad, forget_w) + project_back(logit_grad, outgate_w)
    )
    input_norm_grad, gain_first_grad = norm_back(inputs, inv_first, gain_first32, normed_grad)
    input_grad = (residual_grad + input_norm_grad).astype(bf16)
    bias_grad = jnp.sum(forget_grad, 0, dtype=f32)
    small = lax.psum((gain_first_grad, gain_second_grad, bias_grad), ("ctx", "fsdp"))
    summed = (
        attn_parts[0],
        attn_parts[1],
        attn_parts[2],
        attn_parts[3],
        attn_parts[4],
        attn_parts[5],
        ffn_parts[0],
        ffn_parts[1],
        ffn_parts[2],
    )
    shares = (
        lax.all_gather(summed[0].astype(jnp.bfloat16), "ctx", axis=0, tiled=True).astype(
            jnp.float32
        ),
        lax.all_gather(summed[1].astype(jnp.bfloat16), "ctx", axis=0, tiled=True).astype(
            jnp.float32
        ),
        lax.all_gather(summed[2].astype(jnp.bfloat16), "ctx", axis=0, tiled=True).astype(
            jnp.float32
        ),
        lax.all_gather(summed[3].astype(jnp.bfloat16), "ctx", axis=0, tiled=True).astype(
            jnp.float32
        ),
        lax.all_gather(summed[4].astype(jnp.bfloat16), "ctx", axis=0, tiled=True).astype(
            jnp.float32
        ),
        lax.all_gather(summed[5].astype(jnp.bfloat16), "ctx", axis=0, tiled=True).astype(
            jnp.float32
        ),
        lax.all_gather(summed[6].astype(jnp.bfloat16), "ctx", axis=0, tiled=True).astype(
            jnp.float32
        ),
        lax.all_gather(summed[7].astype(jnp.bfloat16), "ctx", axis=0, tiled=True).astype(
            jnp.float32
        ),
        lax.all_gather(summed[8].astype(jnp.bfloat16), "ctx", axis=0, tiled=True).astype(
            jnp.float32
        ),
    )
    gain_share = small[0].shape[0] // fsdp_count
    bias_share = small[2].shape[0] // fsdp_count
    first_share = lax.dynamic_slice_in_dim(small[0], fsdp_index * gain_share, gain_share)
    second_share = lax.dynamic_slice_in_dim(small[1], fsdp_index * gain_share, gain_share)
    bias_part = lax.dynamic_slice_in_dim(small[2], fsdp_index * bias_share, bias_share)
    return (
        result[None],
        input_grad[None],
        first_share,
        shares[0],
        shares[1],
        shares[2],
        shares[3],
        bias_part,
        shares[4],
        shares[5],
        second_share,
        shares[6],
        shares[7],
        shares[8],
    )


def solution(mesh):
    return jax.shard_map(
        per_device,
        mesh=mesh,
        in_specs=(
            P("fsdp", "ctx", None),
            P("fsdp", "ctx", None),
            P("fsdp"),
            P(),
            P("fsdp"),
            P("fsdp", None),
            P("fsdp", None),
            P("fsdp", None),
            P("fsdp", None),
            P("fsdp"),
            P("fsdp", None),
            P("fsdp", None),
            P("fsdp"),
            P("fsdp", None),
            P("fsdp", None),
            P("fsdp", None),
        ),
        out_specs=(
            P("fsdp", "ctx", None),
            P("fsdp", "ctx", None),
            P("fsdp"),
            P("fsdp", None),
            P("fsdp", None),
            P("fsdp", None),
            P("fsdp", None),
            P("fsdp"),
            P("fsdp", None),
            P("fsdp", None),
            P("fsdp"),
            P("fsdp", None),
            P("fsdp", None),
            P("fsdp", None),
        ),
        check_vma=False,
    )
```

profile of v0, /device:TPU:1, one launch (start us, length us, event | category | flops | bytes accessed | tf_op | source)
XLA Modules:
  0.0 3455.5 jit_solution(10344335818912814920)
XLA Ops:
  14.6 24.0 all-reduce.20
  52.3 31.7 all-gather.28.cloned.1.call-done
  91.9 12.8 all-gather
  106.2 19.2 all-gather.1
  126.4 18.5 all_gather.86
  152.2 31.8 all-gather.26.cloned.1.call-done
  184.0 16.3 reshape.423
  200.3 14.1 copy.224
  214.4 33.2 all-gather.30.cloned.1.call-done
  247.6 16.3 reshape.424
  263.9 14.1 copy.225
  278.1 45.7 %while.43 = (s32[]{:T(128)}, f32[24,128]{1,0:T(8,128)S(1)}, f32[24,128]{1,0:T(8,128)S(1)}, s32[4,512]{1,0:T(4,128)S(1)}, bf16[4,512,24,64]{1,3,2,0:T(8,128)(2,1)...) while((s32[]{:T(128)}, f32[24,128]{1,0:T(8,128)S(1)}, ...), condition=%wide.region_8.9_spmd.clone, body=%wide.region_5.8_spmd.clone.sunk | while | flops 218709120 | bytes 15134868 | solution.py:135
  323.8 26.0 while.44
  358.5 30.0 all-gather.38.cloned.1.call-done
  396.2 61.7 %all-gather.40.cloned.1.call-done = bf16[1536,4096]{1,0:T(8,128)(2,1)} async-done(((bf16[192,4096]{1,0:T(8,128)(2,1)}), bf16[1536,4096]{1,0:T(8,128)(2,1)}) %all-gather.40.cloned.1.call-update) | async-done | bytes 12582928 | tf_op jit(solution)/shard_map/all_gather | solution.py:164
  465.6 61.6 %all-gather.42.cloned.1.call-done = bf16[4096,1536]{1,0:T(8,128)(2,1)} async-done(((bf16[512,1536]{1,0:T(8,128)(2,1)}), bf16[4096,1536]{1,0:T(8,128)(2,1)}) %all-gather.42.cloned.1.call-update) | async-done | bytes 12582928 | tf_op jit(solution)/shard_map/all_gather | solution.py:165
  527.2 11.8 multiply_convert_fusion
  564.6 111.2 %while.45 = (s32[]{:T(128)}, f32[128,24,64]{0,2,1:T(8,128)}, f32[24,128]{1,0:T(8,128)S(1)}, bf16[4,512,24,64]{1,3,2,0:T(8,128)(2,1)}, bf16[4,512,24,64]{1,3,2,0:...) while((s32[]{:T(128)}, f32[128,24,64]{0,2,1:T(8,128)}, ...), condition=%wide.region_17.18_spmd.clone, body=%wide.region_14.17_spmd.clone.sunk | while | flops 1034816640 | bytes 71144040 | solution.py:231
  686.3 14.6 copy.264
  700.8 16.9 reshape.417
  717.8 14.4 copy.265
  732.2 16.9 reshape.419
  766.0 411.0 %fusion.135 = (f32[16,1536]{1,0:T(8,128)S(1)}, f32[16,4096]{1,0:T(8,128)S(1)}) fusion(f32[1536,1536]{1,0:T(8,128)} %fusion.113, f32[1536,4096]{1,0:T(8,128)} %fusion.155), kind=kCustom, calls=%all-reduce-scatter.9 | all-reduce-scatter fusion | flops 11534337 | bytes 34963456
  1191.5 14.1 collective-permute-start.214
  1222.9 15.0 collective-permute-start.209
  1255.2 11.5 collective-permute-start.202
  1305.2 81.3 %concatenate.6 = bf16[524,4096]{1,0:T(8,128)(2,1)} concatenate(bf16[12,4096]{1,0:T(8,128)(2,1)S(1)} %collective-permute-done.223, bf16[16,4096]{1,0:T(8,128)(2,1)S(1)} %collective-permute-done.222, bf16[16,4096]{1,0:T(8,128)(2,1)S(1)} %collective-permute-done.221, bf16[16,4096]{1,0:T(8,128)(2,1)S(1)} %collective-permute-done.220, bf16[16,4096]{1,0:T(8,128)(2,1)S(1)} %collective-permute-done.219, ...), dimensions={0} | concatenate | bytes 8716288
  1388.2 360.4 %fusion.13 = f32[16,4096]{1,0:T(8,128)S(1)} fusion(f32[1536,4096]{1,0:T(8,128)} %fusion.156), kind=kCustom, calls=%all-reduce-scatter.7 | all-reduce-scatter fusion | flops 8388609 | bytes 25427968
  1789.4 13.5 collective-permute-start.241
  1821.5 11.5 collective-permute-start.234
  1864.5 81.3 %concatenate.7 = bf16[524,4096]{1,0:T(8,128)(2,1)} concatenate(bf16[12,4096]{1,0:T(8,128)(2,1)S(1)} %collective-permute-done.255, bf16[16,4096]{1,0:T(8,128)(2,1)S(1)} %collective-permute-done.254, bf16[16,4096]{1,0:T(8,128)(2,1)S(1)} %collective-permute-done.253, bf16[16,4096]{1,0:T(8,128)(2,1)S(1)} %collective-permute-done.252, bf16[16,4096]{1,0:T(8,128)(2,1)S(1)} %collective-permute-done.251, ...), dimensions={0} | concatenate | bytes 8716288
  1967.6 10.8 collective-permute-start.190
  2086.8 438.9 %fusion.134 = (f32[16,1536]{1,0:T(8,128)S(1)}, f32[16,1536]{1,0:T(8,128)S(1)}, f32[16,1536]{1,0:T(8,128)S(1)}, f32[16,24]{1,0:T(8,128)S(1)}, f32[16,1536]{1,0:T(8,128)S(1)}) fusion(f32[1536,1536]{1,0:T(8,128)} %fusion.150, f32[1536,1536]{1,0:T(8,128)} %fusion.151, f32[1536,1536]{1,0:T(8,128)} %fusion.152, f32[1536,24]{1,0:T(8,128)} %fusion.153, ...), kind=kCustom, calls=%all-reduce-scatter.8 | all-reduce-scatter fusion | flops 12632065 | bytes 38290944
  2688.9 10.7 collective-permute-start.30
  2844.7 48.7 %concatenate.5 = bf16[524,1536]{1,0:T(8,128)(2,1)} concatenate(bf16[12,1536]{1,0:T(8,128)(2,1)S(1)} %copy-done.59, bf16[16,1536]{1,0:T(8,128)(2,1)} %collective-permute-done.190, bf16[16,1536]{1,0:T(8,128)(2,1)S(1)} %copy-done.57, bf16[16,1536]{1,0:T(8,128)(2,1)} %collective-permute-done.188, bf16[16,1536]{1,0:T(8,128)(2,1)} %collective-permute-done.187, ...), dimensions={0} | concatenate | bytes 3268608
  2921.8 16.3 all-gather.7
  3037.5 64.1 %all-reduce.19 = (f32[1536]{0:T(1024)S(1)}, f32[24]{0:T(128)S(1)}, f32[1536]{0:T(1024)S(1)}) all-reduce(f32[1536]{0:T(1024)S(1)} %get-tuple-element.559, f32[24]{0:T(128)} %get-tuple-element.651, f32[1536]{0:T(1024)} %get-tuple-element.557), channel_id=1, replica_groups=mesh['ctx'=16,'fsdp'=8] {'ctx','fsdp'}, use_global_device_ids=true, to_apply=%region_26.27 | all-reduce | flops 3096 | bytes 24768 | tf_op jit(solution)/shard_map/psum | solution.py:303
  3103.5 24.7 concatenate.3
  3143.9 17.9 all-gather.5
  3182.6 26.7 concatenate
  3228.6 22.2 concatenate.1
  3261.5 19.9 concatenate.2
  3309.2 17.8 all-gather.2
  3346.7 17.8 all-gather.3
  3364.5 11.0 collective-permute-start.132
  3388.2 20.6 all-gather.4
  3412.2 13.9 concatenate.4
  3426.2 17.7 all-gather.6
  (1284 shorter events, 1173.8 us)
Async XLA Ops:
  7.9 76.1 %all-gather.28.cloned.1.call-start = ((), (), s32[]{:S(2)}) async-start(), calls=%async_computation.6 | async-start | bytes 5308416 | tf_op jit(solution)/shard_map/all_gather | solution.py:83
  8.7 140.1 %all-gather.32.cloned.1.call-start = ((), (), s32[]{:S(2)}) async-start(), calls=%async_computation.8 | async-start | bytes 5308416 | tf_op jit(solution)/shard_map/all_gather | solution.py:82
  9.4 174.6 %all-gather.26.cloned.1.call-start = ((), (), s32[]{:S(2)}) async-start(), calls=%async_computation.5 | async-start | bytes 6684672 | tf_op jit(solution)/shard_map/all_gather | solution.py:110
  52.2 195.3 %all-gather.30.cloned.1.call-start = ((), (), s32[]{:S(2)}) async-start(), calls=%async_computation.7 | async-start | bytes 6684672 | tf_op jit(solution)/shard_map/all_gather | solution.py:109
  88.0 262.4 %all-gather.34.cloned.1.call-start = ((), (), s32[]{:S(2)}) async-start(), calls=%async_computation.9 | async-start | bytes 5308416 | tf_op jit(solution)/shard_map/all_gather | solution.py:87
  88.6 266.3 %all-gather.36.cloned.1.call-start = ((), (), s32[]{:S(2)}) async-start(), calls=%async_computation.10 | async-start | bytes 5308416 | tf_op jit(solution)/shard_map/all_gather | solution.py:88
  89.3 299.1 %all-gather.38.cloned.1.call-start = ((), (), s32[]{:S(2)}) async-start(), calls=%async_computation.11 | async-start | bytes 14155776 | tf_op jit(solution)/shard_map/all_gather | solution.py:163
  90.1 367.8 %all-gather.40.cloned.1.call-start = ((), (), s32[]{:S(2)}) async-start(), calls=%async_computation.12 | async-start | bytes 14155776 | tf_op jit(solution)/shard_map/all_gather | solution.py:164
  90.8 436.4 %all-gather.42.cloned.1.call-start = ((), (), s32[]{:S(2)}) async-start(), calls=%async_computation.13 | async-start | bytes 14155776 | tf_op jit(solution)/shard_map/all_gather | solution.py:165
  91.4 1911.1 %reduce-scatter.33.cloned.1.call-start = ((), (), s32[]{:S(2)}) async-start(), calls=%async_computation.20 | async-start | bytes 557056
  686.2 1362.3 %reduce-scatter.29.cloned.1.call-start = ((), (), s32[]{:S(2)}) async-start(), calls=%async_computation.18 | async-start | bytes 6684672
  717.7 1349.2 %reduce-scatter.31.cloned.1.call-start = ((), (), s32[]{:S(2)}) async-start(), calls=%async_computation.19 | async-start | bytes 6684672
  749.1 2190.1 %all-gather.46.cloned.1.call-start = ((), (), s32[]{:S(2)}) async-start(), calls=%async_computation.16 | async-start | bytes 2228224 | tf_op jit(solution)/shard_map/all_gather | solution.py:334
  1388.2 1554.8 %all-gather.48.cloned.1.call-start = ((), (), s32[]{:S(2)}) async-start(), calls=%async_computation.17 | async-start | bytes 2228224 | tf_op jit(solution)/shard_map/all_gather | solution.py:337
  1947.5 1027.4 %reduce-scatter.27.cloned.1.call-start = ((), (), s32[]{:S(2)}) async-start(), calls=%async_computation.14 | async-start | bytes 25362432 | tf_op jit(solution)/shard_map/reduce_scatter | solution.py:190
  1959.1 1486.0 %all-gather.44.cloned.1.call-start = ((), (), s32[]{:S(2)}) async-start(), calls=%async_computation.15 | async-start | bytes 1671168 | tf_op jit(solution)/shard_map/all_gather | solution.py:340
  2073.1 452.7 %collective-permute-start.164 = (bf16[16,1536]{1,0:T(8,128)(2,1)}, bf16[16,1536]{1,0:T(8,128)(2,1)}, u32[]{:S(2)}, u32[]{:S(2)}) collective-permute-start(bf16[16,1536]{1,0:T(8,128)(2,1)} %convert.551), channel_id=1, source_target_pairs={{0,5},{1,6},{2,7},{3,8},{4,9},{5,10},{6,11},{7,12},{8,13},{9,14},{... | collective-permute-start | bytes 147464
  2075.4 451.6 %collective-permute-start.163 = (bf16[16,1536]{1,0:T(8,128)(2,1)}, bf16[16,1536]{1,0:T(8,128)(2,1)}, u32[]{:S(2)}, u32[]{:S(2)}) collective-permute-start(bf16[16,1536]{1,0:T(8,128)(2,1)} %convert.551), channel_id=1, source_target_pairs={{0,4},{1,5},{2,6},{3,7},{4,8},{5,9},{6,10},{7,11},{8,12},{9,13},{1... | collective-permute-start | bytes 147464
  2078.3 457.8 %collective-permute-start.162 = (bf16[16,1536]{1,0:T(8,128)(2,1)}, bf16[16,1536]{1,0:T(8,128)(2,1)}, u32[]{:S(2)}, u32[]{:S(2)}) collective-permute-start(bf16[16,1536]{1,0:T(8,128)(2,1)} %convert.551), channel_id=1, source_target_pairs={{0,3},{1,4},{2,5},{3,6},{4,7},{5,8},{6,9},{7,10},{8,11},{9,12},{10... | collective-permute-start | bytes 147464
  2082.1 464.3 %collective-permute-start.161 = (bf16[16,1536]{1,0:T(8,128)(2,1)}, bf16[16,1536]{1,0:T(8,128)(2,1)}, u32[]{:S(2)}, u32[]{:S(2)}) collective-permute-start(bf16[16,1536]{1,0:T(8,128)(2,1)} %convert.551), channel_id=1, source_target_pairs={{0,2},{1,3},{2,4},{3,5},{4,6},{5,7},{6,8},{7,9},{8,10},{9,11},{10,... | collective-permute-start | bytes 147464
  2084.3 465.7 %collective-permute-start.160 = (bf16[16,1536]{1,0:T(8,128)(2,1)}, bf16[16,1536]{1,0:T(8,128)(2,1)}, u32[]{:S(2)}, u32[]{:S(2)}) collective-permute-start(bf16[16,1536]{1,0:T(8,128)(2,1)} %convert.551), channel_id=1, source_target_pairs={{0,1},{1,2},{2,3},{3,4},{4,5},{5,6},{6,7},{7,8},{8,9},{9,10},{10,1... | collective-permute-start | bytes 147464
  2525.8 178.1 %collective-permute-start.31 = (bf16[12,1536]{1,0:T(8,128)(2,1)S(1)}, bf16[12,1536]{1,0:T(8,128)(2,1)S(1)}, u32[]{:S(2)}, u32[]{:S(2)}) collective-permute-start(bf16[12,1536]{1,0:T(8,128)(2,1)S(1)} %slice), channel_id=1, source_target_pairs={{0,32},{1,33},{2,34},{3,35},{4,36},{5,37},{6,38},{7,39},{8,40},{9,... | collective-permute-start | bytes 110600
  2527.1 178.1 %collective-permute-start.63 = (bf16[12,1536]{1,0:T(8,128)(2,1)S(1)}, bf16[12,1536]{1,0:T(8,128)(2,1)S(1)}, u32[]{:S(2)}, u32[]{:S(2)}) collective-permute-start(bf16[12,1536]{1,0:T(8,128)(2,1)S(1)} %slice.1), channel_id=1, source_target_pairs={{0,32},{1,33},{2,34},{3,35},{4,36},{5,37},{6,38},{7,39},{8,40},{9,... | collective-permute-start | bytes 110600
  2536.1 171.1 %collective-permute-start.95 = (bf16[12,1536]{1,0:T(8,128)(2,1)S(1)}, bf16[12,1536]{1,0:T(8,128)(2,1)S(1)}, u32[]{:S(2)}, u32[]{:S(2)}) collective-permute-start(bf16[12,1536]{1,0:T(8,128)(2,1)S(1)} %slice.2), channel_id=1, source_target_pairs={{0,32},{1,33},{2,34},{3,35},{4,36},{5,37},{6,38},{7,39},{8,40},{9,... | collective-permute-start | bytes 110600
  2830.4 62.9 %collective-permute-start.49 = (bf16[16,1536]{1,0:T(8,128)(2,1)}, bf16[16,1536]{1,0:T(8,128)(2,1)S(1)}, u32[]{:S(2)}, u32[]{:S(2)}) collective-permute-start(bf16[16,1536]{1,0:T(8,128)(2,1)} %convert.554), channel_id=1, source_target_pairs={{0,18},{1,19},{2,20},{3,21},{4,22},{5,23},{6,24},{7,25},{8,26},{9,... | collective-permute-start | bytes 147464
  2832.4 63.8 %collective-permute-start.48 = (bf16[16,1536]{1,0:T(8,128)(2,1)}, bf16[16,1536]{1,0:T(8,128)(2,1)S(1)}, u32[]{:S(2)}, u32[]{:S(2)}) collective-permute-start(bf16[16,1536]{1,0:T(8,128)(2,1)} %convert.554), channel_id=1, source_target_pairs={{0,17},{1,18},{2,19},{3,20},{4,21},{5,22},{6,23},{7,24},{8,25},{9,... | collective-permute-start | bytes 147464
  2834.0 64.9 %collective-permute-start.47 = (bf16[16,1536]{1,0:T(8,128)(2,1)}, bf16[16,1536]{1,0:T(8,128)(2,1)S(1)}, u32[]{:S(2)}, u32[]{:S(2)}) collective-permute-start(bf16[16,1536]{1,0:T(8,128)(2,1)} %convert.554), channel_id=1, source_target_pairs={{0,16},{1,17},{2,18},{3,19},{4,20},{5,21},{6,22},{7,23},{8,24},{9,... | collective-permute-start | bytes 147464
  2835.6 67.4 %collective-permute-start.46 = (bf16[16,1536]{1,0:T(8,128)(2,1)}, bf16[16,1536]{1,0:T(8,128)(2,1)S(1)}, u32[]{:S(2)}, u32[]{:S(2)}) collective-permute-start(bf16[16,1536]{1,0:T(8,128)(2,1)} %convert.554), channel_id=1, source_target_pairs={{0,15},{1,16},{2,17},{3,18},{4,19},{5,20},{6,21},{7,22},{8,23},{9,... | collective-permute-start | bytes 147464
  2838.8 65.5 %collective-permute-start.45 = (bf16[16,1536]{1,0:T(8,128)(2,1)}, bf16[16,1536]{1,0:T(8,128)(2,1)S(1)}, u32[]{:S(2)}, u32[]{:S(2)}) collective-permute-start(bf16[16,1536]{1,0:T(8,128)(2,1)} %convert.554), channel_id=1, source_target_pairs={{0,14},{1,15},{2,16},{3,17},{4,18},{5,19},{6,20},{7,21},{8,22},{9,... | collective-permute-start | bytes 147464
  2909.7 46.6 %collective-permute-start.38 = (bf16[16,1536]{1,0:T(8,128)(2,1)}, bf16[16,1536]{1,0:T(8,128)(2,1)}, u32[]{:S(2)}, u32[]{:S(2)}) collective-permute-start(bf16[16,1536]{1,0:T(8,128)(2,1)} %convert.554), channel_id=1, source_target_pairs={{0,7},{1,8},{2,9},{3,10},{4,11},{5,12},{6,13},{7,14},{8,15},{9,16}... | collective-permute-start | bytes 147464
  2912.0 46.8 %collective-permute-start.37 = (bf16[16,1536]{1,0:T(8,128)(2,1)}, bf16[16,1536]{1,0:T(8,128)(2,1)}, u32[]{:S(2)}, u32[]{:S(2)}) collective-permute-start(bf16[16,1536]{1,0:T(8,128)(2,1)} %convert.554), channel_id=1, source_target_pairs={{0,6},{1,7},{2,8},{3,9},{4,10},{5,11},{6,12},{7,13},{8,14},{9,15},... | collective-permute-start | bytes 147464
  2916.3 44.4 %collective-permute-start.36 = (bf16[16,1536]{1,0:T(8,128)(2,1)}, bf16[16,1536]{1,0:T(8,128)(2,1)}, u32[]{:S(2)}, u32[]{:S(2)}) collective-permute-start(bf16[16,1536]{1,0:T(8,128)(2,1)} %convert.554), channel_id=1, source_target_pairs={{0,5},{1,6},{2,7},{3,8},{4,9},{5,10},{6,11},{7,12},{8,13},{9,14},{... | collective-permute-start | bytes 147464
  2918.2 46.2 %collective-permute-start.35 = (bf16[16,1536]{1,0:T(8,128)(2,1)}, bf16[16,1536]{1,0:T(8,128)(2,1)}, u32[]{:S(2)}, u32[]{:S(2)}) collective-permute-start(bf16[16,1536]{1,0:T(8,128)(2,1)} %convert.554), channel_id=1, source_target_pairs={{0,4},{1,5},{2,6},{3,7},{4,8},{5,9},{6,10},{7,11},{8,12},{9,13},{1... | collective-permute-start | bytes 147464
  3023.4 104.8 %collective-permute-start.77 = (bf16[16,1536]{1,0:T(8,128)(2,1)}, bf16[16,1536]{1,0:T(8,128)(2,1)S(1)}, u32[]{:S(2)}, u32[]{:S(2)}) collective-permute-start(bf16[16,1536]{1,0:T(8,128)(2,1)} %convert.553), channel_id=1, source_target_pairs={{0,14},{1,15},{2,16},{3,17},{4,18},{5,19},{6,20},{7,21},{8,22},{9,... | collective-permute-start | bytes 147464
  3024.7 105.8 %collective-permute-start.76 = (bf16[16,1536]{1,0:T(8,128)(2,1)}, bf16[16,1536]{1,0:T(8,128)(2,1)S(1)}, u32[]{:S(2)}, u32[]{:S(2)}) collective-permute-start(bf16[16,1536]{1,0:T(8,128)(2,1)} %convert.553), channel_id=1, source_target_pairs={{0,13},{1,14},{2,15},{3,16},{4,17},{5,18},{6,19},{7,20},{8,21},{9,... | collective-permute-start | bytes 147464
  3027.0 105.8 %collective-permute-start.75 = (bf16[16,1536]{1,0:T(8,128)(2,1)}, bf16[16,1536]{1,0:T(8,128)(2,1)S(1)}, u32[]{:S(2)}, u32[]{:S(2)}) collective-permute-start(bf16[16,1536]{1,0:T(8,128)(2,1)} %convert.553), channel_id=1, source_target_pairs={{0,12},{1,13},{2,14},{3,15},{4,16},{5,17},{6,18},{7,19},{8,20},{9,... | collective-permute-start | bytes 147464
  3030.5 105.7 %collective-permute-start.74 = (bf16[16,1536]{1,0:T(8,128)(2,1)}, bf16[16,1536]{1,0:T(8,128)(2,1)S(1)}, u32[]{:S(2)}, u32[]{:S(2)}) collective-permute-start(bf16[16,1536]{1,0:T(8,128)(2,1)} %convert.553), channel_id=1, source_target_pairs={{0,11},{1,12},{2,13},{3,14},{4,15},{5,16},{6,17},{7,18},{8,19},{9,... | collective-permute-start | bytes 147464
  3034.3 105.8 %collective-permute-start.73 = (bf16[16,1536]{1,0:T(8,128)(2,1)}, bf16[16,1536]{1,0:T(8,128)(2,1)S(1)}, u32[]{:S(2)}, u32[]{:S(2)}) collective-permute-start(bf16[16,1536]{1,0:T(8,128)(2,1)} %convert.553), channel_id=1, source_target_pairs={{0,10},{1,11},{2,12},{3,13},{4,14},{5,15},{6,16},{7,17},{8,18},{9,... | collective-permute-start | bytes 147464
  3161.7 47.6 %collective-permute-start.67 = (bf16[16,1536]{1,0:T(8,128)(2,1)}, bf16[16,1536]{1,0:T(8,128)(2,1)}, u32[]{:S(2)}, u32[]{:S(2)}) collective-permute-start(bf16[16,1536]{1,0:T(8,128)(2,1)} %convert.553), channel_id=1, source_target_pairs={{0,4},{1,5},{2,6},{3,7},{4,8},{5,9},{6,10},{7,11},{8,12},{9,13},{1... | collective-permute-start | bytes 147464
  3168.1 47.4 %collective-permute-start.66 = (bf16[16,1536]{1,0:T(8,128)(2,1)}, bf16[16,1536]{1,0:T(8,128)(2,1)}, u32[]{:S(2)}, u32[]{:S(2)}) collective-permute-start(bf16[16,1536]{1,0:T(8,128)(2,1)} %convert.553), channel_id=1, source_target_pairs={{0,3},{1,4},{2,5},{3,6},{4,7},{5,8},{6,9},{7,10},{8,11},{9,12},{10... | collective-permute-start | bytes 147464
  3173.9 45.0 %collective-permute-start.65 = (bf16[16,1536]{1,0:T(8,128)(2,1)}, bf16[16,1536]{1,0:T(8,128)(2,1)}, u32[]{:S(2)}, u32[]{:S(2)}) collective-permute-start(bf16[16,1536]{1,0:T(8,128)(2,1)} %convert.553), channel_id=1, source_target_pairs={{0,2},{1,3},{2,4},{3,5},{4,6},{5,7},{6,8},{7,9},{8,10},{9,11},{10,... | collective-permute-start | bytes 147464
  3176.7 47.3 %collective-permute-start.64 = (bf16[16,1536]{1,0:T(8,128)(2,1)}, bf16[16,1536]{1,0:T(8,128)(2,1)}, u32[]{:S(2)}, u32[]{:S(2)}) collective-permute-start(bf16[16,1536]{1,0:T(8,128)(2,1)} %convert.553), channel_id=1, source_target_pairs={{0,1},{1,2},{2,3},{3,4},{4,5},{5,6},{6,7},{7,8},{8,9},{9,10},{10,1... | collective-permute-start | bytes 147464
  3178.9 48.0 %collective-permute-start.158 = (bf16[16,1536]{1,0:T(8,128)(2,1)S(1)}, bf16[16,1536]{1,0:T(8,128)(2,1)S(1)}, u32[]{:S(2)}, u32[]{:S(2)}) collective-permute-start(bf16[16,1536]{1,0:T(8,128)(2,1)S(1)} %convert.552), channel_id=1, source_target_pairs={{0,31},{1,32},{2,33},{3,34},{4,35},{5,36},{6,37},{7,38},{8,39},{9,... | collective-permute-start | bytes 147464
  3329.7 45.8 %collective-permute-start.136 = (bf16[16,1536]{1,0:T(8,128)(2,1)S(1)}, bf16[16,1536]{1,0:T(8,128)(2,1)S(1)}, u32[]{:S(2)}, u32[]{:S(2)}) collective-permute-start(bf16[16,1536]{1,0:T(8,128)(2,1)S(1)} %convert.552), channel_id=1, source_target_pairs={{0,9},{1,10},{2,11},{3,12},{4,13},{5,14},{6,15},{7,16},{8,17},{9,1... | collective-permute-start | bytes 147464
  3336.2 43.0 %collective-permute-start.135 = (bf16[16,1536]{1,0:T(8,128)(2,1)S(1)}, bf16[16,1536]{1,0:T(8,128)(2,1)S(1)}, u32[]{:S(2)}, u32[]{:S(2)}) collective-permute-start(bf16[16,1536]{1,0:T(8,128)(2,1)S(1)} %convert.552), channel_id=1, source_target_pairs={{0,8},{1,9},{2,10},{3,11},{4,12},{5,13},{6,14},{7,15},{8,16},{9,17... | collective-permute-start | bytes 147464
  3340.1 41.6 %collective-permute-start.134 = (bf16[16,1536]{1,0:T(8,128)(2,1)S(1)}, bf16[16,1536]{1,0:T(8,128)(2,1)S(1)}, u32[]{:S(2)}, u32[]{:S(2)}) collective-permute-start(bf16[16,1536]{1,0:T(8,128)(2,1)S(1)} %convert.552), channel_id=1, source_target_pairs={{0,7},{1,8},{2,9},{3,10},{4,11},{5,12},{6,13},{7,14},{8,15},{9,16}... | collective-permute-start | bytes 147464
  3341.6 42.9 %collective-permute-start.133 = (bf16[16,1536]{1,0:T(8,128)(2,1)S(1)}, bf16[16,1536]{1,0:T(8,128)(2,1)S(1)}, u32[]{:S(2)}, u32[]{:S(2)}) collective-permute-start(bf16[16,1536]{1,0:T(8,128)(2,1)S(1)} %convert.552), channel_id=1, source_target_pairs={{0,6},{1,7},{2,8},{3,9},{4,10},{5,11},{6,12},{7,13},{8,14},{9,15},... | collective-permute-start | bytes 147464
  3364.5 47.6 %collective-permute-start.132 = (bf16[16,1536]{1,0:T(8,128)(2,1)S(1)}, bf16[16,1536]{1,0:T(8,128)(2,1)}, u32[]{:S(2)}, u32[]{:S(2)}) collective-permute-start(bf16[16,1536]{1,0:T(8,128)(2,1)S(1)} %convert.552), channel_id=1, source_target_pairs={{0,5},{1,6},{2,7},{3,8},{4,9},{5,10},{6,11},{7,12},{8,13},{9,14},{... | collective-permute-start | bytes 147464
  (455 other events, 21663.2 us)
Sparse Core Ops, SparseCore 0:
  9.7 38.4 all-gather.23
  49.9 34.1 all-gather.27
  85.7 34.4 all-gather.31
  122.8 61.1 all-gather.25
  186.5 60.9 all-gather.29
  249.1 34.2 all-gather.33
  285.1 34.2 all-gather.35
  321.1 67.3 all-gather.37
  390.2 67.6 all-gather.39
  459.4 67.6 all-gather.41
  686.3 70.7 reduce-scatter.32
  760.8 187.2 reduce-scatter.28
  951.9 141.2 reduce-scatter.30
  1388.3 69.2 all-gather.45
  1947.6 47.6 all-gather.47
  2001.4 277.4 reduce-scatter.26
  2976.7 42.3 all-gather.43
where the time goes:
time: 3490 us; the launch traced here: 3460 us
  blocking collectives  1460 us (42%)
  starting transfers between devices  856 us (25%)
  local copies, waits for them, and re-layouts  510 us (15%)
  matrix products  289 us (8%)
  waiting for transfers between devices  271 us (8%)
  other arithmetic  49.3 us (1%)
    unnamed x4, blocking collectives  1230 us
    unnamed x259, starting transfers between devices  856 us
    unnamed x407, local copies, waits for them, and re-layouts  427 us
  transfers between devices with their start and end apart: 273, of which 14 were waited for; matrix products, arithmetic and copies ran while one was open for 55% of the time, Pallas kernels for 0%

commit v1 on v0

v1 whole, which is shorter than its diff:
```python
import jax
import jax.numpy as jnp
from jax import lax
from jax.experimental import pallas as pl
from jax.experimental.pallas import tpu as pltpu
from jax.sharding import PartitionSpec as P

EPS = 1e-06
NEG = -1e30
HD = 64
QB = 256
SPAN = 2048
SHARED = ((0, 3, 4, 7), (1, 2, 5, 6))
F32 = jnp.float32
BF16 = jnp.bfloat16
HIGH = lax.Precision.HIGHEST
NN = (((1,), (0,)), ((), ()))
NT = (((1,), (1,)), ((), ()))
TN = (((0,), (0,)), ((), ()))
MIB = 2**20
SMEM = pl.BlockSpec(memory_space=pltpu.SMEM)
VMEM = pl.BlockSpec(memory_space=pltpu.VMEM)
ANY = pl.BlockSpec(memory_space=pl.ANY)
BOTH = ("ctx", "fsdp")


def dot(a, b, dims=NN):
    return lax.dot_general(a, b, dims, preferred_element_type=F32)


def shape(*dims, dtype=BF16):
    return jax.ShapeDtypeStruct(dims, dtype)


def call(kernel, outs, name, args, scratch=(), ins=None, flops=10**9, moved=10**7, limit=60):
    return pl.pallas_call(
        kernel,
        grid=(1,),
        out_shape=outs,
        in_specs=ins or [VMEM] * len(args),
        out_specs=jax.tree.map(lambda _: VMEM, outs),
        scratch_shapes=list(scratch),
        compiler_params=pltpu.CompilerParams(vmem_limit_bytes=limit * MIB),
        cost_estimate=pl.CostEstimate(flops=flops, bytes_accessed=moved, transcendentals=0),
        name=name,
    )(*args)


def pack_kernel(wq, wk, wv, wf, g1, g2, out):
    lane = lax.broadcasted_iota(jnp.int32, (192, 64), 1)
    rows = jnp.concatenate(
        [g1[...].astype(F32), g2[...].astype(F32), jnp.zeros((6, 192), F32)], 0
    ).T
    base = jnp.where(lane == 3, rows[:, 0:1], jnp.where(lane == 4, rows[:, 1:2], 0.0))
    forget = wf[...].astype(F32)
    for d in range(8):
        parts = []
        for h in range(3):
            at = d * 192 + h * 64
            parts += [wq[:, at : at + 64], wk[:, at : at + 64], wv[:, at : at + 64]]
        ext = base
        for h in range(3):
            ext = jnp.where(lane == h, forget[:, 3 * d + h : 3 * d + h + 1], ext)
        parts.append(ext.astype(BF16))
        for m in range(5):
            out[d, :, m * 128 : (m + 1) * 128] = jnp.concatenate(
                [parts[2 * m], parts[2 * m + 1]], 1
            )


def pack_two_kernel(f_ref, wg, wu, wo, *refs):
    outs, all_s = refs[:8], refs[8]
    for d in range(8):
        all_s[d, :, 0:512] = wg[:, d * 512 : (d + 1) * 512]
        all_s[d, :, 512:1024] = wu[:, d * 512 : (d + 1) * 512]
        at = d * 192
        heads = [wo[:, at + h * 64 : at + h * 64 + 64] for h in range(3)]
        all_s[d, :, 1024:1152] = jnp.concatenate([heads[0], heads[1]], 1)
        all_s[d, :, 1152:1280] = jnp.concatenate([heads[1], heads[2]], 1)
    for k in range(8):
        outs[k][...] = all_s[lax.rem(f_ref[0] + k, 8)]


def place_kernel(f_ref, n1, *refs):
    ins, w2, sig = refs[:8], refs[8], refs[9]
    for k in range(8):
        at = pl.multiple_of(lax.rem(f_ref[0] + 8 - k, 8) * 192, 64)
        w2[pl.ds(at, 192), :] = ins[k][...]
    sig[...] = jax.nn.sigmoid(dot(n1[...], w2[:, 1024:1280]))


def mask_kernel(live, c, _n1, out):
    keep = live[:, 0:1] > 0.5
    out[...] = jnp.where(keep, c[...].astype(F32), 0.0).astype(BF16)


def proj_kernel(x, w1, bias, _part, n1, send, fpre, gains):
    gains[...] = w1[:, 512:640].astype(F32).T[64:72]
    x32 = x[...].astype(F32)
    r1 = lax.rsqrt(jnp.mean(x32 * x32, -1, keepdims=True) + EPS)
    normed = (x32 * r1 * gains[3:4]).astype(BF16)
    n1[...] = normed
    proj = dot(normed, w1[...])
    rows = proj[:, 512:640].T[64:72] + bias[...]
    fpre[...] = rows
    logs = jnp.minimum(rows, 0.0) - jnp.log1p(jnp.exp(-jnp.abs(rows)))
    low = proj[:, 0:576].astype(BF16)
    for s in range(4):
        for j in range(2):
            send[2 * s + j, 0:128, :] = low[s * 128 : (s + 1) * 128, j * 192 : j * 192 + 384]
            line = jnp.concatenate(
                [
                    logs[j : j + 1, s * 128 : (s + 1) * 128],
                    logs[j + 1 : j + 2, s * 128 : (s + 1) * 128],
                    jnp.zeros((1, 128), F32),
                ],
                1,
            )
            send[2 * s + j, 128:144, :] = jnp.broadcast_to(line, (16, 384)).astype(BF16)


def project(x_all, w1, bias, after):
    def fixed(*dims):
        return pl.BlockSpec(dims, lambda i: (0,) * len(dims))

    return pl.pallas_call(
        proj_kernel,
        grid=(2,),
        out_shape=(
            shape(1024, 1536),
            shape(16, 144, 384),
            shape(8, 1024, dtype=F32),
            shape(8, 1536, dtype=F32),
        ),
        in_specs=[
            pl.BlockSpec((512, 1536), lambda i: (i, 0)),
            fixed(1536, 640),
            fixed(8, 1),
            ANY,
        ],
        out_specs=(
            pl.BlockSpec((512, 1536), lambda i: (i, 0)),
            pl.BlockSpec((8, 144, 384), lambda i: (i, 0, 0)),
            pl.BlockSpec((8, 512), lambda i: (0, i)),
            fixed(8, 1536),
        ),
        compiler_params=pltpu.CompilerParams(vmem_limit_bytes=40 * MIB),
        cost_estimate=pl.CostEstimate(
            flops=2 * 10**9, bytes_accessed=10**7, transcendentals=0
        ),
        name="project",
    )(x_all, w1, bias, after)


def score_cols(hs, b, q_s, k_s, fc_s, fr):
    n = (b + 1) * QB
    q0 = b * QB
    qq = q_s[hs, q0 : q0 + QB, :]
    cols = dot(k_s[hs, 0:n, :], qq, NT)
    bias = fr[hs, :, q0 : q0 + 1] - fc_s[hs, 0:n, :]
    cols = cols + bias
    keep = lax.broadcasted_iota(jnp.int32, (QB, QB), 0) <= lax.broadcasted_iota(
        jnp.int32, (QB, QB), 1
    )
    tail = jnp.where(keep, cols[n - QB : n], NEG)
    if b:
        cols = jnp.concatenate([cols[: n - QB], tail], 0)
    else:
        cols = tail
    return cols, qq, n, q0


def run_units(j, unit):
    for b in range(SPAN // QB):
        unit(j, b)
    for half in range(2):

        @pl.when(j == half)
        def _():
            for b in SHARED[half]:
                unit(1 - half, b)


def load_heads(bm_ref, r1, q_s, k_s, v_s):
    for blk in range(32):
        at = pl.multiple_of(bm_ref[blk] * 64, 64)
        c, r = divmod(blk, 2)
        for hs in range(2):
            part = r1[c, r * 64 : (r + 1) * 64, hs * 192 : (hs + 1) * 192]
            q_s[hs, pl.ds(at, 64), :] = (part[:, 0:64].astype(F32) * 0.125).astype(BF16)
            k_s[hs, pl.ds(at, 64), :] = part[:, 64:128]
            v_s[hs, pl.ds(at, 64), :] = part[:, 128:192]


def column_decay(fr, fc_s):
    both = jnp.concatenate([fr[0], fr[1], jnp.zeros((6, SPAN), F32)], 0).T
    fc_s[0] = both[:, 0:1]
    fc_s[1] = both[:, 1:2]


def fwd_kernel(bm_ref, j_ref, r1, fr, _a, _b, _c, o_ref, attn_ref, l_ref, q_s, k_s, v_s, vt_s, fc_s, o_s):
    j = j_ref[0]
    load_heads(bm_ref, r1, q_s, k_s, v_s)
    column_decay(fr, fc_s)
    for hs in range(2):
        vt_s[hs, 0:64, :] = v_s[hs].astype(F32).T.astype(BF16)
        vt_s[hs, 64:80, :] = jnp.ones((16, SPAN), BF16)
        o_s[hs] = jnp.zeros((SPAN, HD), BF16)

    def unit(hs, b):
        cols, _, n, q0 = score_cols(hs, b, q_s, k_s, fc_s, fr)
        top = jnp.max(cols, 0, keepdims=True)
        probs = jnp.exp(cols - top).astype(BF16)
        acc = dot(vt_s[hs, :, 0:n], probs)
        total = acc[64:65]
        rows = (acc[0:64] / total).T
        attn_ref[hs, q0 : q0 + QB, :] = rows
        l_ref[hs, :, q0 : q0 + QB] = top + jnp.log(total)
        o_s[hs, q0 : q0 + QB, :] = rows.astype(BF16)

    run_units(j, unit)
    for blk in range(32):
        at = pl.multiple_of(bm_ref[blk] * 64, 64)
        c, r = divmod(blk, 2)
        o_ref[c, r * 64 : (r + 1) * 64, :] = jnp.concatenate(
            [o_s[0, pl.ds(at, 64), :], o_s[1, pl.ds(at, 64), :]], 1
        )


def suffix_sums(row, dl_s, hs):
    grid = jnp.concatenate([row[:, b * 64 : (b + 1) * 64] for b in range(32)], 0)
    tri = lax.broadcasted_iota(jnp.int32, (64, 64), 0) >= lax.broadcasted_iota(
        jnp.int32, (64, 64), 1
    )
    within = jnp.dot(grid, tri.astype(F32), precision=HIGH, preferred_element_type=F32)
    total = jnp.broadcast_to(within[:, 0:1], (32, 64))
    later = lax.broadcasted_iota(jnp.int32, (32, 32), 0) < lax.broadcasted_iota(
        jnp.int32, (32, 32), 1
    )
    dl_s[hs] = within + jnp.dot(
        later.astype(F32), total, precision=HIGH, preferred_element_type=F32
    )


def bwd_kernel(
    bm_ref, j_ref, r1, da_r, attn_ref, l_ref, fr, go,
    ds_ref,
    q_s, k_s, v_s, da_s, kt_s, fc_s, dk_s, dv_s, out_s, rs_ref, dl_s,
):
    j = j_ref[0]
    for c in range(16):
        ds_ref[c, 144:192, :] = go[c]
    load_heads(bm_ref, r1, q_s, k_s, v_s)
    column_decay(fr, fc_s)
    for blk in range(32):
        at = pl.multiple_of(bm_ref[blk] * 64, 64)
        c, r = divmod(blk, 2)
        part = da_r[c, r * 64 : (r + 1) * 64, :]
        for hs in range(2):
            da_s[hs, pl.ds(at, 64), :] = part[:, hs * 64 : (hs + 1) * 64]
    for hs in range(2):
        kt_s[hs, 0:64, :] = k_s[hs].astype(F32).T.astype(BF16)
        kt_s[hs, 64:80, :] = jnp.ones((16, SPAN), BF16)
        dk_s[hs] = jnp.zeros((SPAN, 128), F32)
        dv_s[hs] = jnp.zeros((SPAN, HD), F32)
        out_s[hs] = jnp.zeros((SPAN, 192), BF16)
        rs_ref[hs] = jnp.zeros((1, SPAN), F32)

    def unit(hs, b):
        cols, qq, n, q0 = score_cols(hs, b, q_s, k_s, fc_s, fr)
        datt = da_s[hs, q0 : q0 + QB, :]
        attn = attn_ref[hs, q0 : q0 + QB, :]
        delta = jnp.sum((datt.astype(F32) * attn).T, 0, keepdims=True)
        probs = jnp.exp(cols - l_ref[hs, :, q0 : q0 + QB])
        dv_s[hs, 0:n, :] += dot(probs.astype(BF16), datt)
        back = dot(v_s[hs, 0:n, :], datt, NT)
        dscore = (probs * (back - delta)).astype(BF16)
        wide = jnp.concatenate([qq, jnp.ones((QB, HD), BF16)], 1)
        dk_s[hs, 0:n, :] += dot(dscore, wide)
        dq = dot(kt_s[hs, :, 0:n], dscore)
        rs_ref[hs, :, q0 : q0 + QB] = dq[64:65]
        out_s[hs, q0 : q0 + QB, 0:64] = (dq[0:64].T * 0.125).astype(BF16)

    run_units(j, unit)
    for hs in range(2):
        both = dk_s[hs]
        suffix_sums(rs_ref[hs] - both.T[64:65], dl_s, hs)
        out_s[hs, :, 64:128] = both[:, 0:64].astype(BF16)
        out_s[hs, :, 128:192] = dv_s[hs].astype(BF16)
    for blk in range(32):
        at = pl.multiple_of(bm_ref[blk] * 64, 64)
        c, r = divmod(blk, 2)
        ds_ref[c, r * 64 : (r + 1) * 64, :] = jnp.concatenate(
            [out_s[0, pl.ds(at, 64), :], out_s[1, pl.ds(at, 64), :]], 1
        )
    for c in range(16):
        lines = [
            dl_s[hs, pl.ds(bm_ref[2 * c + r], 1), :] for hs in range(2) for r in range(2)
        ]
        line = jnp.concatenate(lines + [jnp.zeros((1, 128), F32)], 1)
        ds_ref[c, 128:144, :] = jnp.broadcast_to(line, (16, 384)).astype(BF16)


HEADS = [pltpu.VMEM((2, SPAN, HD), BF16)] * 3


def attend(block_map, j, r1, decay, after):
    return call(
        fwd_kernel,
        (shape(16, 128, 128), shape(2, SPAN, HD, dtype=F32), shape(2, 1, SPAN, dtype=F32)),
        "attend",
        (block_map, j, r1, decay, *after),
        HEADS
        + [
            pltpu.VMEM((2, 80, SPAN), BF16),
            pltpu.VMEM((2, SPAN, 1), F32),
            pltpu.VMEM((2, SPAN, HD), BF16),
        ],
        [SMEM, SMEM, VMEM, VMEM, ANY, ANY, ANY],
        flops=4 * 10**9,
    )


def attend_back(block_map, j, r1, upstream, attn, logs, decay, go):
    return call(
        bwd_kernel,
        shape(16, 192, 384),
        "attend_back",
        (block_map, j, r1, upstream, attn, logs, decay, go),
        HEADS
        + [
            pltpu.VMEM((2, SPAN, HD), BF16),
            pltpu.VMEM((2, 80, SPAN), BF16),
            pltpu.VMEM((2, SPAN, 1), F32),
            pltpu.VMEM((2, SPAN, 128), F32),
            pltpu.VMEM((2, SPAN, HD), F32),
            pltpu.VMEM((2, SPAN, 192), BF16),
            pltpu.VMEM((2, 1, SPAN), F32),
            pltpu.VMEM((2, 32, 64), F32),
        ],
        [SMEM, SMEM] + [VMEM] * 6,
        flops=10**10,
    )


def mid_kernel(o_r, wo, x, gains, h_ref, n2_ref, r2_ref):
    acc = x[...].astype(F32)
    for f in range(8):
        at = f * 192
        acc += dot(o_r[f, :, 0:128], wo[at : at + 128, :])
        acc += dot(o_r[f, :, 128:256], wo[at + 64 : at + 192, :])
    h_ref[...] = acc
    r2 = lax.rsqrt(jnp.mean(acc * acc, -1, keepdims=True) + EPS)
    r2_ref[...] = jnp.broadcast_to(r2, (128, 128))
    n2_ref[...] = (acc * r2 * gains[4:5]).astype(BF16)


def mid_back_kernel(
    dn2_r, h_ref, r2_ref, c_ref, gains, wo, _a, _b, _c, _d,
    dh_ref, da_ref, do_ref, g2_ref,
):
    h = h_ref[...]
    r2 = r2_ref[:, 0:1]
    dn2 = dn2_r[...].astype(F32)
    g2_ref[...] = jnp.sum(dn2 * h * r2, 0, keepdims=True)
    scaled = dn2 * gains[4:5]
    dh = (
        c_ref[...].astype(F32)
        + r2 * scaled
        - h * (r2 * r2 * r2) * jnp.mean(scaled * h, -1, keepdims=True)
    )
    dh_ref[...] = dh
    da = dh.astype(BF16)
    da_ref[...] = da
    for f in range(8):
        at = f * 192
        do_ref[f, :, 0:128] = dot(da, wo[at : at + 128, :], NT).astype(BF16)
        do_ref[f, :, 128:256] = dot(da, wo[at + 64 : at + 192, :], NT).astype(BF16)


def ffn_kernel(n2, c, w2, wd, dn2_ref, ffo_ref, u_ref, dpre_ref):
    pre = dot(n2[...], w2[:, 0:1024])
    gate, up = pre[:, 0:512], pre[:, 512:1024]
    sig = jax.nn.sigmoid(gate)
    act = gate * sig
    u = (act * up).astype(BF16)
    u_ref[...] = u
    du = dot(c[...], wd[...], NT)
    dgate = (du * up * (sig * (1.0 + gate * (1.0 - sig)))).astype(BF16)
    dup = (du * act).astype(BF16)
    dpre = jnp.concatenate([dgate, dup], 1)
    dpre_ref[...] = dpre
    dn2_ref[...] = dot(dpre, w2[:, 0:1024], NT).astype(BF16)
    ffo_ref[...] = dot(u, wd[...]).astype(BF16)


def feed_forward(n2, c_all, w2, wd):
    rows = 256
    return pl.pallas_call(
        ffn_kernel,
        grid=(1024 // rows,),
        out_shape=(
            shape(1024, 1536),
            shape(1024, 1536),
            shape(1024, 512),
            shape(1024, 1024),
        ),
        in_specs=[
            pl.BlockSpec((rows, 1536), lambda i: (i, 0)),
            pl.BlockSpec((rows, 1536), lambda i: (i, 0)),
            pl.BlockSpec((1536, 1280), lambda i: (0, 0)),
            pl.BlockSpec((512, 1536), lambda i: (0, 0)),
        ],
        out_specs=(
            pl.BlockSpec((rows, 1536), lambda i: (i, 0)),
            pl.BlockSpec((rows, 1536), lambda i: (i, 0)),
            pl.BlockSpec((rows, 512), lambda i: (i, 0)),
            pl.BlockSpec((rows, 1024), lambda i: (i, 0)),
        ),
        compiler_params=pltpu.CompilerParams(vmem_limit_bytes=48 * MIB),
        cost_estimate=pl.CostEstimate(
            flops=10**10, bytes_accessed=2 * 10**7, transcendentals=0
        ),
        name="feed_forward",
    )(n2, c_all, w2, wd)


HALF = 576


def ffn_grad_kernel(zy_ref, n2, dpre, u, c, *refs):
    outs, all_s = refs[:8], refs[8]
    for part in range(4):
        g = dot(n2[:, part * 384 : (part + 1) * 384], dpre[...], TN).astype(BF16)
        for sub in range(2):
            f = 2 * part + sub
            for cr in range(4):
                for col in range(8):
                    cc, half = divmod(col, 2)
                    at = f * 96 + half * 48
                    all_s[cr * 4 + cc, at : at + 48, :] = g[
                        sub * 192 + cr * 48 : sub * 192 + cr * 48 + 48,
                        col * 128 : (col + 1) * 128,
                    ]
    for part in range(4):
        g = dot(u[:, part * 128 : (part + 1) * 128], c[...], TN).astype(BF16)
        for sub in range(4):
            for col in range(12):
                at = 768 + col * 32
                all_s[4 * part + sub, at : at + 32, :] = g[
                    sub * 32 : sub * 32 + 32, col * 128 : (col + 1) * 128
                ]
    for k in range(4):
        y = lax.rem(zy_ref[1] + k, 4)
        z = lax.rem(zy_ref[0] + k, 4)
        for i in range(4):
            outs[k][i] = all_s[i * 4 + y, 0:HALF, :]
            outs[4 + k][i] = all_s[z * 4 + i, HALF:1152, :]


def first_sum_kernel(zy_ref, *refs):
    ins, outs, acc_s = refs[:8], refs[8:16], refs[16]
    for half in range(2):
        for i in range(4):
            acc = ins[4 * half][i].astype(F32)
            for k in range(1, 4):
                acc += ins[4 * half + k][i].astype(F32)
            acc_s[half, i] = acc.astype(BF16)
        for k in range(4):
            outs[4 * half + k][...] = acc_s[half, lax.rem(zy_ref[half] + k, 4)]


def second_sum_kernel(*refs):
    ins, cols, down = refs[:8], refs[8], refs[9]
    sums = []
    for half in range(2):
        acc = ins[4 * half][...].astype(F32)
        for k in range(1, 4):
            acc += ins[4 * half + k][...].astype(F32)
        sums.append(acc.astype(BF16))
    full = jnp.concatenate(sums, 0)
    cols[...] = full[0:768].reshape(8, 96, 128)
    down[...] = full[768:1152]


def shift(arrays, axis):
    out = [arrays[0]]
    for k in range(1, 4):
        pairs = []
        for z in range(4):
            for y in range(4):
                to = ((z + k) % 4, y) if axis == 0 else (z, (y + k) % 4)
                pairs.append((z * 4 + y, to[0] * 4 + to[1]))
        out.append(lax.ppermute(arrays[k], "ctx", pairs))
    return out


def out_grad_kernel(f_ref, o, *refs):
    pieces, out, o_s, da_s = refs[:8], refs[8], refs[9], refs[10]
    fi = f_ref[0]
    for k in range(8):
        first = fi if k < 4 else fi + 1 - 2 * lax.rem(fi, 2)
        slot = lax.rem(first + 8 - 2 * (k % 4), 8)
        at = pl.multiple_of(slot * 128, 128)
        o_s[k * 128 : (k + 1) * 128, :] = o[pl.ds(at, 128), :]
        da_s[k * 128 : (k + 1) * 128, :] = pieces[k][...]
    t = dot(o_s[...], da_s[...], TN)
    t = jnp.concatenate([t[0:64], t[64:128] + t[128:192], t[192:256]], 0).astype(BF16)
    for c in range(16):
        cr, cc = divmod(c, 4)
        out[c] = t[cr * 48 : (cr + 1) * 48, cc * 384 : (cc + 1) * 384]


def head_grad_kernel(n1, dback, dlog2, out, dproj):
    for s in range(8):
        d0, d1 = dback[2 * s], dback[2 * s + 1]
        dproj[s * 128 : (s + 1) * 128, :] = jnp.concatenate(
            [d0[0:128, 0:192], d0[0:128, 192:384] + d1[0:128, 0:192], d1[0:128, 192:384]], 1
        )
    for c in (14, 15):
        out[c] = jnp.zeros((8, 80, 128), BF16)
    for part in range(2):
        left = n1[:, part * 768 : (part + 1) * 768]
        heads = dot(left, dproj[...], TN)
        gate = dot(left, dlog2[...], TN)
        mid = gate[:, 64:128] + gate[:, 128:192]
        g = jnp.concatenate([heads, gate[:, 0:64], mid, gate[:, 192:256]], 1).astype(BF16)
        for sub in range(4):
            f = 4 * part + sub
            for t in range(72):
                rt, lt = divmod(t, 6)
                c, slot = divmod(t, 5)
                row = sub * 192 + rt * 16
                out[c, f, slot * 16 : (slot + 1) * 16, :] = g[
                    row : row + 16, lt * 128 : (lt + 1) * 128
                ]


def input_grad_kernel(
    f_ref, dproj, dlog2, dl, fpre, w1, w2, gains, n1, gain2, out
):
    fi = f_ref[0]
    rows = [[], [], []]
    for s in range(8):
        d0 = dl[2 * s : 2 * s + 1].astype(F32)
        d1 = dl[2 * s + 1 : 2 * s + 2].astype(F32)
        rows[0].append(d0[:, 0:128])
        rows[1].append(d0[:, 128:256] + d1[:, 0:128])
        rows[2].append(d1[:, 128:256])
    dlf = jnp.concatenate(
        [jnp.concatenate(r, 1) for r in rows] + [jnp.zeros((5, 1024), F32)], 0
    )
    is_head = lax.broadcasted_iota(jnp.int32, (8, 1024), 0) < 3
    dfpre = jnp.where(is_head, dlf * jax.nn.sigmoid(-fpre[...]), 0.0).astype(BF16)
    w_forget = gains[...].astype(BF16)
    gain1 = jnp.zeros((1, 1536), F32)
    for p in range(4):
        at = p * 256
        part = (
            dot(dproj[at : at + 256, :], w1[:, 0:576], NT)
            + dot(dlog2[at : at + 256, :], w2[:, 1024:1280], NT)
            + dot(dfpre[:, at : at + 256], w_forget, TN)
        )
        gain1 += jnp.sum(part * n1[at : at + 256, :].astype(F32), 0, keepdims=True)
        out[2 * p : 2 * p + 2, 0:128, :] = part.astype(BF16).reshape(2, 128, 1536)
    gain1 = gain1 / gains[3:4]
    forget = dot(dfpre, n1[...])
    bias = jnp.sum(dfpre.astype(F32), 1, keepdims=True)
    lane = lax.broadcasted_iota(jnp.int32, (8, 1536), 1)
    mine = (lane >= fi * 192) & (lane < fi * 192 + 192)
    for d in range(8):
        at = d * 192
        top = jnp.concatenate([forget[:, at : at + 192]] * 8, 1)
        top = jnp.where(mine, top, 0.0)
        own = jnp.broadcast_to(bias[0:3], (3, 1536)) * (fi == d).astype(F32)
        low = jnp.concatenate(
            [
                jnp.concatenate([gain1[:, at : at + 192]] * 8, 1),
                jnp.concatenate([gain2[:, at : at + 192]] * 8, 1),
                own,
                jnp.zeros((3, 1536), F32),
            ],
            0,
        )
        out[d, 128:144, :] = jnp.concatenate([top, low], 0).astype(BF16)


def head_sum_kernel(r, go, out):
    for f in range(8):
        acc = r[0, f].astype(F32)
        for c in range(1, 16):
            acc += r[c, f].astype(F32)
        out[f * 80 : (f + 1) * 80, :] = acc.astype(BF16)
    acc = go[0].astype(F32)
    for c in range(1, 16):
        acc += go[c].astype(F32)
    for lt in range(3):
        out[640 + lt * 48 : 688 + lt * 48, :] = acc[:, lt * 128 : (lt + 1) * 128].astype(BF16)


def unpack_ffn_kernel(r, gate, up, down):
    for cc in range(4):
        to = gate if cc < 2 else up
        for f in range(8):
            for half in range(2):
                at = f * 96 + half * 48
                col = f * 512 + (cc % 2) * 256 + half * 128
                to[:, col : col + 128] = r[cc, at : at + 48, :].astype(F32)
        for col in range(12):
            at = 768 + col * 32
            down[cc * 32 : (cc + 1) * 32, col * 128 : (col + 1) * 128] = r[
                cc, at : at + 32, :
            ].astype(F32)


def unpack_ffn(gathered):
    return pl.pallas_call(
        unpack_ffn_kernel,
        grid=(4,),
        out_shape=(
            shape(192, 4096, dtype=F32),
            shape(192, 4096, dtype=F32),
            shape(512, 1536, dtype=F32),
        ),
        in_specs=[pl.BlockSpec((4, 1152, 128), lambda i: (i, 0, 0))],
        out_specs=(
            pl.BlockSpec((48, 4096), lambda i: (i, 0)),
            pl.BlockSpec((48, 4096), lambda i: (i, 0)),
            pl.BlockSpec((128, 1536), lambda i: (i, 0)),
        ),
        compiler_params=pltpu.CompilerParams(vmem_limit_bytes=40 * MIB),
        cost_estimate=pl.CostEstimate(flops=0, bytes_accessed=2 * 10**7, transcendentals=0),
        name="unpack_ffn",
    )(gathered)


def unpack_kernel(r, q, k, v, g, o):
    for rt in range(12):
        rows = [[], [], [], []]
        for f in range(8):
            tiles = []
            for lt in range(6):
                c, slot = divmod(rt * 6 + lt, 5)
                at = f * 80 + slot * 16
                tiles.append(r[c, at : at + 16, :].astype(F32))
            line = jnp.concatenate(tiles, 1)
            for h in range(3):
                for w in range(3):
                    at = h * 192 + w * 64
                    rows[w].append(line[:, at : at + 64])
            rows[3].append(line[:, 576:768])
        for w, to in enumerate((q, k, v, g)):
            to[rt * 16 : (rt + 1) * 16, :] = jnp.concatenate(rows[w], 1)
    for c in range(16):
        cr, cc = divmod(c, 4)
        for lt in range(3):
            col = cc * 384 + lt * 128
            o[cr * 48 : (cr + 1) * 48, col : col + 128] = r[
                c, 640 + lt * 48 : 688 + lt * 48, :
            ].astype(F32)


def swap(array, axis):
    return lax.all_to_all(array, axis, 0, 0, tiled=True)


def gather(array, axis):
    return lax.all_gather(array, axis, axis=0, tiled=True)


def tie(*arrays):
    return lax.optimization_barrier(arrays)


def per_device(
    tokens, cotangent, lengths, block_map, norm_gain, w_query, w_key, w_value, w_forget,
    forget_bias, w_outgate, w_output, ffn_gain, w_gate, w_up, w_down,
):
    ci = lax.axis_index("ctx").astype(jnp.int32)
    fi = lax.axis_index("fsdp").astype(jnp.int32)
    j = lax.rem(ci, 2)[None]
    zy = jnp.stack([ci // 4, lax.rem(ci, 4)])
    offsets = jnp.arange(64, dtype=jnp.int32)
    own_blocks = lax.dynamic_slice_in_dim(block_map, 2 * ci, 2)
    live = ((own_blocks[:, None] * 64 + offsets[None, :]).reshape(128) < lengths[0])[:, None]
    x_own = tokens[0]
    live32 = jnp.broadcast_to(live.astype(F32), (128, 128))

    w1 = call(
        pack_kernel,
        shape(8, 192, 640),
        "pack",
        (w_query, w_key, w_value, w_forget, norm_gain[None], ffn_gain[None]),
    )
    x_own, w1 = tie(x_own, w1)
    x_all = gather(x_own, "fsdp")
    w1 = swap(w1, "fsdp").reshape(1536, 640)
    parts = call(
        pack_two_kernel,
        (shape(192, 1280),) * 8,
        "pack_two",
        (fi[None], w_gate, w_up, w_outgate),
        [pltpu.VMEM((8, 192, 1280), BF16)],
        [SMEM] + [VMEM] * 3,
    )
    parts = [parts[0]] + [
        lax.ppermute(parts[k], "fsdp", [(f, (f + k) % 8) for f in range(8)]) for k in range(1, 8)
    ]
    w_output, x_all = tie(w_output, x_all)
    wo_all = gather(w_output, "fsdp")

    bias = jnp.pad(forget_bias.astype(F32), (0, 5))[:, None]
    n1, send, fpre, gains = project(x_all, w1, bias, parts[0])
    c_own = call(
        mask_kernel, shape(128, 1536), "mask", (live32, cotangent[0], n1), ins=[VMEM, VMEM, ANY]
    )
    c_all = gather(c_own, "fsdp")
    recv = swap(send, "ctx")
    w2, sig2 = call(
        place_kernel,
        (shape(1536, 1280), shape(1024, 256, dtype=F32)),
        "place",
        (fi[None], n1, *parts),
        ins=[SMEM] + [VMEM] * 9,
    )

    tri = (offsets[:, None] <= offsets[None, :]).astype(BF16)
    blocks = jnp.arange(32, dtype=jnp.int32)
    pick = (block_map[None, :] == blocks[:, None]).astype(BF16)
    logs = recv[:, 128, 0:256].reshape(16, 2, 2, 64).transpose(0, 2, 1, 3).reshape(32, 128)
    logs = dot(pick, logs).astype(BF16).reshape(32, 2, 64)
    within = jnp.einsum("bht,tu->hbu", logs, tri, preferred_element_type=F32)
    before = (blocks[None, :] < blocks[:, None]).astype(F32)
    starts = jnp.sum(before[None, :, :] * within[:, None, :, 63], -1)
    decay = (within + starts[:, :, None]).reshape(2, 1, SPAN)

    attn_own, attn, log_total = attend(block_map, j, recv, decay, parts[1:4])
    attn2 = swap(attn_own, "ctx").reshape(8, 2, 128, 128).transpose(0, 2, 1, 3)
    attn2 = attn2.reshape(1024, 256)
    o2 = (attn2.astype(F32) * sig2).astype(BF16)
    o_own = swap(o2.reshape(8, 128, 256), "fsdp")
    o_own, c_all = tie(o_own, c_all)
    h, n2_own, inv2 = call(
        mid_kernel,
        (shape(128, 1536, dtype=F32), shape(128, 1536), shape(128, 128, dtype=F32)),
        "mid",
        (o_own, wo_all, x_own, gains),
    )
    n2 = gather(n2_own, "fsdp")
    dn2, ffo, u, dpre = feed_forward(n2, c_all, w2, w_down)
    dn2 = lax.psum_scatter(dn2, "fsdp", scatter_dimension=0, tiled=True)

    fg = call(
        ffn_grad_kernel,
        (shape(4, HALF, 128),) * 8,
        "ffn_grad",
        (zy, n2, dpre, u, c_all),
        [pltpu.VMEM((16, 1152, 128), BF16)],
        [SMEM] + [VMEM] * 4,
        flops=5 * 10**9,
    )
    fg = shift(fg[:4], 1) + shift(fg[4:], 0)

    dh, da_own, do_own, gain2_part = call(
        mid_back_kernel,
        (
            shape(128, 1536, dtype=F32),
            shape(128, 1536),
            shape(8, 128, 256),
            shape(1, 1536, dtype=F32),
        ),
        "mid_back",
        (dn2, h, inv2, c_own, gains, wo_all, fg[1], fg[5], fg[2], fg[6]),
        ins=[VMEM] * 6 + [ANY] * 4,
    )
    do2 = swap(do_own, "fsdp").reshape(1024, 256)
    near = [da_own] + [
        lax.ppermute(da_own, "fsdp", [(f, (f + 2 * k) % 8) for f in range(8)]) for k in range(1, 4)
    ]
    da = near + [lax.ppermute(piece, "fsdp", [(f, f ^ 1) for f in range(8)]) for piece in near]
    fg = call(
        first_sum_kernel,
        (shape(HALF, 128),) * 8,
        "first_sum",
        (zy, *fg),
        [pltpu.VMEM((2, 4, HALF, 128), BF16)],
        [SMEM] + [VMEM] * 8,
    )
    fg = shift(fg[:4], 0) + shift(fg[4:], 1)
    do2 = do2.astype(F32)
    datt2 = (do2 * sig2).astype(BF16)
    dlog2 = (do2 * attn2.astype(F32) * sig2 * (1.0 - sig2)).astype(BF16)
    datt = swap(datt2.reshape(8, 128, 2, 128).transpose(0, 2, 1, 3).reshape(16, 128, 128), "ctx")
    datt, *fg = tie(datt, *fg)
    cols_g, down_g = call(second_sum_kernel, (shape(8, 96, 128), shape(384, 128)), "second_sum", fg)
    ffo, da_own = tie(ffo, da_own)
    ffo = lax.psum_scatter(ffo, "fsdp", scatter_dimension=0, tiled=True)
    go = call(
        out_grad_kernel,
        shape(16, 48, 384),
        "out_grad",
        (fi[None], o2, *da),
        [pltpu.VMEM((1024, 256), BF16), pltpu.VMEM((1024, 1536), BF16)],
        [SMEM] + [VMEM] * 9,
    )
    cols_g = swap(cols_g, "fsdp").reshape(768, 128)
    dheads = attend_back(block_map, j, recv, datt, attn, log_total, decay, go)
    dheads, cols_g, ffo = tie(dheads, cols_g, ffo)
    ffn = gather(jnp.concatenate([cols_g, down_g], 0), "ctx").reshape(16, 1152, 128)
    dback = swap(dheads, "ctx")
    mixed = jnp.where(live, h + ffo.astype(F32), 0.0).astype(BF16)

    g1, dproj = call(
        head_grad_kernel,
        (shape(16, 8, 80, 128), shape(1024, 576)),
        "head_grad",
        (n1, dback, dlog2),
        flops=3 * 10**9,
    )
    g1 = swap(g1.reshape(128, 80, 128), BOTH).reshape(16, 8, 80, 128)

    dn1 = call(
        input_grad_kernel,
        shape(8, 144, 1536),
        "input_grad",
        (fi[None], dproj, dlog2, dback[:, 128, 0:256], fpre, w1, w2, gains, n1, gain2_part),
        ins=[SMEM] + [VMEM] * 9,
        flops=3 * 10**9,
    )
    dn1 = lax.psum_scatter(
        dn1.reshape(1152, 1536), "fsdp", scatter_dimension=0, tiled=True
    )
    g1, ffn = tie(g1, ffn)
    att = call(head_sum_kernel, shape(784, 128), "head_sum", (g1, dback[:, 144:192]))
    att, dn1 = tie(att, dn1)
    att = gather(att, "ctx").reshape(16, 784, 128)

    small = jnp.concatenate([dn1[128:131], dn1[136:141]], 0)
    small = swap(jnp.broadcast_to(small[None], (16, 8, 1536)), "ctx")
    small = jnp.sum(small.astype(F32), 0)
    forget_g = small[0:3].reshape(3, 8, 192).transpose(2, 1, 0).reshape(192, 24)

    dn1 = dn1[0:128].astype(F32)
    gain1 = gains[3:4]
    x_own32 = x_own.astype(F32)
    r1_own = lax.rsqrt(jnp.mean(x_own32 * x_own32, -1, keepdims=True) + EPS)
    scaled1 = dn1 * gain1
    tokens_grad = (
        dh
        + r1_own * scaled1
        - x_own32 * (r1_own * r1_own * r1_own) * jnp.mean(scaled1 * x_own32, -1, keepdims=True)
    ).astype(BF16)

    gate_g, up_g, down_g = unpack_ffn(ffn)
    mat = shape(192, 1536, dtype=F32)
    query_g, key_g, value_g, outgate_g, output_g = call(
        unpack_kernel, (mat,) * 5, "unpack_heads", (att,)
    )
    return (
        mixed[None], tokens_grad[None], small[3, 0:192], query_g, key_g, value_g, forget_g,
        small[5:8, 0], outgate_g, output_g, small[4, 0:192], gate_g, up_g, down_g,
    )


def solution(mesh):
    act = P("fsdp", "ctx", None)
    vec, mat = P("fsdp"), P("fsdp", None)
    return jax.shard_map(
        per_device,
        mesh=mesh,
        in_specs=(act, act, vec, P(), vec, mat, mat, mat, mat, vec, mat, mat, vec, mat, mat, mat),
        out_specs=(act, act, vec, mat, mat, mat, mat, vec, mat, mat, vec, mat, mat, mat),
        check_vma=False,
    )
```

time: 3490 us -> 576 us (0.17)
  blocking collectives: 1460 us -> 54.8 us
  starting transfers between devices: 856 us -> 81.3 us
  local copies, waits for them, and re-layouts: 510 us -> 28.2 us
  matrix products: 289 us -> 0.26 us
  Pallas kernels: 0 us -> 131 us
  other arithmetic: 49.3 us -> 7.41 us
    unnamed x4 -> x0, blocking collectives: 1230 us -> none
    unnamed x259 -> x0, starting transfers between devices: 856 us -> none
    unnamed x407 -> x74, local copies, waits for them, and re-layouts: 427 us -> 16.6 us
    dot_general x55 -> x2, matrix products: 289 us -> 0.26 us  [the longest x1 0.13 us: per_device(): within = jnp.einsum('bht,tu->hbu', logs, tri, preferred_element_type=F32)]
    all_gather x13 -> x6, waiting for transfers between devices: 258 us -> 85.1 us  [gather(): return lax.all_gather(array, axis, axis=0, tiled=True)]
    all_gather x9 -> x0, blocking collectives: 159 us -> none  [the longest x1 20.6 us: per_device(): lax.all_gather(summed[2].astype(jnp.bfloat16), 'ctx', axis=0, tiled=True)]
    pallas_call x0 -> x19, Pallas kernels: none -> 131 us  [the longest x16 108 us: call(): pl.pallas_call(kernel, grid=(1,), out_shape=outs, in_specs=ins or [VMEM]...]
    ppermute x0 -> x26, waiting for transfers between devices: none -> 92.4 us  [the longest x12 34.5 us: shift(): out.append(lax.ppermute(arrays[k], 'ctx', pairs))]
  transfers between devices with their start and end apart: 273 -> 43, of which waited for: 14 -> 20; matrix products, arithmetic and copies ran while one was open for 55% -> 3% of each run, Pallas kernels for 0% -> 16%
where the time goes in v1:
time: 576 us; the launch traced here: 570 us
  waiting for transfers between devices  252 us (44%)
  Pallas kernels  131 us (23%)
  starting transfers between devices  81.3 us (14%)
  blocking collectives  54.8 us (10%)
  local copies, waits for them, and re-layouts  28.2 us (5%)
  between operations  15.3 us (3%)
  other arithmetic  7.41 us (1%)
    pallas_call x16, Pallas kernels, call(): pl.pallas_call(kernel, grid=(1,), out_shape=outs, in_specs=ins or [VMEM]...  108 us
    all_gather x6, waiting for transfers between devices, gather(): return lax.all_gather(array, axis, axis=0, tiled=True)  85.1 us
    all_to_all x8, waiting for transfers between devices, swap(): return lax.all_to_all(array, axis, 0, 0, tiled=True)  71 us
    all_to_all x2, blocking collectives, swap(): return lax.all_to_all(array, axis, 0, 0, tiled=True)  54.8 us
    all_to_all x8, starting transfers between devices, swap(): return lax.all_to_all(array, axis, 0, 0, tiled=True)  48.2 us
    ppermute x12, waiting for transfers between devices, shift(): out.append(lax.ppermute(arrays[k], 'ctx', pairs))  34.5 us
    ppermute x7, waiting for transfers between devices, per_device(): lax.ppermute(parts[k], 'fsdp', [(f, (f + k) % 8) for f in range(8)])  31.9 us
    ppermute x3, waiting for transfers between devices, per_device(): lax.ppermute(da_own, 'fsdp', [(f, (f + 2 * k) % 8) for f in range(8)])  26 us
  transfers between devices with their start and end apart: 43, of which 20 were waited for; matrix products, arithmetic and copies ran while one was open for 3% of the time, Pallas kernels for 16%

profile of v1, /device:TPU:1, one launch (start us, length us, event | category | flops | bytes accessed | tf_op | source)
XLA Modules:
  0.0 570.1 jit_solution(6968692959186288878)
XLA Ops:
  11.1 3.9 pack.1
  15.0 5.8 %all-to-all-start = ((bf16[8,192,640]{2,1,0:T(8,128)(2,1)}), bf16[8,192,640]{2,1,0:T(8,128)(2,1)S(1)}, u32[]{:S(2)}, u32[]{:S(2)}) async-start(bf16[8,192,640]{2,1,0:T(8,128)(2,1)} %pack.1), calls=%async_computation | async-start | bytes 3932160 | tf_op jit(solution)/shard_map/all_to_all | solution.py:664
  21.8 4.4 pack_two.1
  26.2 32.7 %all-gather.7.cloned.1.call-done.x = bf16[1024,1536]{1,0:T(8,128)(2,1)} async-done(((bf16[128,1536]{1,0:T(8,128)(2,1)}), bf16[1024,1536]{1,0:T(8,128)(2,1)}) %all-gather.7.cloned.1.call-update) | async-done | bytes 3145744 | tf_op jit(solution)/shard_map/all_gather | solution.py:668
  62.2 4.8 project.1
  73.3 7.2 %all-to-all-start.1 = ((bf16[16,144,384]{2,1,0:T(8,128)(2,1)}), bf16[16,144,384]{2,1,0:T(8,128)(2,1)S(1)}, u32[]{:S(2)}, u32[]{:S(2)}) async-start(bf16[16,144,384]{2,1,0:T(8,128)(2,1)} %get-tuple-element.97), calls=%async_computation.1 | async-start | bytes 3538944 | tf_op jit(solution)/shard_map/all_to_all | solution.py:664
  85.4 2.6 collective-permute-start.4
  88.1 17.5 %all-to-all-done.1.r1 = bf16[16,144,384]{2,1,0:T(8,128)(2,1)S(1)} async-done(((bf16[16,144,384]{2,1,0:T(8,128)(2,1)}), bf16[16,144,384]{2,1,0:T(8,128)(2,1)S(1)}, u32[]{:S(2)}, u32[]{:S(2)}) %all-to-all-start.1) | async-done | bytes 1769504 | tf_op jit(solution)/shard_map/all_to_all | solution.py:664
  108.3 11.1 %collective-permute-done.1._b.refs_2_ = bf16[192,1280]{1,0:T(8,128)(2,1)S(1)} collective-permute-done((bf16[192,1280]{1,0:T(8,128)(2,1)}, bf16[192,1280]{1,0:T(8,128)(2,1)S(1)}, u32[]{:S(2)}, u32[]{:S(2)}) %collective-permute-start.1) | collective-permute-done | bytes 491552 | tf_op jit(solution)/shard_map/ppermute | solution.py:707
  119.4 20.8 %collective-permute-done.2._c.refs_3_ = bf16[192,1280]{1,0:T(8,128)(2,1)S(1)} collective-permute-done((bf16[192,1280]{1,0:T(8,128)(2,1)}, bf16[192,1280]{1,0:T(8,128)(2,1)S(1)}, u32[]{:S(2)}, u32[]{:S(2)}) %collective-permute-start.2) | collective-permute-done | bytes 491552 | tf_op jit(solution)/shard_map/ppermute | solution.py:707
  141.0 13.9 %attend.1 = (bf16[16,128,128]{2,1,0:T(8,128)(2,1)}, f32[2,2048,64]{2,1,0:T(8,128)}, f32[2,1,2048]{2,1,0:T(1,128)}) custom-call(s32[32]{0:T(128)} %bm_ref.3, s32[1]{0:T(128)} %bitcast.1.j_ref, bf16[16,144,384]{2,1,0:T(8,128)(2,1)} %copy-done.19, f32[2,1,2048]{2,1,0:T(1,128)} %reshape.146.fr, bf16[192,1280]{1,0:T(8,128)(2,1)} %copy-done.24, ...), custom_call_target="tpu_custom_call" | custom-call | flops 4000000000 | bytes 10000000 | tf_op jit(solution)/shard_map/attend/pallas_call | solution.py:36
  154.9 6.9 %all-to-all-start.2 = ((bf16[16,128,128]{2,1,0:T(8,128)(2,1)}), bf16[16,128,128]{2,1,0:T(8,128)(2,1)S(1)}, u32[]{:S(2)}, u32[]{:S(2)}) async-start(bf16[16,128,128]{2,1,0:T(8,128)(2,1)} %get-tuple-element.101), calls=%async_computation.2 | async-start | bytes 1048576 | tf_op jit(solution)/shard_map/all_to_all | solution.py:664
  161.9 5.6 place.1
  167.5 3.3 all-to-all-done.2
  172.7 12.3 %all_to_all.50.o_r = bf16[8,128,256]{2,1,0:T(8,128)(2,1)} all-to-all(bf16[8,128,256]{2,1,0:T(8,128)(2,1)S(1)} %bitcast.66), channel_id=1, replica_groups=mesh['ctx'=16,'fsdp'=8] {'fsdp'}, dimensions={0} | all-to-all | bytes 1048576 | tf_op jit(solution)/shard_map/all_to_all | solution.py:664
  185.1 5.5 mid.1
  190.6 24.2 %all-gather.13.cloned.1.call-done.n2 = bf16[1024,1536]{1,0:T(8,128)(2,1)} async-done(((bf16[128,1536]{1,0:T(8,128)(2,1)}), bf16[1024,1536]{1,0:T(8,128)(2,1)}) %all-gather.13.cloned.1.call-update) | async-done | bytes 3145744 | tf_op jit(solution)/shard_map/all_gather | solution.py:668
  214.9 14.6 %feed_forward.1 = (bf16[1024,1536]{1,0:T(8,128)(2,1)}, bf16[1024,1536]{1,0:T(8,128)(2,1)}, bf16[1024,512]{1,0:T(8,128)(2,1)S(1)}, bf16[1024,1024]{1,0:T(8,128)(2,1)S(1)}) custom-call(bf16[1024,1536]{1,0:T(8,128)(2,1)} %all-gather.13.cloned.1.call-done.n2, bf16[1024,1536]{1,0:T(8,128)(2,1)} %all-gather.9.cloned.1.call-done.c, ...), custom_call_target="tpu_custom_call" | custom-call | flops 10000000000 | bytes 20000000 | tf_op jit(solution)/shard_map/feed_forward/pallas_call | solution.py:399
  233.0 10.9 %ffn_grad.1 = (bf16[4,576,128]{2,1,0:T(8,128)(2,1)}, bf16[4,576,128]{2,1,0:T(8,128)(2,1)}, bf16[4,576,128]{2,1,0:T(8,128)(2,1)}, bf16[4,576,128]{2,1,0:T(8,128)(...) custom-call(s32[2]{0:T(128)} %pad_add_fusion.zy_ref, ...), custom_call_target="tpu_custom_call" | custom-call | flops 5000000000 | bytes 10000000 | tf_op jit(solution)/shard_map/ffn_grad/pallas_call | solution.py:36
  246.5 2.5 collective-permute-start.9
  249.0 2.6 collective-permute-start.10
  251.6 8.5 %collective-permute-done.7._a.refs_1_ = bf16[4,576,128]{2,1,0:T(8,128)(2,1)S(1)} collective-permute-done((bf16[4,576,128]{2,1,0:T(8,128)(2,1)}, bf16[4,576,128]{2,1,0:T(8,128)(2,1)S(1)}, u32[]{:S(2)}, u32[]{:S(2)}) %collective-permute-start.7) | collective-permute-done | bytes 589856 | tf_op jit(solution)/shard_map/ppermute | solution.py:494
  261.1 12.8 %collective-permute-done.9._c.refs_2_ = bf16[4,576,128]{2,1,0:T(8,128)(2,1)S(1)} collective-permute-done((bf16[4,576,128]{2,1,0:T(8,128)(2,1)}, bf16[4,576,128]{2,1,0:T(8,128)(2,1)S(1)}, u32[]{:S(2)}, u32[]{:S(2)}) %collective-permute-start.9) | collective-permute-done | bytes 589856 | tf_op jit(solution)/shard_map/ppermute | solution.py:494
  275.0 5.8 %mid_back.1 = (f32[128,1536]{1,0:T(8,128)}, bf16[128,1536]{1,0:T(8,128)(2,1)}, bf16[8,128,256]{2,1,0:T(8,128)(2,1)}, f32[1,1536]{1,0:T(1,128)}) custom-call(bf16[128,1536]{1,0:T(8,128)(2,1)} %reduce-scatter.4.cloned.1.call-done.dn2_r, f32[128,1536]{1,0:T(8,128)} %get-tuple-element.111.h_ref, f32[128,128]{1,0:T(8,128)} %get-tuple-element.116.r2_ref, ...), custom_call_target="tpu_custom_call" | custom-call | flops 1000000000 | bytes 10000000 | tf_op jit(solution)/shard_map/mid_back/pallas_call | solution.py:36
  282.2 5.0 all-to-all-start.4
  288.7 2.4 collective-permute-start.20
  294.7 2.2 collective-permute-start.22
  296.9 13.3 %collective-permute-done.19.refs_1_ = bf16[128,1536]{1,0:T(8,128)(2,1)} collective-permute-done((bf16[128,1536]{1,0:T(8,128)(2,1)}, bf16[128,1536]{1,0:T(8,128)(2,1)}, u32[]{:S(2)}, u32[]{:S(2)}) %collective-permute-start.19) | collective-permute-done | bytes 393248 | tf_op jit(solution)/shard_map/ppermute | solution.py:778
  310.9 12.6 %collective-permute-done.20.refs_2_ = bf16[128,1536]{1,0:T(8,128)(2,1)} collective-permute-done((bf16[128,1536]{1,0:T(8,128)(2,1)}, bf16[128,1536]{1,0:T(8,128)(2,1)}, u32[]{:S(2)}, u32[]{:S(2)}) %collective-permute-start.20) | collective-permute-done | bytes 393248 | tf_op jit(solution)/shard_map/ppermute | solution.py:778
  326.6 3.7 all-to-all-start.5
  330.3 4.0 first_sum.1
  335.7 8.3 %collective-permute-done.13.refs_1_ = bf16[576,128]{1,0:T(8,128)(2,1)S(1)} collective-permute-done((bf16[576,128]{1,0:T(8,128)(2,1)}, bf16[576,128]{1,0:T(8,128)(2,1)S(1)}, u32[]{:S(2)}, u32[]{:S(2)}) %collective-permute-start.13) | collective-permute-done | bytes 147488 | tf_op jit(solution)/shard_map/ppermute | solution.py:494
  347.9 3.8 out_grad.1.go
  355.5 6.3 %all-to-all-start.6 = ((bf16[8,96,128]{2,1,0:T(8,128)(2,1)}), bf16[8,96,128]{2,1,0:T(8,128)(2,1)S(1)}, u32[]{:S(2)}, u32[]{:S(2)}) async-start(bf16[8,96,128]{2,1,0:T(8,128)(2,1)} %get-tuple-element.148), calls=%async_computation.7 | async-start | bytes 393216 | tf_op jit(solution)/shard_map/all_to_all | solution.py:664
  361.9 18.6 %attend_back.1 = bf16[16,192,384]{2,1,0:T(8,128)(2,1)} custom-call(s32[32]{0:T(128)} %bm_ref.3, s32[1]{0:T(128)} %bitcast.1.j_ref, bf16[16,144,384]{2,1,0:T(8,128)(2,1)} %copy-done.19, bf16[16,128,128]{2,1,0:T(8,128)(2,1)} %copy-done.23, f32[2,2048,64]{2,1,0:T(8,128)} %get-tuple-element.137.attn_ref, f32[2,1,2048]{2,1,0:T(1,128)} %get-tuple-element.138.l_ref, ...), custom_call_target="tpu_custom_call" | custom-call | flops 10000000000 | bytes 10000000 | tf_op jit(solution)/shard_map/attend_back/pallas_call | solution.py:36
  381.3 42.5 %all_to_all.51.dback = bf16[16,192,384]{2,1,0:T(8,128)(2,1)S(1)} all-to-all(bf16[16,192,384]{2,1,0:T(8,128)(2,1)} %attend_back.1), channel_id=1, replica_groups=mesh['ctx'=16,'fsdp'=8] {'ctx'}, dimensions={0} | all-to-all | bytes 4718592 | tf_op jit(solution)/shard_map/all_to_all | solution.py:664
  425.2 8.2 %head_grad.1 = (bf16[16,8,80,128]{3,2,1,0:T(8,128)(2,1)}, bf16[1024,576]{1,0:T(8,128)(2,1)}) custom-call(bf16[1024,1536]{1,0:T(8,128)(2,1)} %copy-done, bf16[16,192,384]{2,1,0:T(8,128)(2,1)} %copy-done.13, bf16[1024,256]{1,0:T(8,128)(2,1)} %get-tuple-element.174.dlog2), custom_call_target="tpu_custom_call" | custom-call | flops 3000000000 | bytes 10000000 | tf_op jit(solution)/shard_map/head_grad/pallas_call | solution.py:36
  433.4 11.0 %input_grad.1 = bf16[8,144,1536]{2,1,0:T(8,128)(2,1)} custom-call(s32[1]{0:T(128)} %bitcast.5.f_ref, bf16[1024,576]{1,0:T(8,128)(2,1)} %get-tuple-element.158.dproj, bf16[1024,256]{1,0:T(8,128)(2,1)} %get-tuple-element.174.dlog2, bf16[16,256]{1,0:T(8,128)(2,1)} %bitcast.74, f32[8,1024]{1,0:T(8,128)} %copy-done.5, bf16[1536,640]{1,0:T(8,128)(2,1)} %bitcast.57, ...), custom_call_target="tpu_custom_call" | custom-call | flops 3000000000 | bytes 10000000 | tf_op jit(solution)/shard_map/input_grad/pallas_call | solution.py:36
  444.4 6.2 %all-to-all-start.8 = ((bf16[128,80,128]{2,1,0:T(8,128)(2,1)}), bf16[128,80,128]{2,1,0:T(8,128)(2,1)S(1)}, u32[]{:S(2)}, u32[]{:S(2)}) async-start(bf16[128,80,128]{2,1,0:T(8,128)(2,1)} %bitcast.21), calls=%async_computation.10 | async-start | bytes 5242880 | tf_op jit(solution)/shard_map/all_to_all | solution.py:664
  452.7 41.8 %all-to-all-done.8 = bf16[128,80,128]{2,1,0:T(8,128)(2,1)S(1)} async-done(((bf16[128,80,128]{2,1,0:T(8,128)(2,1)}), bf16[128,80,128]{2,1,0:T(8,128)(2,1)S(1)}, u32[]{:S(2)}, u32[]{:S(2)}) %all-to-all-start.8) | async-done | bytes 2621472 | tf_op jit(solution)/shard_map/all_to_all | solution.py:664
  496.0 3.0 head_sum.1
  499.0 2.6 reduce-scatter.8.cloned.1.call-done
  504.3 2.3 copy-done.2
  506.6 3.8 unpack_ffn.1
  511.3 6.9 %all-to-all-start.9 = ((bf16[16,8,1536]{2,1,0:T(8,128)(2,1)}), bf16[16,8,1536]{2,1,0:T(8,128)(2,1)S(1)}, u32[]{:S(2)}, u32[]{:S(2)}) async-start(bf16[16,8,1536]{2,1,0:T(8,128)(2,1)} %broadcast_in_dim.73), calls=%async_computation.12 | async-start | bytes 786432 | tf_op jit(solution)/shard_map/all_to_all | solution.py:664
  519.6 8.3 %all-to-all-done.9 = bf16[16,8,1536]{2,1,0:T(8,128)(2,1)S(1)} async-done(((bf16[16,8,1536]{2,1,0:T(8,128)(2,1)}), bf16[16,8,1536]{2,1,0:T(8,128)(2,1)S(1)}, u32[]{:S(2)}, u32[]{:S(2)}) %all-to-all-start.9) | async-done | bytes 393248 | tf_op jit(solution)/shard_map/all_to_all | solution.py:664
  529.9 28.1 %all-gather.17.cloned.1.call-done = bf16[12544,128]{1,0:T(8,128)(2,1)} async-done(((bf16[784,128]{1,0:T(8,128)(2,1)}), bf16[12544,128]{1,0:T(8,128)(2,1)}) %all-gather.17.cloned.1.call-update) | async-done | bytes 3211280 | tf_op jit(solution)/shard_map/all_gather | solution.py:668
  558.1 5.1 unpack_heads.1
  (190 shorter events, 64.1 us)
Async XLA Ops:
  7.2 51.8 %all-gather.7.cloned.1.call-start = ((), (), s32[]{:S(2)}) async-start(), calls=%async_computation.13 | async-start | bytes 3538944 | tf_op jit(solution)/shard_map/all_gather | solution.py:668
  15.0 44.0 %all-to-all-start = ((bf16[8,192,640]{2,1,0:T(8,128)(2,1)}), bf16[8,192,640]{2,1,0:T(8,128)(2,1)S(1)}, u32[]{:S(2)}, u32[]{:S(2)}) async-start(bf16[8,192,640]{2,1,0:T(8,128)(2,1)} %pack.1), calls=%async_computation | async-start | bytes 3932160 | tf_op jit(solution)/shard_map/all_to_all | solution.py:664
  20.8 164.2 %all-gather.9.cloned.1.call-start = ((), (), s32[]{:S(2)}) async-start(), calls=%async_computation.14 | async-start | bytes 3538944 | tf_op jit(solution)/shard_map/all_gather | solution.py:668
  72.6 112.5 %all-gather.11.cloned.1.call-start = ((), (), s32[]{:S(2)}) async-start(), calls=%async_computation.15 | async-start | bytes 5308416 | tf_op jit(solution)/shard_map/all_gather | solution.py:668
  73.3 32.2 %all-to-all-start.1 = ((bf16[16,144,384]{2,1,0:T(8,128)(2,1)}), bf16[16,144,384]{2,1,0:T(8,128)(2,1)S(1)}, u32[]{:S(2)}, u32[]{:S(2)}) async-start(bf16[16,144,384]{2,1,0:T(8,128)(2,1)} %get-tuple-element.97), calls=%async_computation.1 | async-start | bytes 3538944 | tf_op jit(solution)/shard_map/all_to_all | solution.py:664
  80.5 26.7 %collective-permute-start = (bf16[192,1280]{1,0:T(8,128)(2,1)}, bf16[192,1280]{1,0:T(8,128)(2,1)S(1)}, u32[]{:S(2)}, u32[]{:S(2)}) collective-permute-start(bf16[192,1280]{1,0:T(8,128)(2,1)} %get-tuple-element.98), channel_id=1, source_target_pairs={{0,1},{1,2},{2,3},{3,4},{4,5},{5,6},{6,7},{7,0},{8,9},{9,10},{10,1... | collective-permute-start | bytes 1474568 | tf_op jit(solution)/shard_map/ppermute | solution.py:707
  81.9 37.5 %collective-permute-start.1 = (bf16[192,1280]{1,0:T(8,128)(2,1)}, bf16[192,1280]{1,0:T(8,128)(2,1)S(1)}, u32[]{:S(2)}, u32[]{:S(2)}) collective-permute-start(bf16[192,1280]{1,0:T(8,128)(2,1)} %get-tuple-element.99), channel_id=1, source_target_pairs={{0,2},{1,3},{2,4},{3,5},{4,6},{5,7},{6,0},{7,1},{8,10},{9,11},{10,... | collective-permute-start | bytes 1474568 | tf_op jit(solution)/shard_map/ppermute | solution.py:707
  81.9 58.3 %collective-permute-start.2 = (bf16[192,1280]{1,0:T(8,128)(2,1)}, bf16[192,1280]{1,0:T(8,128)(2,1)S(1)}, u32[]{:S(2)}, u32[]{:S(2)}) collective-permute-start(bf16[192,1280]{1,0:T(8,128)(2,1)} %get-tuple-element.100), channel_id=1, source_target_pairs={{0,3},{1,4},{2,5},{3,6},{4,7},{5,0},{6,1},{7,2},{8,11},{9,12},{10,... | collective-permute-start | bytes 1474568 | tf_op jit(solution)/shard_map/ppermute | solution.py:707
  84.0 77.9 %collective-permute-start.3 = (bf16[192,1280]{1,0:T(8,128)(2,1)}, bf16[192,1280]{1,0:T(8,128)(2,1)}, u32[]{:S(2)}, u32[]{:S(2)}) collective-permute-start(bf16[192,1280]{1,0:T(8,128)(2,1)} %get-tuple-element.103), channel_id=1, source_target_pairs={{0,4},{1,5},{2,6},{3,7},{4,0},{5,1},{6,2},{7,3},{8,12},{9,13},{10,... | collective-permute-start | bytes 1474568 | tf_op jit(solution)/shard_map/ppermute | solution.py:707
  85.4 76.5 %collective-permute-start.4 = (bf16[192,1280]{1,0:T(8,128)(2,1)}, bf16[192,1280]{1,0:T(8,128)(2,1)}, u32[]{:S(2)}, u32[]{:S(2)}) collective-permute-start(bf16[192,1280]{1,0:T(8,128)(2,1)} %get-tuple-element.104), channel_id=1, source_target_pairs={{0,5},{1,6},{2,7},{3,0},{4,1},{5,2},{6,3},{7,4},{8,13},{9,14},{10,... | collective-permute-start | bytes 1474568 | tf_op jit(solution)/shard_map/ppermute | solution.py:707
  105.6 34.6 %copy-start.19 = (bf16[16,144,384]{2,1,0:T(8,128)(2,1)}, bf16[16,144,384]{2,1,0:T(8,128)(2,1)S(1)}, u32[]{:S(2)}) copy-start(bf16[16,144,384]{2,1,0:T(8,128)(2,1)S(1)} %all-to-all-done.1.r1) | copy-start | bytes 5308420
  107.2 33.0 %copy-start.24 = (bf16[192,1280]{1,0:T(8,128)(2,1)}, bf16[192,1280]{1,0:T(8,128)(2,1)S(1)}, u32[]{:S(2)}) copy-start(bf16[192,1280]{1,0:T(8,128)(2,1)S(1)} %collective-permute-done._a.refs_1_) | copy-start | bytes 1474564
  107.2 54.7 %collective-permute-start.5 = (bf16[192,1280]{1,0:T(8,128)(2,1)}, bf16[192,1280]{1,0:T(8,128)(2,1)}, u32[]{:S(2)}, u32[]{:S(2)}) collective-permute-start(bf16[192,1280]{1,0:T(8,128)(2,1)} %get-tuple-element.105), channel_id=1, source_target_pairs={{0,6},{1,7},{2,0},{3,1},{4,2},{5,3},{6,4},{7,5},{8,14},{9,15},{10,... | collective-permute-start | bytes 1474568 | tf_op jit(solution)/shard_map/ppermute | solution.py:707
  119.4 42.5 %collective-permute-start.6 = (bf16[192,1280]{1,0:T(8,128)(2,1)}, bf16[192,1280]{1,0:T(8,128)(2,1)}, u32[]{:S(2)}, u32[]{:S(2)}) collective-permute-start(bf16[192,1280]{1,0:T(8,128)(2,1)} %get-tuple-element.106), channel_id=1, source_target_pairs={{0,7},{1,0},{2,1},{3,2},{4,3},{5,4},{6,5},{7,6},{8,15},{9,8},{10,9... | collective-permute-start | bytes 1474568 | tf_op jit(solution)/shard_map/ppermute | solution.py:707
  154.9 15.9 %all-to-all-start.2 = ((bf16[16,128,128]{2,1,0:T(8,128)(2,1)}), bf16[16,128,128]{2,1,0:T(8,128)(2,1)S(1)}, u32[]{:S(2)}, u32[]{:S(2)}) async-start(bf16[16,128,128]{2,1,0:T(8,128)(2,1)} %get-tuple-element.101), calls=%async_computation.2 | async-start | bytes 1048576 | tf_op jit(solution)/shard_map/all_to_all | solution.py:664
  161.8 53.0 %all-gather.13.cloned.1.call-start = ((), (), s32[]{:S(2)}) async-start(), calls=%async_computation.16 | async-start | bytes 3538944 | tf_op jit(solution)/shard_map/all_gather | solution.py:668
  185.1 29.8 %copy-start.7 = (bf16[512,1536]{1,0:T(8,128)(2,1)S(1)}, bf16[512,1536]{1,0:T(8,128)(2,1)}, u32[]{:S(2)}) copy-start(bf16[512,1536]{1,0:T(8,128)(2,1)} %wd.1) | copy-start | bytes 4718596
  190.6 84.4 %reduce-scatter.4.cloned.1.call-start = ((), (), s32[]{:S(2)}) async-start(), calls=%async_computation.17 | async-start | bytes 3538944 | tf_op jit(solution)/shard_map/reduce_scatter | solution.py:751
  231.8 148.7 %reduce-scatter.6.cloned.1.call-start = ((), (), s32[]{:S(2)}) async-start(), calls=%async_computation.18 | async-start | bytes 3538944 | tf_op jit(solution)/shard_map/reduce_scatter | solution.py:797
  243.9 16.2 %collective-permute-start.7 = (bf16[4,576,128]{2,1,0:T(8,128)(2,1)}, bf16[4,576,128]{2,1,0:T(8,128)(2,1)S(1)}, u32[]{:S(2)}, u32[]{:S(2)}) collective-permute-start(bf16[4,576,128]{2,1,0:T(8,128)(2,1)} %get-tuple-element.119), channel_id=1, source_target_pairs={{0,8},{8,16},{16,24},{24,0},{32,40},{40,48},{48,56},{56,32},{64,72... | collective-permute-start | bytes 1769480 | tf_op jit(solution)/shard_map/ppermute | solution.py:494
  245.2 15.9 %collective-permute-start.8 = (bf16[4,576,128]{2,1,0:T(8,128)(2,1)}, bf16[4,576,128]{2,1,0:T(8,128)(2,1)S(1)}, u32[]{:S(2)}, u32[]{:S(2)}) collective-permute-start(bf16[4,576,128]{2,1,0:T(8,128)(2,1)} %get-tuple-element.120), channel_id=1, source_target_pairs={{0,32},{8,40},{16,48},{24,56},{32,64},{40,72},{48,80},{56,88},{64,... | collective-permute-start | bytes 1769480 | tf_op jit(solution)/shard_map/ppermute | solution.py:494
  246.5 27.4 %collective-permute-start.9 = (bf16[4,576,128]{2,1,0:T(8,128)(2,1)}, bf16[4,576,128]{2,1,0:T(8,128)(2,1)S(1)}, u32[]{:S(2)}, u32[]{:S(2)}) collective-permute-start(bf16[4,576,128]{2,1,0:T(8,128)(2,1)} %get-tuple-element.121), channel_id=1, source_target_pairs={{0,16},{8,24},{16,0},{24,8},{32,48},{40,56},{48,32},{56,40},{64,80... | collective-permute-start | bytes 1769480 | tf_op jit(solution)/shard_map/ppermute | solution.py:494
  249.0 25.9 %collective-permute-start.10 = (bf16[4,576,128]{2,1,0:T(8,128)(2,1)}, bf16[4,576,128]{2,1,0:T(8,128)(2,1)}, u32[]{:S(2)}, u32[]{:S(2)}) collective-permute-start(bf16[4,576,128]{2,1,0:T(8,128)(2,1)} %get-tuple-element.122), channel_id=1, source_target_pairs={{0,64},{8,72},{16,80},{24,88},{32,96},{40,104},{48,112},{56,120},{... | collective-permute-start | bytes 1769480 | tf_op jit(solution)/shard_map/ppermute | solution.py:494
  280.8 43.6 %copy-start.12 = (f32[1024,256]{1,0:T(8,128)S(1)}, f32[1024,256]{1,0:T(8,128)}, u32[]{:S(2)}) copy-start(f32[1024,256]{1,0:T(8,128)} %get-tuple-element.107) | copy-start | bytes 3145732
  280.8 13.8 %collective-permute-start.11 = (bf16[4,576,128]{2,1,0:T(8,128)(2,1)}, bf16[4,576,128]{2,1,0:T(8,128)(2,1)S(1)}, u32[]{:S(2)}, u32[]{:S(2)}) collective-permute-start(bf16[4,576,128]{2,1,0:T(8,128)(2,1)} %get-tuple-element.125), channel_id=1, source_target_pairs={{0,24},{8,0},{16,8},{24,16},{32,56},{40,32},{48,40},{56,48},{64,88... | collective-permute-start | bytes 1769480 | tf_op jit(solution)/shard_map/ppermute | solution.py:494
  282.2 42.2 %all-to-all-start.4 = ((bf16[8,128,256]{2,1,0:T(8,128)(2,1)}), bf16[8,128,256]{2,1,0:T(8,128)(2,1)S(1)}, u32[]{:S(2)}, u32[]{:S(2)}) async-start(bf16[8,128,256]{2,1,0:T(8,128)(2,1)} %get-tuple-element.123), calls=%async_computation.5 | async-start | bytes 1048576 | tf_op jit(solution)/shard_map/all_to_all | solution.py:664
  287.3 22.9 %collective-permute-start.19 = (bf16[128,1536]{1,0:T(8,128)(2,1)}, bf16[128,1536]{1,0:T(8,128)(2,1)}, u32[]{:S(2)}, u32[]{:S(2)}) collective-permute-start(bf16[128,1536]{1,0:T(8,128)(2,1)} %get-tuple-element.139.refs_0_), channel_id=1, source_target_pairs={{0,2},{1,3},{2,4},{3,5},{4,6},{5,7},{6,0},{7,1},{8,10},{9,11},{10,... | collective-permute-start | bytes 1179656 | tf_op jit(solution)/shard_map/ppermute | solution.py:778
  288.7 34.9 %collective-permute-start.20 = (bf16[128,1536]{1,0:T(8,128)(2,1)}, bf16[128,1536]{1,0:T(8,128)(2,1)}, u32[]{:S(2)}, u32[]{:S(2)}) collective-permute-start(bf16[128,1536]{1,0:T(8,128)(2,1)} %get-tuple-element.139.refs_0_), channel_id=1, source_target_pairs={{0,4},{1,5},{2,6},{3,7},{4,0},{5,1},{6,2},{7,3},{8,12},{9,13},{10,... | collective-permute-start | bytes 1179656 | tf_op jit(solution)/shard_map/ppermute | solution.py:778
  291.1 33.3 %collective-permute-start.21 = (bf16[128,1536]{1,0:T(8,128)(2,1)}, bf16[128,1536]{1,0:T(8,128)(2,1)}, u32[]{:S(2)}, u32[]{:S(2)}) collective-permute-start(bf16[128,1536]{1,0:T(8,128)(2,1)} %get-tuple-element.139.refs_0_), channel_id=1, source_target_pairs={{0,6},{1,7},{2,0},{3,1},{4,2},{5,3},{6,4},{7,5},{8,14},{9,15},{10,... | collective-permute-start | bytes 1179656 | tf_op jit(solution)/shard_map/ppermute | solution.py:778
  292.3 38.1 %collective-permute-start.12 = (bf16[4,576,128]{2,1,0:T(8,128)(2,1)}, bf16[4,576,128]{2,1,0:T(8,128)(2,1)}, u32[]{:S(2)}, u32[]{:S(2)}) collective-permute-start(bf16[4,576,128]{2,1,0:T(8,128)(2,1)} %get-tuple-element.127), channel_id=1, source_target_pairs={{0,96},{8,104},{16,112},{24,120},{32,0},{40,8},{48,16},{56,24},{64... | collective-permute-start | bytes 1769480 | tf_op jit(solution)/shard_map/ppermute | solution.py:494
  294.7 49.3 %collective-permute-start.22 = (bf16[128,1536]{1,0:T(8,128)(2,1)}, bf16[128,1536]{1,0:T(8,128)(2,1)}, u32[]{:S(2)}, u32[]{:S(2)}) collective-permute-start(bf16[128,1536]{1,0:T(8,128)(2,1)} %get-tuple-element.139.refs_0_), channel_id=1, source_target_pairs={{0,1},{1,0},{2,3},{3,2},{4,5},{5,4},{6,7},{7,6},{8,9},{9,8},{10,11... | collective-permute-start | bytes 1179656 | tf_op jit(solution)/shard_map/ppermute | solution.py:780
  310.2 34.1 %collective-permute-start.23 = (bf16[128,1536]{1,0:T(8,128)(2,1)}, bf16[128,1536]{1,0:T(8,128)(2,1)}, u32[]{:S(2)}, u32[]{:S(2)}) collective-permute-start(bf16[128,1536]{1,0:T(8,128)(2,1)} %collective-permute-done.19.refs_1_), channel_id=1, source_target_pairs={{0,1},{1,0},{2,3},{3,2},{4,5},{5,4},{6,7},{7,6},{8,9},{9,8},{10,11... | collective-permute-start | bytes 1179656 | tf_op jit(solution)/shard_map/ppermute | solution.py:780
  323.5 21.5 %collective-permute-start.24 = (bf16[128,1536]{1,0:T(8,128)(2,1)}, bf16[128,1536]{1,0:T(8,128)(2,1)}, u32[]{:S(2)}, u32[]{:S(2)}) collective-permute-start(bf16[128,1536]{1,0:T(8,128)(2,1)} %collective-permute-done.20.refs_2_), channel_id=1, source_target_pairs={{0,1},{1,0},{2,3},{3,2},{4,5},{5,4},{6,7},{7,6},{8,9},{9,8},{10,11... | collective-permute-start | bytes 1179656 | tf_op jit(solution)/shard_map/ppermute | solution.py:780
  324.4 22.6 %collective-permute-start.25 = (bf16[128,1536]{1,0:T(8,128)(2,1)}, bf16[128,1536]{1,0:T(8,128)(2,1)}, u32[]{:S(2)}, u32[]{:S(2)}) collective-permute-start(bf16[128,1536]{1,0:T(8,128)(2,1)} %collective-permute-done.21.refs_3_), channel_id=1, source_target_pairs={{0,1},{1,0},{2,3},{3,2},{4,5},{5,4},{6,7},{7,6},{8,9},{9,8},{10,11... | collective-permute-start | bytes 1179656 | tf_op jit(solution)/shard_map/ppermute | solution.py:780
  326.6 26.1 %all-to-all-start.5 = ((bf16[16,128,128]{2,1,0:T(8,128)(2,1)}), bf16[16,128,128]{2,1,0:T(8,128)(2,1)S(1)}, u32[]{:S(2)}, u32[]{:S(2)}) async-start(bf16[16,128,128]{2,1,0:T(8,128)(2,1)} %bitcast.17), calls=%async_computation.6 | async-start | bytes 1048576 | tf_op jit(solution)/shard_map/all_to_all | solution.py:664
  334.4 9.6 %collective-permute-start.13 = (bf16[576,128]{1,0:T(8,128)(2,1)}, bf16[576,128]{1,0:T(8,128)(2,1)S(1)}, u32[]{:S(2)}, u32[]{:S(2)}) collective-permute-start(bf16[576,128]{1,0:T(8,128)(2,1)} %get-tuple-element.129), channel_id=1, source_target_pairs={{0,32},{8,40},{16,48},{24,56},{32,64},{40,72},{48,80},{56,88},{64,... | collective-permute-start | bytes 442376 | tf_op jit(solution)/shard_map/ppermute | solution.py:494
  344.0 7.7 %collective-permute-start.14 = (bf16[576,128]{1,0:T(8,128)(2,1)}, bf16[576,128]{1,0:T(8,128)(2,1)S(1)}, u32[]{:S(2)}, u32[]{:S(2)}) collective-permute-start(bf16[576,128]{1,0:T(8,128)(2,1)} %get-tuple-element.130), channel_id=1, source_target_pairs={{0,64},{8,72},{16,80},{24,88},{32,96},{40,104},{48,112},{56,120},{... | collective-permute-start | bytes 442376 | tf_op jit(solution)/shard_map/ppermute | solution.py:494
  344.0 7.7 %collective-permute-start.15 = (bf16[576,128]{1,0:T(8,128)(2,1)}, bf16[576,128]{1,0:T(8,128)(2,1)S(1)}, u32[]{:S(2)}, u32[]{:S(2)}) collective-permute-start(bf16[576,128]{1,0:T(8,128)(2,1)} %get-tuple-element.131), channel_id=1, source_target_pairs={{0,96},{8,104},{16,112},{24,120},{32,0},{40,8},{48,16},{56,24},{64... | collective-permute-start | bytes 442376 | tf_op jit(solution)/shard_map/ppermute | solution.py:494
  344.3 7.4 %collective-permute-start.16 = (bf16[576,128]{1,0:T(8,128)(2,1)}, bf16[576,128]{1,0:T(8,128)(2,1)S(1)}, u32[]{:S(2)}, u32[]{:S(2)}) collective-permute-start(bf16[576,128]{1,0:T(8,128)(2,1)} %get-tuple-element.133), channel_id=1, source_target_pairs={{0,8},{8,16},{16,24},{24,0},{32,40},{40,48},{48,56},{56,32},{64,72... | collective-permute-start | bytes 442376 | tf_op jit(solution)/shard_map/ppermute | solution.py:494
  345.1 6.9 %collective-permute-start.17 = (bf16[576,128]{1,0:T(8,128)(2,1)}, bf16[576,128]{1,0:T(8,128)(2,1)S(1)}, u32[]{:S(2)}, u32[]{:S(2)}) collective-permute-start(bf16[576,128]{1,0:T(8,128)(2,1)} %get-tuple-element.134), channel_id=1, source_target_pairs={{0,16},{8,24},{16,0},{24,8},{32,48},{40,56},{48,32},{56,40},{64,80... | collective-permute-start | bytes 442376 | tf_op jit(solution)/shard_map/ppermute | solution.py:494
  347.0 5.7 %collective-permute-start.18 = (bf16[576,128]{1,0:T(8,128)(2,1)}, bf16[576,128]{1,0:T(8,128)(2,1)S(1)}, u32[]{:S(2)}, u32[]{:S(2)}) collective-permute-start(bf16[576,128]{1,0:T(8,128)(2,1)} %get-tuple-element.135), channel_id=1, source_target_pairs={{0,24},{8,0},{16,8},{24,16},{32,56},{40,32},{48,40},{56,48},{64,88... | collective-permute-start | bytes 442376 | tf_op jit(solution)/shard_map/ppermute | solution.py:494
  355.5 24.9 %all-to-all-start.6 = ((bf16[8,96,128]{2,1,0:T(8,128)(2,1)}), bf16[8,96,128]{2,1,0:T(8,128)(2,1)S(1)}, u32[]{:S(2)}, u32[]{:S(2)}) async-start(bf16[8,96,128]{2,1,0:T(8,128)(2,1)} %get-tuple-element.148), calls=%async_computation.7 | async-start | bytes 393216 | tf_op jit(solution)/shard_map/all_to_all | solution.py:664
  361.8 132.7 %all-gather.15.cloned.1.call-start = ((), (), s32[]{:S(2)}) async-start(), calls=%async_computation.19 | async-start | bytes 5013504 | tf_op jit(solution)/shard_map/all_gather | solution.py:668
  381.2 120.4 %reduce-scatter.8.cloned.1.call-start = ((), (), s32[]{:S(2)}) async-start(), calls=%async_computation.20 | async-start | bytes 3981312 | tf_op jit(solution)/shard_map/reduce_scatter | solution.py:830
  444.4 50.1 %all-to-all-start.8 = ((bf16[128,80,128]{2,1,0:T(8,128)(2,1)}), bf16[128,80,128]{2,1,0:T(8,128)(2,1)S(1)}, u32[]{:S(2)}, u32[]{:S(2)}) async-start(bf16[128,80,128]{2,1,0:T(8,128)(2,1)} %bitcast.21), calls=%async_computation.10 | async-start | bytes 5242880 | tf_op jit(solution)/shard_map/all_to_all | solution.py:664
  450.6 51.8 %copy-start.14 = (f32[128,1536]{1,0:T(8,128)S(1)}, f32[128,1536]{1,0:T(8,128)}, u32[]{:S(2)}) copy-start(f32[128,1536]{1,0:T(8,128)} %get-tuple-element.111.h_ref) | copy-start | bytes 2359300
  450.7 107.4 %all-gather.17.cloned.1.call-start = ((), (), s32[]{:S(2)}) async-start(), calls=%async_computation.21 | async-start | bytes 3411968 | tf_op jit(solution)/shard_map/all_gather | solution.py:668
  511.3 16.7 %all-to-all-start.9 = ((bf16[16,8,1536]{2,1,0:T(8,128)(2,1)}), bf16[16,8,1536]{2,1,0:T(8,128)(2,1)S(1)}, u32[]{:S(2)}, u32[]{:S(2)}) async-start(bf16[16,8,1536]{2,1,0:T(8,128)(2,1)} %broadcast_in_dim.73), calls=%async_computation.12 | async-start | bytes 786432 | tf_op jit(solution)/shard_map/all_to_all | solution.py:664
  (32 other events, 205.4 us)
Sparse Core Ops, SparseCore 0:
  15.1 43.8 all-gather.6
  72.7 49.9 all-gather.8
  124.4 40.4 all-gather.10
  190.7 24.1 all-gather.12
  231.9 32.7 reduce-scatter.3
  281.0 52.6 reduce-scatter.5
  381.3 70.5 all-gather.14
  454.4 47.1 reduce-scatter.7
  504.5 53.5 all-gather.16

commit v2 on v1

--- a/solution.py
+++ b/solution.py
@@ -46,13 +46,18 @@
     )(*args)
 
 
-def pack_kernel(wq, wk, wv, wf, g1, g2, out):
+def pack_kernel(ids, bm_ref, len_ref, x, cot, wq, wk, wv, wf, gain, wo, wg, wu, out, x_out, c_out):
+    row = lax.broadcasted_iota(jnp.int32, (128, 128), 0)
+    first, second = bm_ref[2 * ids[4]] * 64, bm_ref[2 * ids[4] + 1] * 64
+    pos = row + jnp.where(row < 64, first, second - 64)
+    live = jnp.where(pos < len_ref[0], 1.0, 0.0)[:, 0:1]
+    x_out[...] = x[...]
+    c_out[...] = jnp.where(live > 0.5, cot[...].astype(F32), 0.0).astype(BF16)
     lane = lax.broadcasted_iota(jnp.int32, (192, 64), 1)
     rows = jnp.concatenate(
-        [g1[...].astype(F32), g2[...].astype(F32), jnp.zeros((6, 192), F32)], 0
+        [wf[...].astype(F32), gain[...].astype(F32), jnp.zeros((6, 192), F32)], 0
     ).T
-    base = jnp.where(lane == 3, rows[:, 0:1], jnp.where(lane == 4, rows[:, 1:2], 0.0))
-    forget = wf[...].astype(F32)
+    base = jnp.where(lane == 3, rows[:, 24:25], jnp.where(lane == 4, rows[:, 25:26], 0.0))
     for d in range(8):
         parts = []
         for h in range(3):
@@ -60,47 +65,48 @@
             parts += [wq[:, at : at + 64], wk[:, at : at + 64], wv[:, at : at + 64]]
         ext = base
         for h in range(3):
-            ext = jnp.where(lane == h, forget[:, 3 * d + h : 3 * d + h + 1], ext)
+            ext = jnp.where(lane == h, rows[:, 3 * d + h : 3 * d + h + 1], ext)
         parts.append(ext.astype(BF16))
-        for m in range(5):
-            out[d, :, m * 128 : (m + 1) * 128] = jnp.concatenate(
+        heads = [wo[:, d * 192 + h * 64 : d * 192 + h * 64 + 64] for h in range(3)]
+        parts += [heads[0], heads[1], heads[1], heads[2]]
+        for m in range(7):
+            out[d, 0:192, m * 128 : (m + 1) * 128] = jnp.concatenate(
                 [parts[2 * m], parts[2 * m + 1]], 1
             )
-
-
-def pack_two_kernel(f_ref, wg, wu, wo, *refs):
-    outs, all_s = refs[:8], refs[8]
-    for d in range(8):
-        all_s[d, :, 0:512] = wg[:, d * 512 : (d + 1) * 512]
-        all_s[d, :, 512:1024] = wu[:, d * 512 : (d + 1) * 512]
-        at = d * 192
-        heads = [wo[:, at + h * 64 : at + h * 64 + 64] for h in range(3)]
-        all_s[d, :, 1024:1152] = jnp.concatenate([heads[0], heads[1]], 1)
-        all_s[d, :, 1152:1280] = jnp.concatenate([heads[1], heads[2]], 1)
-    for k in range(8):
-        outs[k][...] = all_s[lax.rem(f_ref[0] + k, 8)]
-
-
-def place_kernel(f_ref, n1, *refs):
-    ins, w2, sig = refs[:8], refs[8], refs[9]
-    for k in range(8):
-        at = pl.multiple_of(lax.rem(f_ref[0] + 8 - k, 8) * 192, 64)
-        w2[pl.ds(at, 192), :] = ins[k][...]
-    sig[...] = jax.nn.sigmoid(dot(n1[...], w2[:, 1024:1280]))
-
-
-def mask_kernel(live, c, _n1, out):
-    keep = live[:, 0:1] > 0.5
-    out[...] = jnp.where(keep, c[...].astype(F32), 0.0).astype(BF16)
-
-
-def proj_kernel(x, w1, bias, _part, n1, send, fpre, gains):
-    gains[...] = w1[:, 512:640].astype(F32).T[64:72]
+        out[d, 192:208, 768:896] = jnp.zeros((16, 128), BF16)
+    for half in range(2):
+
+        @pl.when(ids[1] // 2 == half)
+        def _():
+            w = (wg, wu)[half]
+            for d in range(8):
+                for b in range(6):
+                    lt, part = divmod(b, 3)
+                    at = pl.multiple_of(ids[0] * 48 + part * 16, 16)
+                    col = pl.multiple_of(lax.rem(ids[1], 2) * 256 + (d * 512 + lt * 128), 128)
+                    out[d, 192:208, b * 128 : (b + 1) * 128] = w[pl.ds(at, 16), pl.ds(col, 128)]
+
+
+def open_kernel(n1, w1, _a, sig):
+    sig[...] = jax.nn.sigmoid(dot(n1[...], w1[:, 640:896]))
+
+
+def proj_kernel(x, w1r, bias, wo, n1, send, fpre, gains, w1, w2, wo_out):
+    @pl.when(pl.program_id(0) == 0)
+    def _():
+        for f in range(8):
+            w1[f * 192 : (f + 1) * 192, :] = w1r[f, 0:192, :]
+            for b in range(6):
+                at = f * 96 + b * 16
+                w2[at : at + 16, :] = w1r[f, 192:208, b * 128 : (b + 1) * 128]
+        wo_out[...] = wo[...]
+        gains[...] = w1[:, 512:640].astype(F32).T[64:72]
+
     x32 = x[...].astype(F32)
     r1 = lax.rsqrt(jnp.mean(x32 * x32, -1, keepdims=True) + EPS)
     normed = (x32 * r1 * gains[3:4]).astype(BF16)
     n1[...] = normed
-    proj = dot(normed, w1[...])
+    proj = dot(normed, w1[:, 0:640])
     rows = proj[:, 512:640].T[64:72] + bias[...]
     fpre[...] = rows
     logs = jnp.minimum(rows, 0.0) - jnp.log1p(jnp.exp(-jnp.abs(rows)))
@@ -119,7 +125,7 @@
             send[2 * s + j, 128:144, :] = jnp.broadcast_to(line, (16, 384)).astype(BF16)
 
 
-def project(x_all, w1, bias, after):
+def project(x_all, w1r, bias, wo):
     def fixed(*dims):
         return pl.BlockSpec(dims, lambda i: (0,) * len(dims))
 
@@ -131,25 +137,31 @@
             shape(16, 144, 384),
             shape(8, 1024, dtype=F32),
             shape(8, 1536, dtype=F32),
+            shape(1536, 896),
+            shape(768, 128),
+            shape(192, 1536),
         ),
         in_specs=[
             pl.BlockSpec((512, 1536), lambda i: (i, 0)),
-            fixed(1536, 640),
+            fixed(8, 208, 896),
             fixed(8, 1),
-            ANY,
+            fixed(192, 1536),
         ],
         out_specs=(
             pl.BlockSpec((512, 1536), lambda i: (i, 0)),
             pl.BlockSpec((8, 144, 384), lambda i: (i, 0, 0)),
             pl.BlockSpec((8, 512), lambda i: (0, i)),
             fixed(8, 1536),
+            fixed(1536, 896),
+            fixed(768, 128),
+            fixed(192, 1536),
         ),
-        compiler_params=pltpu.CompilerParams(vmem_limit_bytes=40 * MIB),
+        compiler_params=pltpu.CompilerParams(vmem_limit_bytes=60 * MIB),
         cost_estimate=pl.CostEstimate(
             flops=2 * 10**9, bytes_accessed=10**7, transcendentals=0
         ),
         name="project",
-    )(x_all, w1, bias, after)
+    )(x_all, w1r, bias, wo)
 
 
 def score_cols(hs, b, q_s, k_s, fc_s, fr):
@@ -198,8 +210,8 @@
     fc_s[1] = both[:, 1:2]
 
 
-def fwd_kernel(bm_ref, j_ref, r1, fr, _a, _b, _c, o_ref, attn_ref, l_ref, q_s, k_s, v_s, vt_s, fc_s, o_s):
-    j = j_ref[0]
+def fwd_kernel(bm_ref, ids, r1, fr, _a, _b, _c, o_ref, attn_ref, l_ref, q_s, k_s, v_s, vt_s, fc_s, o_s):
+    j = ids[3]
     load_heads(bm_ref, r1, q_s, k_s, v_s)
     column_decay(fr, fc_s)
     for hs in range(2):
@@ -243,11 +255,11 @@
 
 
 def bwd_kernel(
-    bm_ref, j_ref, r1, da_r, attn_ref, l_ref, fr, go,
+    bm_ref, ids, r1, da_r, attn_ref, l_ref, fr, go,
     ds_ref,
     q_s, k_s, v_s, da_s, kt_s, fc_s, dk_s, dv_s, out_s, rs_ref, dl_s,
 ):
-    j = j_ref[0]
+    j = ids[3]
     for c in range(16):
         ds_ref[c, 144:192, :] = go[c]
     load_heads(bm_ref, r1, q_s, k_s, v_s)
@@ -304,12 +316,12 @@
 HEADS = [pltpu.VMEM((2, SPAN, HD), BF16)] * 3
 
 
-def attend(block_map, j, r1, decay, after):
+def attend(block_map, ids, r1, decay, after):
     return call(
         fwd_kernel,
         (shape(16, 128, 128), shape(2, SPAN, HD, dtype=F32), shape(2, 1, SPAN, dtype=F32)),
         "attend",
-        (block_map, j, r1, decay, *after),
+        (block_map, ids, r1, decay, *after),
         HEADS
         + [
             pltpu.VMEM((2, 80, SPAN), BF16),
@@ -321,12 +333,12 @@
     )
 
 
-def attend_back(block_map, j, r1, upstream, attn, logs, decay, go):
+def attend_back(block_map, ids, r1, upstream, attn, logs, decay, go):
     return call(
         bwd_kernel,
         shape(16, 192, 384),
         "attend_back",
-        (block_map, j, r1, upstream, attn, logs, decay, go),
+        (block_map, ids, r1, upstream, attn, logs, decay, go),
         HEADS
         + [
             pltpu.VMEM((2, SPAN, HD), BF16),
@@ -356,7 +368,7 @@
 
 
 def mid_back_kernel(
-    dn2_r, h_ref, r2_ref, c_ref, gains, wo, _a, _b, _c, _d,
+    dn2_r, h_ref, r2_ref, c_ref, gains, wo, _after,
     dh_ref, da_ref, do_ref, g2_ref,
 ):
     h = h_ref[...]
@@ -378,8 +390,23 @@
         do_ref[f, :, 128:256] = dot(da, wo[at + 64 : at + 192, :], NT).astype(BF16)
 
 
+def ready_kernel(ids, w2g, *refs):
+    parts, w2, c_all = refs[:8], refs[8], refs[9]
+    for k in range(8):
+        first = ids[2] if k < 4 else ids[2] + 1 - 2 * lax.rem(ids[2], 2)
+        slot = lax.rem(first + 8 - 2 * (k % 4), 8)
+        c_all[pl.ds(pl.multiple_of(slot * 128, 128), 128), :] = parts[k][...]
+    for p in range(16):
+        cr, cc = divmod(p, 4)
+        for f in range(8):
+            for lt in range(2):
+                row, col = f * 192 + cr * 48, cc * 256 + lt * 128
+                at = f * 96 + lt * 48
+                w2[row : row + 48, col : col + 128] = w2g[p, at : at + 48, :]
+
+
 def ffn_kernel(n2, c, w2, wd, dn2_ref, ffo_ref, u_ref, dpre_ref):
-    pre = dot(n2[...], w2[:, 0:1024])
+    pre = dot(n2[...], w2[...])
     gate, up = pre[:, 0:512], pre[:, 512:1024]
     sig = jax.nn.sigmoid(gate)
     act = gate * sig
@@ -390,7 +417,7 @@
     dup = (du * act).astype(BF16)
     dpre = jnp.concatenate([dgate, dup], 1)
     dpre_ref[...] = dpre
-    dn2_ref[...] = dot(dpre, w2[:, 0:1024], NT).astype(BF16)
+    dn2_ref[...] = dot(dpre, w2[...], NT).astype(BF16)
     ffo_ref[...] = dot(u, wd[...]).astype(BF16)
 
 
@@ -408,7 +435,7 @@
         in_specs=[
             pl.BlockSpec((rows, 1536), lambda i: (i, 0)),
             pl.BlockSpec((rows, 1536), lambda i: (i, 0)),
-            pl.BlockSpec((1536, 1280), lambda i: (0, 0)),
+            pl.BlockSpec((1536, 1024), lambda i: (0, 0)),
             pl.BlockSpec((512, 1536), lambda i: (0, 0)),
         ],
         out_specs=(
@@ -417,7 +444,7 @@
             pl.BlockSpec((rows, 512), lambda i: (i, 0)),
             pl.BlockSpec((rows, 1024), lambda i: (i, 0)),
         ),
-        compiler_params=pltpu.CompilerParams(vmem_limit_bytes=48 * MIB),
+        compiler_params=pltpu.CompilerParams(vmem_limit_bytes=56 * MIB),
         cost_estimate=pl.CostEstimate(
             flops=10**10, bytes_accessed=2 * 10**7, transcendentals=0
         ),
@@ -425,11 +452,7 @@
     )(n2, c_all, w2, wd)
 
 
-HALF = 576
-
-
-def ffn_grad_kernel(zy_ref, n2, dpre, u, c, *refs):
-    outs, all_s = refs[:8], refs[8]
+def ffn_grad_kernel(n2, dpre, u, c, out):
     for part in range(4):
         g = dot(n2[:, part * 384 : (part + 1) * 384], dpre[...], TN).astype(BF16)
         for sub in range(2):
@@ -438,7 +461,7 @@
                 for col in range(8):
                     cc, half = divmod(col, 2)
                     at = f * 96 + half * 48
-                    all_s[cr * 4 + cc, at : at + 48, :] = g[
+                    out[cr * 4 + cc, at : at + 48, :] = g[
                         sub * 192 + cr * 48 : sub * 192 + cr * 48 + 48,
                         col * 128 : (col + 1) * 128,
                     ]
@@ -447,64 +470,19 @@
         for sub in range(4):
             for col in range(12):
                 at = 768 + col * 32
-                all_s[4 * part + sub, at : at + 32, :] = g[
+                out[4 * part + sub, at : at + 32, :] = g[
                     sub * 32 : sub * 32 + 32, col * 128 : (col + 1) * 128
                 ]
-    for k in range(4):
-        y = lax.rem(zy_ref[1] + k, 4)
-        z = lax.rem(zy_ref[0] + k, 4)
-        for i in range(4):
-            outs[k][i] = all_s[i * 4 + y, 0:HALF, :]
-            outs[4 + k][i] = all_s[z * 4 + i, HALF:1152, :]
-
-
-def first_sum_kernel(zy_ref, *refs):
-    ins, outs, acc_s = refs[:8], refs[8:16], refs[16]
-    for half in range(2):
-        for i in range(4):
-            acc = ins[4 * half][i].astype(F32)
-            for k in range(1, 4):
-                acc += ins[4 * half + k][i].astype(F32)
-            acc_s[half, i] = acc.astype(BF16)
-        for k in range(4):
-            outs[4 * half + k][...] = acc_s[half, lax.rem(zy_ref[half] + k, 4)]
-
-
-def second_sum_kernel(*refs):
-    ins, cols, down = refs[:8], refs[8], refs[9]
-    sums = []
-    for half in range(2):
-        acc = ins[4 * half][...].astype(F32)
-        for k in range(1, 4):
-            acc += ins[4 * half + k][...].astype(F32)
-        sums.append(acc.astype(BF16))
-    full = jnp.concatenate(sums, 0)
-    cols[...] = full[0:768].reshape(8, 96, 128)
-    down[...] = full[768:1152]
-
-
-def shift(arrays, axis):
-    out = [arrays[0]]
-    for k in range(1, 4):
-        pairs = []
-        for z in range(4):
-            for y in range(4):
-                to = ((z + k) % 4, y) if axis == 0 else (z, (y + k) % 4)
-                pairs.append((z * 4 + y, to[0] * 4 + to[1]))
-        out.append(lax.ppermute(arrays[k], "ctx", pairs))
-    return out
-
-
-def out_grad_kernel(f_ref, o, *refs):
-    pieces, out, o_s, da_s = refs[:8], refs[8], refs[9], refs[10]
-    fi = f_ref[0]
+
+
+def split_kernel(ids, r, _after, *outs):
     for k in range(8):
-        first = fi if k < 4 else fi + 1 - 2 * lax.rem(fi, 2)
-        slot = lax.rem(first + 8 - 2 * (k % 4), 8)
-        at = pl.multiple_of(slot * 128, 128)
-        o_s[k * 128 : (k + 1) * 128, :] = o[pl.ds(at, 128), :]
-        da_s[k * 128 : (k + 1) * 128, :] = pieces[k][...]
-    t = dot(o_s[...], da_s[...], TN)
+        at = pl.multiple_of(lax.rem(ids[2] + k, 8) * 96, 16)
+        outs[k][...] = r[pl.ds(at, 96), :]
+
+
+def out_grad_kernel(o, da, out):
+    t = dot(o[...], da[...], TN)
     t = jnp.concatenate([t[0:64], t[64:128] + t[128:192], t[192:256]], 0).astype(BF16)
     for c in range(16):
         cr, cc = divmod(c, 4)
@@ -517,7 +495,7 @@
         dproj[s * 128 : (s + 1) * 128, :] = jnp.concatenate(
             [d0[0:128, 0:192], d0[0:128, 192:384] + d1[0:128, 0:192], d1[0:128, 192:384]], 1
         )
-    for c in (14, 15):
+    for c in (3, 7, 11, 15):
         out[c] = jnp.zeros((8, 80, 128), BF16)
     for part in range(2):
         left = n1[:, part * 768 : (part + 1) * 768]
@@ -529,7 +507,8 @@
             f = 4 * part + sub
             for t in range(72):
                 rt, lt = divmod(t, 6)
-                c, slot = divmod(t, 5)
+                c, slot = divmod((rt % 3) * 6 + lt, 5)
+                c += rt // 3 * 4
                 row = sub * 192 + rt * 16
                 out[c, f, slot * 16 : (slot + 1) * 16, :] = g[
                     row : row + 16, lt * 128 : (lt + 1) * 128
@@ -537,9 +516,9 @@
 
 
 def input_grad_kernel(
-    f_ref, dproj, dlog2, dl, fpre, w1, w2, gains, n1, gain2, out
+    ids, dproj, dlog2, dl, fpre, w1, gains, n1, gain2, ffo, out
 ):
-    fi = f_ref[0]
+    fi = ids[2]
     rows = [[], [], []]
     for s in range(8):
         d0 = dl[2 * s : 2 * s + 1].astype(F32)
@@ -558,7 +537,7 @@
         at = p * 256
         part = (
             dot(dproj[at : at + 256, :], w1[:, 0:576], NT)
-            + dot(dlog2[at : at + 256, :], w2[:, 1024:1280], NT)
+            + dot(dlog2[at : at + 256, :], w1[:, 640:896], NT)
             + dot(dfpre[:, at : at + 256], w_forget, TN)
         )
         gain1 += jnp.sum(part * n1[at : at + 256, :].astype(F32), 0, keepdims=True)
@@ -583,65 +562,70 @@
             0,
         )
         out[d, 128:144, :] = jnp.concatenate([top, low], 0).astype(BF16)
-
-
-def head_sum_kernel(r, go, out):
+        out[d, 144:272, :] = ffo[d * 128 : (d + 1) * 128, :]
+
+
+def head_sum_kernel(r, go, mine, *refs):
+    cols, out = refs[:8], refs[8]
+    for k in range(8):
+        out[k * 96 : (k + 1) * 96, :] = cols[k][...]
+    out[768:1152, :] = mine[768:1152, :]
     for f in range(8):
         acc = r[0, f].astype(F32)
         for c in range(1, 16):
             acc += r[c, f].astype(F32)
-        out[f * 80 : (f + 1) * 80, :] = acc.astype(BF16)
+        at = 1152 + f * 80
+        out[at : at + 80, :] = acc.astype(BF16)
     acc = go[0].astype(F32)
     for c in range(1, 16):
         acc += go[c].astype(F32)
     for lt in range(3):
-        out[640 + lt * 48 : 688 + lt * 48, :] = acc[:, lt * 128 : (lt + 1) * 128].astype(BF16)
-
-
-def unpack_ffn_kernel(r, gate, up, down):
+        at = 1792 + lt * 48
+        out[at : at + 48, :] = acc[:, lt * 128 : (lt + 1) * 128].astype(BF16)
+
+
+def small_sum_kernel(r, out):
+    acc = r[0].astype(F32)
+    for c in range(1, 16):
+        acc += r[c].astype(F32)
+    out[...] = acc
+
+
+def finish_kernel(dn1, dh, x, gains, out):
+    x32 = x[...].astype(F32)
+    r1 = lax.rsqrt(jnp.mean(x32 * x32, -1, keepdims=True) + EPS)
+    scaled = dn1[0:128, :].astype(F32) * gains[3:4]
+    out[...] = (
+        dh[...]
+        + r1 * scaled
+        - x32 * (r1 * r1 * r1) * jnp.mean(scaled * x32, -1, keepdims=True)
+    ).astype(BF16)
+
+
+def unpack_kernel(ids, r, q, k, v, g, o, gate, up, down):
     for cc in range(4):
         to = gate if cc < 2 else up
-        for f in range(8):
+        for d in range(8):
+            f = lax.rem(ids[2] + 8 - d, 8)
             for half in range(2):
-                at = f * 96 + half * 48
-                col = f * 512 + (cc % 2) * 256 + half * 128
-                to[:, col : col + 128] = r[cc, at : at + 48, :].astype(F32)
+                at = d * 96 + half * 48
+                col = pl.multiple_of(f * 512 + ((cc % 2) * 256 + half * 128), 128)
+                to[:, pl.ds(col, 128)] = r[cc, at : at + 48, :].astype(F32)
         for col in range(12):
             at = 768 + col * 32
             down[cc * 32 : (cc + 1) * 32, col * 128 : (col + 1) * 128] = r[
                 cc, at : at + 32, :
             ].astype(F32)
-
-
-def unpack_ffn(gathered):
-    return pl.pallas_call(
-        unpack_ffn_kernel,
-        grid=(4,),
-        out_shape=(
-            shape(192, 4096, dtype=F32),
-            shape(192, 4096, dtype=F32),
-            shape(512, 1536, dtype=F32),
-        ),
-        in_specs=[pl.BlockSpec((4, 1152, 128), lambda i: (i, 0, 0))],
-        out_specs=(
-            pl.BlockSpec((48, 4096), lambda i: (i, 0)),
-            pl.BlockSpec((48, 4096), lambda i: (i, 0)),
-            pl.BlockSpec((128, 1536), lambda i: (i, 0)),
-        ),
-        compiler_params=pltpu.CompilerParams(vmem_limit_bytes=40 * MIB),
-        cost_estimate=pl.CostEstimate(flops=0, bytes_accessed=2 * 10**7, transcendentals=0),
-        name="unpack_ffn",
-    )(gathered)
-
-
-def unpack_kernel(r, q, k, v, g, o):
-    for rt in range(12):
+        for lt in range(3):
+            col = cc * 384 + lt * 128
+            o[:, col : col + 128] = r[cc, 1792 + lt * 48 : 1840 + lt * 48, :].astype(F32)
+    for rt in range(3):
         rows = [[], [], [], []]
         for f in range(8):
             tiles = []
             for lt in range(6):
                 c, slot = divmod(rt * 6 + lt, 5)
-                at = f * 80 + slot * 16
+                at = 1152 + f * 80 + slot * 16
                 tiles.append(r[c, at : at + 16, :].astype(F32))
             line = jnp.concatenate(tiles, 1)
             for h in range(3):
@@ -651,13 +635,36 @@
             rows[3].append(line[:, 576:768])
         for w, to in enumerate((q, k, v, g)):
             to[rt * 16 : (rt + 1) * 16, :] = jnp.concatenate(rows[w], 1)
-    for c in range(16):
-        cr, cc = divmod(c, 4)
-        for lt in range(3):
-            col = cc * 384 + lt * 128
-            o[cr * 48 : (cr + 1) * 48, col : col + 128] = r[
-                c, 640 + lt * 48 : 688 + lt * 48, :
-            ].astype(F32)
+
+
+def unpack(ids, total):
+    def rows(n, width):
+        return shape(4 * n, width, dtype=F32), pl.BlockSpec((n, width), lambda i: (i, 0))
+
+    outs = [rows(48, 1536)] * 5 + [rows(48, 4096)] * 2 + [rows(128, 1536)]
+    return pl.pallas_call(
+        unpack_kernel,
+        grid=(4,),
+        out_shape=tuple(a for a, _ in outs),
+        in_specs=[SMEM, pl.BlockSpec((4, 1936, 128), lambda i: (i, 0, 0))],
+        out_specs=tuple(b for _, b in outs),
+        compiler_params=pltpu.CompilerParams(vmem_limit_bytes=60 * MIB),
+        cost_estimate=pl.CostEstimate(
+            flops=6 * 10**10, bytes_accessed=3 * 10**7, transcendentals=0
+        ),
+        name="unpack",
+    )(ids, total)
+
+
+def after(array, *others):
+    return pl.pallas_call(
+        lambda *refs: None,
+        out_shape=jax.ShapeDtypeStruct(array.shape, array.dtype),
+        in_specs=[ANY] * (1 + len(others)),
+        out_specs=ANY,
+        input_output_aliases={0: 0},
+        name="after",
+    )(array, *others)
 
 
 def swap(array, axis):
@@ -678,51 +685,32 @@
 ):
     ci = lax.axis_index("ctx").astype(jnp.int32)
     fi = lax.axis_index("fsdp").astype(jnp.int32)
-    j = lax.rem(ci, 2)[None]
-    zy = jnp.stack([ci // 4, lax.rem(ci, 4)])
+    ids = jnp.stack([ci // 4, lax.rem(ci, 4), fi, lax.rem(ci, 2), ci])
     offsets = jnp.arange(64, dtype=jnp.int32)
-    own_blocks = lax.dynamic_slice_in_dim(block_map, 2 * ci, 2)
-    live = ((own_blocks[:, None] * 64 + offsets[None, :]).reshape(128) < lengths[0])[:, None]
     x_own = tokens[0]
-    live32 = jnp.broadcast_to(live.astype(F32), (128, 128))
-
-    w1 = call(
+
+    w1r, x_send, c_own = call(
         pack_kernel,
-        shape(8, 192, 640),
+        (shape(8, 208, 896), shape(128, 1536), shape(128, 1536)),
         "pack",
-        (w_query, w_key, w_value, w_forget, norm_gain[None], ffn_gain[None]),
-    )
-    x_own, w1 = tie(x_own, w1)
-    x_all = gather(x_own, "fsdp")
-    w1 = swap(w1, "fsdp").reshape(1536, 640)
-    parts = call(
-        pack_two_kernel,
-        (shape(192, 1280),) * 8,
-        "pack_two",
-        (fi[None], w_gate, w_up, w_outgate),
-        [pltpu.VMEM((8, 192, 1280), BF16)],
-        [SMEM] + [VMEM] * 3,
-    )
-    parts = [parts[0]] + [
-        lax.ppermute(parts[k], "fsdp", [(f, (f + k) % 8) for f in range(8)]) for k in range(1, 8)
+        (
+            ids, block_map, lengths, x_own, cotangent[0], w_query, w_key, w_value, w_forget.T,
+            jnp.stack([norm_gain, ffn_gain]), w_outgate, w_gate, w_up,
+        ),
+        ins=[SMEM] * 3 + [VMEM] * 10,
+    )
+    x_all = gather(x_send, "fsdp")
+    near = [c_own] + [
+        lax.ppermute(c_own, "fsdp", [(f, (f + 2 * k) % 8) for f in range(8)]) for k in range(1, 4)
     ]
-    w_output, x_all = tie(w_output, x_all)
-    wo_all = gather(w_output, "fsdp")
-
+    c_parts = near + [lax.ppermute(p, "fsdp", [(f, f ^ 1) for f in range(8)]) for p in near]
+    w1r = swap(w1r, "fsdp")
     bias = jnp.pad(forget_bias.astype(F32), (0, 5))[:, None]
-    n1, send, fpre, gains = project(x_all, w1, bias, parts[0])
-    c_own = call(
-        mask_kernel, shape(128, 1536), "mask", (live32, cotangent[0], n1), ins=[VMEM, VMEM, ANY]
-    )
-    c_all = gather(c_own, "fsdp")
+    n1, send, fpre, gains, w1, w2p, wo_own = project(x_all, w1r, bias, w_output)
+    wo_all = gather(wo_own, "fsdp")
+    w2g = gather(w2p, "ctx").reshape(16, 768, 128)
     recv = swap(send, "ctx")
-    w2, sig2 = call(
-        place_kernel,
-        (shape(1536, 1280), shape(1024, 256, dtype=F32)),
-        "place",
-        (fi[None], n1, *parts),
-        ins=[SMEM] + [VMEM] * 9,
-    )
+    sig2 = call(open_kernel, shape(1024, 256, dtype=F32), "open", (n1, w1, near[3]), ins=[VMEM] * 2 + [ANY])
 
     tri = (offsets[:, None] <= offsets[None, :]).astype(BF16)
     blocks = jnp.arange(32, dtype=jnp.int32)
@@ -734,12 +722,11 @@
     starts = jnp.sum(before[None, :, :] * within[:, None, :, 63], -1)
     decay = (within + starts[:, :, None]).reshape(2, 1, SPAN)
 
-    attn_own, attn, log_total = attend(block_map, j, recv, decay, parts[1:4])
+    attn_own, attn, log_total = attend(block_map, ids, recv, decay, [wo_all, *near[1:3]])
     attn2 = swap(attn_own, "ctx").reshape(8, 2, 128, 128).transpose(0, 2, 1, 3)
     attn2 = attn2.reshape(1024, 256)
     o2 = (attn2.astype(F32) * sig2).astype(BF16)
     o_own = swap(o2.reshape(8, 128, 256), "fsdp")
-    o_own, c_all = tie(o_own, c_all)
     h, n2_own, inv2 = call(
         mid_kernel,
         (shape(128, 1536, dtype=F32), shape(128, 1536), shape(128, 128, dtype=F32)),
@@ -747,20 +734,23 @@
         (o_own, wo_all, x_own, gains),
     )
     n2 = gather(n2_own, "fsdp")
+    w2, c_all = call(
+        ready_kernel,
+        (shape(1536, 1024), shape(1024, 1536)),
+        "ready",
+        (ids, w2g, *c_parts),
+        ins=[SMEM] + [VMEM] * 9,
+    )
     dn2, ffo, u, dpre = feed_forward(n2, c_all, w2, w_down)
     dn2 = lax.psum_scatter(dn2, "fsdp", scatter_dimension=0, tiled=True)
 
     fg = call(
         ffn_grad_kernel,
-        (shape(4, HALF, 128),) * 8,
+        shape(16, 1152, 128),
         "ffn_grad",
-        (zy, n2, dpre, u, c_all),
-        [pltpu.VMEM((16, 1152, 128), BF16)],
-        [SMEM] + [VMEM] * 4,
+        (n2, dpre, u, c_all),
         flops=5 * 10**9,
     )
-    fg = shift(fg[:4], 1) + shift(fg[4:], 0)
-
     dh, da_own, do_own, gain2_part = call(
         mid_back_kernel,
         (
@@ -770,46 +760,23 @@
             shape(1, 1536, dtype=F32),
         ),
         "mid_back",
-        (dn2, h, inv2, c_own, gains, wo_all, fg[1], fg[5], fg[2], fg[6]),
-        ins=[VMEM] * 6 + [ANY] * 4,
+        (dn2, h, inv2, c_own, gains, wo_all, fg),
+        ins=[VMEM] * 6 + [ANY],
     )
     do2 = swap(do_own, "fsdp").reshape(1024, 256)
-    near = [da_own] + [
-        lax.ppermute(da_own, "fsdp", [(f, (f + 2 * k) % 8) for f in range(8)]) for k in range(1, 4)
-    ]
-    da = near + [lax.ppermute(piece, "fsdp", [(f, f ^ 1) for f in range(8)]) for piece in near]
-    fg = call(
-        first_sum_kernel,
-        (shape(HALF, 128),) * 8,
-        "first_sum",
-        (zy, *fg),
-        [pltpu.VMEM((2, 4, HALF, 128), BF16)],
-        [SMEM] + [VMEM] * 8,
-    )
-    fg = shift(fg[:4], 0) + shift(fg[4:], 1)
+    da = gather(da_own, "fsdp")
     do2 = do2.astype(F32)
     datt2 = (do2 * sig2).astype(BF16)
     dlog2 = (do2 * attn2.astype(F32) * sig2 * (1.0 - sig2)).astype(BF16)
-    datt = swap(datt2.reshape(8, 128, 2, 128).transpose(0, 2, 1, 3).reshape(16, 128, 128), "ctx")
-    datt, *fg = tie(datt, *fg)
-    cols_g, down_g = call(second_sum_kernel, (shape(8, 96, 128), shape(384, 128)), "second_sum", fg)
-    ffo, da_own = tie(ffo, da_own)
-    ffo = lax.psum_scatter(ffo, "fsdp", scatter_dimension=0, tiled=True)
-    go = call(
-        out_grad_kernel,
-        shape(16, 48, 384),
-        "out_grad",
-        (fi[None], o2, *da),
-        [pltpu.VMEM((1024, 256), BF16), pltpu.VMEM((1024, 1536), BF16)],
-        [SMEM] + [VMEM] * 9,
-    )
-    cols_g = swap(cols_g, "fsdp").reshape(768, 128)
-    dheads = attend_back(block_map, j, recv, datt, attn, log_total, decay, go)
-    dheads, cols_g, ffo = tie(dheads, cols_g, ffo)
-    ffn = gather(jnp.concatenate([cols_g, down_g], 0), "ctx").reshape(16, 1152, 128)
+    datt_send = datt2.reshape(8, 128, 2, 128).transpose(0, 2, 1, 3).reshape(16, 128, 128)
+    datt = swap(datt_send, "ctx")
+    fg = after(fg, da_own)
+    fg_rows = lax.psum_scatter(
+        fg.reshape(16 * 1152, 128), "ctx", scatter_dimension=0, tiled=True
+    )
+    go = call(out_grad_kernel, shape(16, 48, 384), "out_grad", (o2, da))
+    dheads = attend_back(block_map, ids, recv, datt, attn, log_total, decay, go)
     dback = swap(dheads, "ctx")
-    mixed = jnp.where(live, h + ffo.astype(F32), 0.0).astype(BF16)
-
     g1, dproj = call(
         head_grad_kernel,
         (shape(16, 8, 80, 128), shape(1024, 576)),
@@ -821,41 +788,44 @@
 
     dn1 = call(
         input_grad_kernel,
-        shape(8, 144, 1536),
+        shape(8, 272, 1536),
         "input_grad",
-        (fi[None], dproj, dlog2, dback[:, 128, 0:256], fpre, w1, w2, gains, n1, gain2_part),
+        (ids, dproj, dlog2, dback[:, 128, 0:256], fpre, w1, gains, n1, gain2_part, ffo),
         ins=[SMEM] + [VMEM] * 9,
         flops=3 * 10**9,
     )
+    cols_g = call(
+        split_kernel, (shape(96, 128),) * 8, "split", (ids, fg_rows, dn1), ins=[SMEM, VMEM, ANY]
+    )
+    cols_g = [cols_g[0]] + [
+        lax.ppermute(cols_g[k], "fsdp", [(f, (f + k) % 8) for f in range(8)]) for k in range(1, 8)
+    ]
     dn1 = lax.psum_scatter(
-        dn1.reshape(1152, 1536), "fsdp", scatter_dimension=0, tiled=True
-    )
-    g1, ffn = tie(g1, ffn)
-    att = call(head_sum_kernel, shape(784, 128), "head_sum", (g1, dback[:, 144:192]))
-    att, dn1 = tie(att, dn1)
-    att = gather(att, "ctx").reshape(16, 784, 128)
+        dn1.reshape(8 * 272, 1536), "fsdp", scatter_dimension=0, tiled=True
+    )
+    total = call(
+        head_sum_kernel,
+        shape(1936, 128),
+        "head_sum",
+        (g1, dback[:, 144:192], fg_rows, *cols_g),
+        flops=3 * 10**9,
+    )
+    total, dn1 = tie(total, dn1)
+    total = gather(total, "ctx").reshape(16, 1936, 128)
 
     small = jnp.concatenate([dn1[128:131], dn1[136:141]], 0)
     small = swap(jnp.broadcast_to(small[None], (16, 8, 1536)), "ctx")
-    small = jnp.sum(small.astype(F32), 0)
+    small = call(
+        small_sum_kernel, shape(8, 1536, dtype=F32), "small_sum", (small,)
+    )
     forget_g = small[0:3].reshape(3, 8, 192).transpose(2, 1, 0).reshape(192, 24)
-
-    dn1 = dn1[0:128].astype(F32)
-    gain1 = gains[3:4]
-    x_own32 = x_own.astype(F32)
-    r1_own = lax.rsqrt(jnp.mean(x_own32 * x_own32, -1, keepdims=True) + EPS)
-    scaled1 = dn1 * gain1
-    tokens_grad = (
-        dh
-        + r1_own * scaled1
-        - x_own32 * (r1_own * r1_own * r1_own) * jnp.mean(scaled1 * x_own32, -1, keepdims=True)
-    ).astype(BF16)
-
-    gate_g, up_g, down_g = unpack_ffn(ffn)
-    mat = shape(192, 1536, dtype=F32)
-    query_g, key_g, value_g, outgate_g, output_g = call(
-        unpack_kernel, (mat,) * 5, "unpack_heads", (att,)
-    )
+    tokens_grad = call(finish_kernel, shape(128, 1536), "finish", (dn1, dh, x_own, gains))
+
+    live = (
+        lax.dynamic_slice_in_dim(block_map, 2 * ci, 2)[:, None] * 64 + offsets[None, :]
+    ).reshape(128) < lengths[0]
+    mixed = jnp.where(live[:, None], h + dn1[144:272].astype(F32), 0.0).astype(BF16)
+    query_g, key_g, value_g, outgate_g, output_g, gate_g, up_g, down_g = unpack(ids, total)
     return (
         mixed[None], tokens_grad[None], small[3, 0:192], query_g, key_g, value_g, forget_g,
         small[5:8, 0], outgate_g, output_g, small[4, 0:192], gate_g, up_g, down_g,

time: 576 us -> 555 us (0.964)
  waiting for transfers between devices: 252 us -> 232 us
  blocking collectives: 54.8 us -> 73.8 us
  starting transfers between devices: 81.3 us -> 64.7 us
  local copies, waits for them, and re-layouts: 28.2 us -> 21.8 us
  Pallas kernels: 131 us -> 137 us
    ppermute x26 -> x14, waiting for transfers between devices: 92.4 us -> 25.2 us  [the longest x3 13.9 us: per_device(): lax.ppermute(c_own, 'fsdp', [(f, (f + 2 * k) % 8) for f in range(8)])]
    reduce_scatter x2, waiting for transfers between devices: 2.58 us -> 27.8 us  [the longest x1 25.6 us: per_device(): lax.psum_scatter(dn1.reshape(8 * 272, 1536), 'fsdp', scatter_dimension=0,...]
    reduce_scatter x1, waiting for transfers between devices: 0.01 us -> 21.1 us  [per_device(): dn2 = lax.psum_scatter(dn2, 'fsdp', scatter_dimension=0, tiled=True)]
    all_to_all x2 -> x3, blocking collectives: 54.8 us -> 73.8 us  [swap(): return lax.all_to_all(array, axis, 0, 0, tiled=True)]
    all_to_all x8 -> x6, starting transfers between devices: 48.2 us -> 38.8 us  [swap(): return lax.all_to_all(array, axis, 0, 0, tiled=True)]
    unnamed x74 -> x61, local copies, waits for them, and re-layouts: 16.6 us -> 7.92 us
    ppermute x26 -> x14, starting transfers between devices: 32.3 us -> 25 us  [the longest x7 20.9 us: per_device(): lax.ppermute(cols_g[k], 'fsdp', [(f, (f + k) % 8) for f in range(8)])]
    all_to_all x8 -> x6, waiting for transfers between devices: 71 us -> 76.3 us  [swap(): return lax.all_to_all(array, axis, 0, 0, tiled=True)]
  transfers between devices with their start and end apart: 43 -> 29, of which waited for: 20 -> 20; matrix products, arithmetic and copies ran while one was open for 3% -> 3% of each run, Pallas kernels for 16% -> 17%
where the time goes in v2:
time: 555 us; the launch traced here: 549 us
  waiting for transfers between devices  232 us (42%)
  Pallas kernels  137 us (25%)
  blocking collectives  73.8 us (13%)
  starting transfers between devices  64.7 us (12%)
  local copies, waits for them, and re-layouts  21.8 us (4%)
  between operations  15.1 us (3%)
    pallas_call x15, Pallas kernels, call(): pl.pallas_call(kernel, grid=(1,), out_shape=outs, in_specs=ins or [VMEM]...  105 us
    all_gather x6, waiting for transfers between devices, gather(): return lax.all_gather(array, axis, axis=0, tiled=True)  79.9 us
    all_to_all x6, waiting for transfers between devices, swap(): return lax.all_to_all(array, axis, 0, 0, tiled=True)  76.3 us
    all_to_all x3, blocking collectives, swap(): return lax.all_to_all(array, axis, 0, 0, tiled=True)  73.8 us
    all_to_all x6, starting transfers between devices, swap(): return lax.all_to_all(array, axis, 0, 0, tiled=True)  38.8 us
    reduce_scatter x1, waiting for transfers between devices, per_device(): lax.psum_scatter(dn1.reshape(8 * 272, 1536), 'fsdp', scatter_dimension=0,...  25.6 us
    reduce_scatter x1, waiting for transfers between devices, per_device(): dn2 = lax.psum_scatter(dn2, 'fsdp', scatter_dimension=0, tiled=True)  21.1 us
    ppermute x7, starting transfers between devices, per_device(): lax.ppermute(cols_g[k], 'fsdp', [(f, (f + k) % 8) for f in range(8)])  20.9 us
  transfers between devices with their start and end apart: 29, of which 20 were waited for; matrix products, arithmetic and copies ran while one was open for 3% of the time, Pallas kernels for 17%

profile of v2, /device:TPU:1, one launch (start us, length us, event | category | flops | bytes accessed | tf_op | source)
XLA Modules:
  0.0 549.4 jit_solution(5393946284667697595)
XLA Ops:
  10.4 6.2 %pack.1 = (bf16[8,208,896]{2,1,0:T(8,128)(2,1)}, bf16[128,1536]{1,0:T(8,128)(2,1)}, bf16[128,1536]{1,0:T(8,128)(2,1)}) custom-call(s32[5]{0:T(128)} %stack.32.ids, s32[32]{0:T(128)} %bm_ref.5, s32[1]{0:T(128)} %copy.59.len_ref, bf16[128,1536]{1,0:T(8,128)(2,1)} %bitcast.65, bf16[128,1536]{1,0:T(8,128)(2,1)} %bitcast.68, bf16[192,1536]{1,0:T(8,128)(2,1)} %wq.1, ...), custom_call_target="tpu_custom_call" | custom-call | flops 1000000000 | bytes 10000000 | tf_op jit(solution)/shard_map/pack/pallas_call | solution.py:36
  16.7 5.8 %all-to-all-start = ((bf16[8,208,896]{2,1,0:T(8,128)(2,1)}), bf16[8,208,896]{2,1,0:T(8,128)(2,1)S(1)}, u32[]{:S(2)}, u32[]{:S(2)}) async-start(bf16[8,208,896]{2,1,0:T(8,128)(2,1)} %get-tuple-element.61), calls=%async_computation | async-start | bytes 5963776 | tf_op jit(solution)/shard_map/all_to_all | solution.py:671
  23.2 47.8 %all-to-all-done.w1r = bf16[8,208,896]{2,1,0:T(8,128)(2,1)S(1)} async-done(((bf16[8,208,896]{2,1,0:T(8,128)(2,1)}), bf16[8,208,896]{2,1,0:T(8,128)(2,1)S(1)}, u32[]{:S(2)}, u32[]{:S(2)}) %all-to-all-start) | async-done | bytes 2981920 | tf_op jit(solution)/shard_map/all_to_all | solution.py:671
  70.9 1.6 copy-done.4
  72.6 7.6 %project.1 = (bf16[1024,1536]{1,0:T(8,128)(2,1)}, bf16[16,144,384]{2,1,0:T(8,128)(2,1)}, f32[8,1024]{1,0:T(8,128)}, f32[8,1536]{1,0:T(8,128)}, bf16[1536,896]{1,...) custom-call(bf16[1024,1536]{1,0:T(8,128)(2,1)} %all-gather.7.cloned.1.call-done.x, ...), custom_call_target="tpu_custom_call" | custom-call | flops 2000000000 | bytes 10000000 | tf_op jit(solution)/shard_map/project/pallas_call | solution.py:132
  80.9 7.8 %all-to-all-start.1 = ((bf16[16,144,384]{2,1,0:T(8,128)(2,1)}), bf16[16,144,384]{2,1,0:T(8,128)(2,1)S(1)}, u32[]{:S(2)}, u32[]{:S(2)}) async-start(bf16[16,144,384]{2,1,0:T(8,128)(2,1)} %get-tuple-element.62), calls=%async_computation.1 | async-start | bytes 3538944 | tf_op jit(solution)/shard_map/all_to_all | solution.py:671
  89.1 1.9 collective-permute-start.1
  91.0 22.7 %all-to-all-done.1.r1 = bf16[16,144,384]{2,1,0:T(8,128)(2,1)S(1)} async-done(((bf16[16,144,384]{2,1,0:T(8,128)(2,1)}), bf16[16,144,384]{2,1,0:T(8,128)(2,1)S(1)}, u32[]{:S(2)}, u32[]{:S(2)}) %all-to-all-start.1) | async-done | bytes 1769504 | tf_op jit(solution)/shard_map/all_to_all | solution.py:671
  115.4 3.8 collective-permute-done.1._c.refs_2_
  119.2 11.2 %all-gather.9.cloned.1.call-done._a.wo = bf16[1536,1536]{1,0:T(8,128)(2,1)} async-done(((bf16[192,1536]{1,0:T(8,128)(2,1)}), bf16[1536,1536]{1,0:T(8,128)(2,1)}) %all-gather.9.cloned.1.call-update) | async-done | bytes 4718608 | tf_op jit(solution)/shard_map/all_gather | solution.py:675
  130.3 13.8 %attend.1 = (bf16[16,128,128]{2,1,0:T(8,128)(2,1)}, f32[2,2048,64]{2,1,0:T(8,128)}, f32[2,1,2048]{2,1,0:T(1,128)}) custom-call(s32[32]{0:T(128)} %bm_ref.5, s32[5]{0:T(128)} %stack.32.ids, bf16[16,144,384]{2,1,0:T(8,128)(2,1)} %copy-done.6, f32[2,1,2048]{2,1,0:T(1,128)} %reshape.116.fr, bf16[1536,1536]{1,0:T(8,128)(2,1)} %all-gather.9.cloned.1.call-done._a.wo, ...), custom_call_target="tpu_custom_call" | custom-call | flops 4000000000 | bytes 10000000 | tf_op jit(solution)/shard_map/attend/pallas_call | solution.py:36
  144.1 6.7 %all-to-all-start.2 = ((bf16[16,128,128]{2,1,0:T(8,128)(2,1)}), bf16[16,128,128]{2,1,0:T(8,128)(2,1)S(1)}, u32[]{:S(2)}, u32[]{:S(2)}) async-start(bf16[16,128,128]{2,1,0:T(8,128)(2,1)} %get-tuple-element.65), calls=%async_computation.2 | async-start | bytes 1048576 | tf_op jit(solution)/shard_map/all_to_all | solution.py:671
  150.9 10.1 %collective-permute-done.2._a.refs_3_ = bf16[128,1536]{1,0:T(8,128)(2,1)S(1)} collective-permute-done((bf16[128,1536]{1,0:T(8,128)(2,1)S(1)}, bf16[128,1536]{1,0:T(8,128)(2,1)S(1)}, u32[]{:S(2)}, u32[]{:S(2)}) %collective-permute-start.2) | collective-permute-done | bytes 393248 | tf_op jit(solution)/shard_map/ppermute | solution.py:704
  161.8 4.7 open.1
  168.4 13.8 %all_to_all.45.o_r = bf16[8,128,256]{2,1,0:T(8,128)(2,1)} all-to-all(bf16[8,128,256]{2,1,0:T(8,128)(2,1)S(1)} %bitcast.60), channel_id=1, replica_groups=mesh['ctx'=16,'fsdp'=8] {'fsdp'}, dimensions={0} | all-to-all | bytes 1048576 | tf_op jit(solution)/shard_map/all_to_all | solution.py:671
  182.2 5.5 mid.1
  192.7 6.3 %ready.1 = (bf16[1536,1024]{1,0:T(8,128)(2,1)}, bf16[1024,1536]{1,0:T(8,128)(2,1)}) custom-call(s32[5]{0:T(128)} %stack.32.ids, bf16[16,768,128]{2,1,0:T(8,128)(2,1)} %bitcast.61, bf16[128,1536]{1,0:T(8,128)(2,1)} %get-tuple-element.64.refs_0_.c_ref, bf16[128,1536]{1,0:T(8,128)(2,1)} %copy-done.12, bf16[128,1536]{1,0:T(8,128)(2,1)} %copy-done.14, ...), custom_call_target="tpu_custom_call" | custom-call | flops 1000000000 | bytes 10000000 | tf_op jit(solution)/shard_map/ready/pallas_call | solution.py:36
  198.9 16.9 %all-gather.11.cloned.1.call-done.n2 = bf16[1024,1536]{1,0:T(8,128)(2,1)} async-done(((bf16[128,1536]{1,0:T(8,128)(2,1)}), bf16[1024,1536]{1,0:T(8,128)(2,1)}) %all-gather.11.cloned.1.call-update) | async-done | bytes 3145744 | tf_op jit(solution)/shard_map/all_gather | solution.py:675
  215.8 15.0 %feed_forward.1 = (bf16[1024,1536]{1,0:T(8,128)(2,1)}, bf16[1024,1536]{1,0:T(8,128)(2,1)}, bf16[1024,512]{1,0:T(8,128)(2,1)}, bf16[1024,1024]{1,0:T(8,128)(2,1)}) custom-call(bf16[1024,1536]{1,0:T(8,128)(2,1)} %all-gather.11.cloned.1.call-done.n2, bf16[1024,1536]{1,0:T(8,128)(2,1)} %get-tuple-element.72.c, bf16[1536,1024]{1,0:T(8,128)(2,1)} %get-tuple-element.73.w2, ...), custom_call_target="tpu_custom_call" | custom-call | flops 10000000000 | bytes 20000000 | tf_op jit(solution)/shard_map/feed_forward/pallas_call | solution.py:426
  231.3 11.0 %ffn_grad.1._after.refs_0_ = bf16[16,1152,128]{2,1,0:T(8,128)(2,1)} custom-call(bf16[1024,1536]{1,0:T(8,128)(2,1)} %all-gather.11.cloned.1.call-done.n2, bf16[1024,1024]{1,0:T(8,128)(2,1)} %get-tuple-element.76.dpre, bf16[1024,512]{1,0:T(8,128)(2,1)} %get-tuple-element.77.u, bf16[1024,1536]{1,0:T(8,128)(2,1)} %get-tuple-element.72.c), custom_call_target="tpu_custom_call" | custom-call | flops 5000000000 | bytes 10000000 | tf_op jit(solution)/shard_map/ffn_grad/pallas_call | solution.py:36
  242.2 21.1 %reduce-scatter.4.cloned.1.call-done.dn2_r = bf16[128,1536]{1,0:T(8,128)(2,1)} async-done(((bf16[1024,1536]{1,0:T(8,128)(2,1)}), bf16[128,1536]{1,0:T(8,128)(2,1)}) %reduce-scatter.4.cloned.1.call-update) | async-done | bytes 393232 | tf_op jit(solution)/shard_map/reduce_scatter | solution.py:745
  263.3 5.8 %mid_back.1 = (f32[128,1536]{1,0:T(8,128)}, bf16[128,1536]{1,0:T(8,128)(2,1)}, bf16[8,128,256]{2,1,0:T(8,128)(2,1)}, f32[1,1536]{1,0:T(1,128)}) custom-call(bf16[128,1536]{1,0:T(8,128)(2,1)} %reduce-scatter.4.cloned.1.call-done.dn2_r, f32[128,1536]{1,0:T(8,128)} %get-tuple-element.69.h_ref, f32[128,128]{1,0:T(8,128)} %get-tuple-element.75.r2_ref, ...), custom_call_target="tpu_custom_call" | custom-call | flops 1000000000 | bytes 10000000 | tf_op jit(solution)/shard_map/mid_back/pallas_call | solution.py:36
  270.3 16.2 %all_to_all.46 = bf16[8,128,256]{2,1,0:T(8,128)(2,1)S(1)} all-to-all(bf16[8,128,256]{2,1,0:T(8,128)(2,1)S(1)} %copy-done.10), channel_id=1, replica_groups=mesh['ctx'=16,'fsdp'=8] {'fsdp'}, dimensions={0} | all-to-all | bytes 1048576 | tf_op jit(solution)/shard_map/all_to_all | solution.py:671
  288.6 6.7 %all-to-all-start.5 = ((bf16[16,128,128]{2,1,0:T(8,128)(2,1)}), bf16[16,128,128]{2,1,0:T(8,128)(2,1)S(1)}, u32[]{:S(2)}, u32[]{:S(2)}) async-start(bf16[16,128,128]{2,1,0:T(8,128)(2,1)} %bitcast.19), calls=%async_computation.6 | async-start | bytes 1048576 | tf_op jit(solution)/shard_map/all_to_all | solution.py:671
  295.5 4.9 all-gather.15.cloned.1.call-done.da
  300.5 3.9 out_grad.1.go
  305.8 18.5 %attend_back.1 = bf16[16,192,384]{2,1,0:T(8,128)(2,1)} custom-call(s32[32]{0:T(128)} %bm_ref.5, s32[5]{0:T(128)} %stack.32.ids, bf16[16,144,384]{2,1,0:T(8,128)(2,1)} %copy-done.6, bf16[16,128,128]{2,1,0:T(8,128)(2,1)} %copy-done.11, f32[2,2048,64]{2,1,0:T(8,128)} %get-tuple-element.79.attn_ref, f32[2,1,2048]{2,1,0:T(1,128)} %get-tuple-element.80.l_ref, ...), custom_call_target="tpu_custom_call" | custom-call | flops 10000000000 | bytes 10000000 | tf_op jit(solution)/shard_map/attend_back/pallas_call | solution.py:36
  324.3 43.7 %all_to_all.47.dback = bf16[16,192,384]{2,1,0:T(8,128)(2,1)S(1)} all-to-all(bf16[16,192,384]{2,1,0:T(8,128)(2,1)} %attend_back.1), channel_id=1, replica_groups=mesh['ctx'=16,'fsdp'=8] {'ctx'}, dimensions={0} | all-to-all | bytes 4718592 | tf_op jit(solution)/shard_map/all_to_all | solution.py:671
  369.4 8.3 %head_grad.1 = (bf16[16,8,80,128]{3,2,1,0:T(8,128)(2,1)}, bf16[1024,576]{1,0:T(8,128)(2,1)}) custom-call(bf16[1024,1536]{1,0:T(8,128)(2,1)} %get-tuple-element.66.n1, bf16[16,192,384]{2,1,0:T(8,128)(2,1)} %copy-done.2, bf16[1024,256]{1,0:T(8,128)(2,1)} %get-tuple-element.106.dlog2), custom_call_target="tpu_custom_call" | custom-call | flops 3000000000 | bytes 10000000 | tf_op jit(solution)/shard_map/head_grad/pallas_call | solution.py:36
  377.8 11.9 %input_grad.1._after = bf16[8,272,1536]{2,1,0:T(8,128)(2,1)} custom-call(s32[5]{0:T(128)} %stack.32.ids, bf16[1024,576]{1,0:T(8,128)(2,1)} %get-tuple-element.83.dproj, bf16[1024,256]{1,0:T(8,128)(2,1)} %get-tuple-element.106.dlog2, bf16[16,256]{1,0:T(8,128)(2,1)} %bitcast.71, f32[8,1024]{1,0:T(8,128)} %get-tuple-element.84.fpre, ...), custom_call_target="tpu_custom_call" | custom-call | flops 3000000000 | bytes 10000000 | tf_op jit(solution)/shard_map/input_grad/pallas_call | solution.py:36
  389.7 5.1 all-to-all-start.7
  394.9 2.2 reduce-scatter.6.cloned.1.call-done.r.mine
  397.1 1.7 split.1
  398.7 13.8 %collective-permute-start.7 = (bf16[96,128]{1,0:T(8,128)(2,1)}, bf16[96,128]{1,0:T(8,128)(2,1)S(1)}, u32[]{:S(2)}, u32[]{:S(2)}) collective-permute-start(bf16[96,128]{1,0:T(8,128)(2,1)} %get-tuple-element.88), channel_id=1, source_target_pairs={{0,1},{1,2},{2,3},{3,4},{4,5},{5,6},{6,7},{7,0},{8,9},{9,10},{10,1... | collective-permute-start | bytes 73736 | tf_op jit(solution)/shard_map/ppermute | solution.py:801
  413.8 2.0 collective-permute-start.10
  416.1 6.0 %collective-permute-done.7.refs_1_ = bf16[96,128]{1,0:T(8,128)(2,1)S(1)} collective-permute-done((bf16[96,128]{1,0:T(8,128)(2,1)}, bf16[96,128]{1,0:T(8,128)(2,1)S(1)}, u32[]{:S(2)}, u32[]{:S(2)}) %collective-permute-start.7) | collective-permute-done | bytes 24608 | tf_op jit(solution)/shard_map/ppermute | solution.py:801
  422.1 2.6 collective-permute-start.12
  424.7 1.7 collective-permute-done.8.refs_2_
  427.4 1.9 slice.46.go
  432.5 3.3 head_sum.1
  435.8 25.6 %reduce-scatter.8.cloned.1.call-done.dn1 = bf16[272,1536]{1,0:T(8,128)(2,1)} async-done(((bf16[2176,1536]{1,0:T(8,128)(2,1)}), bf16[272,1536]{1,0:T(8,128)(2,1)}) %reduce-scatter.8.cloned.1.call-update) | async-done | bytes 835600 | tf_op jit(solution)/shard_map/reduce_scatter | solution.py:803
  464.0 6.7 %all-to-all-start.8 = ((bf16[16,8,1536]{2,1,0:T(8,128)(2,1)}), bf16[16,8,1536]{2,1,0:T(8,128)(2,1)S(1)}, u32[]{:S(2)}, u32[]{:S(2)}) async-start(bf16[16,8,1536]{2,1,0:T(8,128)(2,1)} %broadcast_in_dim.46), calls=%async_computation.11 | async-start | bytes 786432 | tf_op jit(solution)/shard_map/all_to_all | solution.py:671
  470.7 2.6 finish.1
  473.3 1.9 fusion.5
  475.2 4.7 all-to-all-done.8.r
  480.6 1.7 small_sum.1
  486.5 46.9 %all-gather.17.cloned.1.call-done = bf16[30976,128]{1,0:T(8,128)(2,1)} async-done(((bf16[1936,128]{1,0:T(8,128)(2,1)}), bf16[30976,128]{1,0:T(8,128)(2,1)}) %all-gather.17.cloned.1.call-update) | async-done | bytes 7929872 | tf_op jit(solution)/shard_map/all_gather | solution.py:675
  533.4 9.2 %unpack.1 = (f32[192,1536]{1,0:T(8,128)}, f32[192,1536]{1,0:T(8,128)}, f32[192,1536]{1,0:T(8,128)}, f32[192,1536]{1,0:T(8,128)}, f32[192,1536]{1,0:T(8,128)}, /*...) custom-call(s32[5]{0:T(128)} %stack.32.ids, bf16[16,1936,128]{2,1,0:T(8,128)(2,1)} %bitcast.75), custom_call_target="tpu_custom_call" | custom-call | flops 60000002048 | bytes 30000000 | tf_op jit(solution)/shard_map/unpack/pallas_call | solution.py:645
  (141 shorter events, 33.5 us)
Async XLA Ops:
  7.2 63.8 %all-gather.7.cloned.1.call-start = ((), (), s32[]{:S(2)}) async-start(), calls=%async_computation.12 | async-start | bytes 3538944 | tf_op jit(solution)/shard_map/all_gather | solution.py:675
  16.7 5.8 %copy-start.29 = (bf16[3]{0:T(256)(128)(2,1)S(1)}, bf16[3]{0:T(256)(128)(2,1)}, u32[]{:S(2)}) copy-start(bf16[3]{0:T(256)(128)(2,1)} %param.25) | copy-start | bytes 22
  16.7 54.3 %all-to-all-start = ((bf16[8,208,896]{2,1,0:T(8,128)(2,1)}), bf16[8,208,896]{2,1,0:T(8,128)(2,1)S(1)}, u32[]{:S(2)}, u32[]{:S(2)}) async-start(bf16[8,208,896]{2,1,0:T(8,128)(2,1)} %get-tuple-element.61), calls=%async_computation | async-start | bytes 5963776 | tf_op jit(solution)/shard_map/all_to_all | solution.py:671
  22.5 107.8 %all-gather.9.cloned.1.call-start = ((), (), s32[]{:S(2)}) async-start(), calls=%async_computation.13 | async-start | bytes 5308416 | tf_op jit(solution)/shard_map/all_gather | solution.py:675
  80.1 8.6 %copy-start.7 = (bf16[128,1536]{1,0:T(8,128)(2,1)S(1)}, bf16[128,1536]{1,0:T(8,128)(2,1)}, u32[]{:S(2)}) copy-start(bf16[128,1536]{1,0:T(8,128)(2,1)} %get-tuple-element.64.refs_0_.c_ref) | copy-start | bytes 1179652
  80.1 33.9 %copy-start.20 = (s32[32]{0:T(128)S(1)}, s32[32]{0:T(128)}, u32[]{:S(2)}) copy-start(s32[32]{0:T(128)} %bm_ref.5) | copy-start | bytes 388
  80.2 112.5 %all-gather.13.cloned.1.call-start = ((), (), s32[]{:S(2)}) async-start(), calls=%async_computation.15 | async-start | bytes 3342336 | tf_op jit(solution)/shard_map/all_gather | solution.py:675
  80.9 32.8 %all-to-all-start.1 = ((bf16[16,144,384]{2,1,0:T(8,128)(2,1)}), bf16[16,144,384]{2,1,0:T(8,128)(2,1)S(1)}, u32[]{:S(2)}, u32[]{:S(2)}) async-start(bf16[16,144,384]{2,1,0:T(8,128)(2,1)} %get-tuple-element.62), calls=%async_computation.1 | async-start | bytes 3538944 | tf_op jit(solution)/shard_map/all_to_all | solution.py:671
  88.7 26.7 %collective-permute-start = (bf16[128,1536]{1,0:T(8,128)(2,1)S(1)}, bf16[128,1536]{1,0:T(8,128)(2,1)S(1)}, u32[]{:S(2)}, u32[]{:S(2)}) collective-permute-start(bf16[128,1536]{1,0:T(8,128)(2,1)S(1)} %copy-done.7), channel_id=1, source_target_pairs={{0,2},{1,3},{2,4},{3,5},{4,6},{5,7},{6,0},{7,1},{8,10},{9,11},{10,... | collective-permute-start | bytes 1179656 | tf_op jit(solution)/shard_map/ppermute | solution.py:704
  89.1 30.1 %collective-permute-start.1 = (bf16[128,1536]{1,0:T(8,128)(2,1)S(1)}, bf16[128,1536]{1,0:T(8,128)(2,1)S(1)}, u32[]{:S(2)}, u32[]{:S(2)}) collective-permute-start(bf16[128,1536]{1,0:T(8,128)(2,1)S(1)} %copy-done.7), channel_id=1, source_target_pairs={{0,4},{1,5},{2,6},{3,7},{4,0},{5,1},{6,2},{7,3},{8,12},{9,13},{10,... | collective-permute-start | bytes 1179656 | tf_op jit(solution)/shard_map/ppermute | solution.py:704
  113.7 16.6 %copy-start.6 = (bf16[16,144,384]{2,1,0:T(8,128)(2,1)}, bf16[16,144,384]{2,1,0:T(8,128)(2,1)S(1)}, u32[]{:S(2)}) copy-start(bf16[16,144,384]{2,1,0:T(8,128)(2,1)S(1)} %all-to-all-done.1.r1) | copy-start | bytes 5308420
  115.4 15.0 %copy-start.12 = (bf16[128,1536]{1,0:T(8,128)(2,1)}, bf16[128,1536]{1,0:T(8,128)(2,1)S(1)}, u32[]{:S(2)}) copy-start(bf16[128,1536]{1,0:T(8,128)(2,1)S(1)} %collective-permute-done._b.refs_1_) | copy-start | bytes 1179652
  119.2 11.2 %copy-start.14 = (bf16[128,1536]{1,0:T(8,128)(2,1)}, bf16[128,1536]{1,0:T(8,128)(2,1)S(1)}, u32[]{:S(2)}) copy-start(bf16[128,1536]{1,0:T(8,128)(2,1)S(1)} %collective-permute-done.1._c.refs_2_) | copy-start | bytes 1179652
  144.1 22.3 %all-to-all-start.2 = ((bf16[16,128,128]{2,1,0:T(8,128)(2,1)}), bf16[16,128,128]{2,1,0:T(8,128)(2,1)S(1)}, u32[]{:S(2)}, u32[]{:S(2)}) async-start(bf16[16,128,128]{2,1,0:T(8,128)(2,1)} %get-tuple-element.65), calls=%async_computation.2 | async-start | bytes 1048576 | tf_op jit(solution)/shard_map/all_to_all | solution.py:671
  150.8 65.0 %all-gather.11.cloned.1.call-start = ((), (), s32[]{:S(2)}) async-start(), calls=%async_computation.14 | async-start | bytes 3538944 | tf_op jit(solution)/shard_map/all_gather | solution.py:675
  150.8 10.2 %collective-permute-start.2 = (bf16[128,1536]{1,0:T(8,128)(2,1)S(1)}, bf16[128,1536]{1,0:T(8,128)(2,1)S(1)}, u32[]{:S(2)}, u32[]{:S(2)}) collective-permute-start(bf16[128,1536]{1,0:T(8,128)(2,1)S(1)} %copy-done.7), channel_id=1, source_target_pairs={{0,6},{1,7},{2,0},{3,1},{4,2},{5,3},{6,4},{7,5},{8,14},{9,15},{10,... | collective-permute-start | bytes 1179656 | tf_op jit(solution)/shard_map/ppermute | solution.py:704
  168.4 19.3 %copy-start.1 = (bf16[1024,256]{1,0:T(8,128)(2,1)}, bf16[1024,256]{1,0:T(8,128)(2,1)S(1)}, u32[]{:S(2)}) copy-start(bf16[1024,256]{1,0:T(8,128)(2,1)S(1)} %fusion.4.o) | copy-start | bytes 1572868
  182.2 6.7 %copy-start.13 = (bf16[128,1536]{1,0:T(8,128)(2,1)S(1)}, bf16[128,1536]{1,0:T(8,128)(2,1)}, u32[]{:S(2)}) copy-start(bf16[128,1536]{1,0:T(8,128)(2,1)} %copy-done.12) | copy-start | bytes 1179652
  182.2 6.8 %copy-start.15 = (bf16[128,1536]{1,0:T(8,128)(2,1)S(1)}, bf16[128,1536]{1,0:T(8,128)(2,1)}, u32[]{:S(2)}) copy-start(bf16[128,1536]{1,0:T(8,128)(2,1)} %copy-done.14) | copy-start | bytes 1179652
  182.2 7.2 %copy-start.9 = (bf16[128,1536]{1,0:T(8,128)(2,1)S(1)}, bf16[128,1536]{1,0:T(8,128)(2,1)}, u32[]{:S(2)}) copy-start(bf16[128,1536]{1,0:T(8,128)(2,1)} %copy-done.8) | copy-start | bytes 1179652
  187.7 75.6 %reduce-scatter.4.cloned.1.call-start = ((), (), s32[]{:S(2)}) async-start(), calls=%async_computation.16 | async-start | bytes 3538944 | tf_op jit(solution)/shard_map/reduce_scatter | solution.py:745
  187.8 2.5 collective-permute-start.3
  188.9 1.9 collective-permute-start.4
  189.0 2.9 collective-permute-start.5
  189.4 3.3 collective-permute-start.6
  190.2 2.4 copy-start.16
  190.8 1.9 copy-start.17
  230.8 69.6 %all-gather.15.cloned.1.call-start = ((), (), s32[]{:S(2)}) async-start(), calls=%async_computation.17 | async-start | bytes 3538944 | tf_op jit(solution)/shard_map/all_gather | solution.py:675
  269.2 127.9 %reduce-scatter.6.cloned.1.call-start = ((), (), s32[]{:S(2)}) async-start(), calls=%async_computation.18 | async-start | bytes 5013504 | tf_op jit(solution)/shard_map/reduce_scatter | solution.py:774
  269.3 17.3 %copy-start = (f32[1024,256]{1,0:T(8,128)S(1)}, f32[1024,256]{1,0:T(8,128)}, u32[]{:S(2)}) copy-start(f32[1024,256]{1,0:T(8,128)} %open.1) | copy-start | bytes 3145732
  288.6 16.4 %all-to-all-start.5 = ((bf16[16,128,128]{2,1,0:T(8,128)(2,1)}), bf16[16,128,128]{2,1,0:T(8,128)(2,1)S(1)}, u32[]{:S(2)}, u32[]{:S(2)}) async-start(bf16[16,128,128]{2,1,0:T(8,128)(2,1)} %bitcast.19), calls=%async_computation.6 | async-start | bytes 1048576 | tf_op jit(solution)/shard_map/all_to_all | solution.py:671
  295.3 166.1 %reduce-scatter.8.cloned.1.call-start = ((), (), s32[]{:S(2)}) async-start(), calls=%async_computation.19 | async-start | bytes 7520256 | tf_op jit(solution)/shard_map/reduce_scatter | solution.py:803
  389.7 41.3 %all-to-all-start.7 = ((bf16[128,80,128]{2,1,0:T(8,128)(2,1)}), bf16[128,80,128]{2,1,0:T(8,128)(2,1)S(1)}, u32[]{:S(2)}, u32[]{:S(2)}) async-start(bf16[128,80,128]{2,1,0:T(8,128)(2,1)} %bitcast.21), calls=%async_computation.8 | async-start | bytes 5242880 | tf_op jit(solution)/shard_map/all_to_all | solution.py:671
  394.8 138.6 %all-gather.17.cloned.1.call-start = ((), (), s32[]{:S(2)}) async-start(), calls=%async_computation.20 | async-start | bytes 8425472 | tf_op jit(solution)/shard_map/all_gather | solution.py:675
  398.7 23.4 %collective-permute-start.7 = (bf16[96,128]{1,0:T(8,128)(2,1)}, bf16[96,128]{1,0:T(8,128)(2,1)S(1)}, u32[]{:S(2)}, u32[]{:S(2)}) collective-permute-start(bf16[96,128]{1,0:T(8,128)(2,1)} %get-tuple-element.88), channel_id=1, source_target_pairs={{0,1},{1,2},{2,3},{3,4},{4,5},{5,6},{6,7},{7,0},{8,9},{9,10},{10,1... | collective-permute-start | bytes 73736 | tf_op jit(solution)/shard_map/ppermute | solution.py:801
  412.5 13.9 %collective-permute-start.8 = (bf16[96,128]{1,0:T(8,128)(2,1)}, bf16[96,128]{1,0:T(8,128)(2,1)S(1)}, u32[]{:S(2)}, u32[]{:S(2)}) collective-permute-start(bf16[96,128]{1,0:T(8,128)(2,1)} %get-tuple-element.89), channel_id=1, source_target_pairs={{0,2},{1,3},{2,4},{3,5},{4,6},{5,7},{6,0},{7,1},{8,10},{9,11},{10,... | collective-permute-start | bytes 73736 | tf_op jit(solution)/shard_map/ppermute | solution.py:801
  412.5 16.8 %collective-permute-start.9 = (bf16[96,128]{1,0:T(8,128)(2,1)}, bf16[96,128]{1,0:T(8,128)(2,1)S(1)}, u32[]{:S(2)}, u32[]{:S(2)}) collective-permute-start(bf16[96,128]{1,0:T(8,128)(2,1)} %get-tuple-element.90), channel_id=1, source_target_pairs={{0,3},{1,4},{2,5},{3,6},{4,7},{5,0},{6,1},{7,2},{8,11},{9,12},{10,... | collective-permute-start | bytes 73736 | tf_op jit(solution)/shard_map/ppermute | solution.py:801
  413.8 15.5 %collective-permute-start.10 = (bf16[96,128]{1,0:T(8,128)(2,1)}, bf16[96,128]{1,0:T(8,128)(2,1)S(1)}, u32[]{:S(2)}, u32[]{:S(2)}) collective-permute-start(bf16[96,128]{1,0:T(8,128)(2,1)} %get-tuple-element.91), channel_id=1, source_target_pairs={{0,4},{1,5},{2,6},{3,7},{4,0},{5,1},{6,2},{7,3},{8,12},{9,13},{10,... | collective-permute-start | bytes 73736 | tf_op jit(solution)/shard_map/ppermute | solution.py:801
  415.8 13.5 %collective-permute-start.11 = (bf16[96,128]{1,0:T(8,128)(2,1)}, bf16[96,128]{1,0:T(8,128)(2,1)S(1)}, u32[]{:S(2)}, u32[]{:S(2)}) collective-permute-start(bf16[96,128]{1,0:T(8,128)(2,1)} %get-tuple-element.92), channel_id=1, source_target_pairs={{0,5},{1,6},{2,7},{3,0},{4,1},{5,2},{6,3},{7,4},{8,13},{9,14},{10,... | collective-permute-start | bytes 73736 | tf_op jit(solution)/shard_map/ppermute | solution.py:801
  422.1 8.9 %copy-start.22 = (bf16[96,128]{1,0:T(8,128)(2,1)}, bf16[96,128]{1,0:T(8,128)(2,1)S(1)}, u32[]{:S(2)}) copy-start(bf16[96,128]{1,0:T(8,128)(2,1)S(1)} %collective-permute-done.7.refs_1_) | copy-start | bytes 73732
  422.1 7.2 %collective-permute-start.12 = (bf16[96,128]{1,0:T(8,128)(2,1)}, bf16[96,128]{1,0:T(8,128)(2,1)S(1)}, u32[]{:S(2)}, u32[]{:S(2)}) collective-permute-start(bf16[96,128]{1,0:T(8,128)(2,1)} %get-tuple-element.93), channel_id=1, source_target_pairs={{0,6},{1,7},{2,0},{3,1},{4,2},{5,3},{6,4},{7,5},{8,14},{9,15},{10,... | collective-permute-start | bytes 73736 | tf_op jit(solution)/shard_map/ppermute | solution.py:801
  426.5 4.6 copy-start.23
  426.5 4.1 collective-permute-start.13
  429.3 1.7 copy-start.24
  429.3 1.7 copy-start.25
  432.5 28.9 %copy-start.21 = (s32[32]{0:T(128)S(1)}, s32[32]{0:T(128)}, u32[]{:S(2)}) copy-start(s32[32]{0:T(128)} %bm_ref.5) | copy-start | bytes 388
  435.8 37.5 %copy-start.3 = (f32[128,1536]{1,0:T(8,128)S(1)}, f32[128,1536]{1,0:T(8,128)}, u32[]{:S(2)}) copy-start(f32[128,1536]{1,0:T(8,128)} %get-tuple-element.69.h_ref) | copy-start | bytes 2359300
  464.0 15.9 %all-to-all-start.8 = ((bf16[16,8,1536]{2,1,0:T(8,128)(2,1)}), bf16[16,8,1536]{2,1,0:T(8,128)(2,1)S(1)}, u32[]{:S(2)}, u32[]{:S(2)}) async-start(bf16[16,8,1536]{2,1,0:T(8,128)(2,1)} %broadcast_in_dim.46), calls=%async_computation.11 | async-start | bytes 786432 | tf_op jit(solution)/shard_map/all_to_all | solution.py:671
  (11 other events, 12.5 us)
Sparse Core Ops, SparseCore 0:
  16.8 47.2 all-gather.6
  80.3 49.9 all-gather.8
  132.5 49.8 all-gather.12
  187.8 27.9 all-gather.10
  231.0 32.3 reduce-scatter.3
  269.3 31.0 all-gather.14
  303.8 93.2 reduce-scatter.5
  399.5 61.8 reduce-scatter.7
  464.4 68.9 all-gather.16

commit v3 on v2

--- a/solution.py
+++ b/solution.py
@@ -210,7 +210,7 @@
     fc_s[1] = both[:, 1:2]
 
 
-def fwd_kernel(bm_ref, ids, r1, fr, _a, _b, _c, o_ref, attn_ref, l_ref, q_s, k_s, v_s, vt_s, fc_s, o_s):
+def fwd_kernel(bm_ref, ids, r1, fr, _a, o_ref, attn_ref, l_ref, q_s, k_s, v_s, vt_s, fc_s, o_s):
     j = ids[3]
     load_heads(bm_ref, r1, q_s, k_s, v_s)
     column_decay(fr, fc_s)
@@ -328,7 +328,7 @@
             pltpu.VMEM((2, SPAN, 1), F32),
             pltpu.VMEM((2, SPAN, HD), BF16),
         ],
-        [SMEM, SMEM, VMEM, VMEM, ANY, ANY, ANY],
+        [SMEM, SMEM, VMEM, VMEM, ANY],
         flops=4 * 10**9,
     )
 
@@ -373,7 +373,7 @@
 ):
     h = h_ref[...]
     r2 = r2_ref[:, 0:1]
-    dn2 = dn2_r[...].astype(F32)
+    dn2 = dn2_r[:, 0:1536].astype(F32)
     g2_ref[...] = jnp.sum(dn2 * h * r2, 0, keepdims=True)
     scaled = dn2 * gains[4:5]
     dh = (
@@ -405,7 +405,7 @@
                 w2[row : row + 48, col : col + 128] = w2g[p, at : at + 48, :]
 
 
-def ffn_kernel(n2, c, w2, wd, dn2_ref, ffo_ref, u_ref, dpre_ref):
+def ffn_kernel(n2, c, w2, wd, both, u_ref, dpre_ref):
     pre = dot(n2[...], w2[...])
     gate, up = pre[:, 0:512], pre[:, 512:1024]
     sig = jax.nn.sigmoid(gate)
@@ -417,8 +417,8 @@
     dup = (du * act).astype(BF16)
     dpre = jnp.concatenate([dgate, dup], 1)
     dpre_ref[...] = dpre
-    dn2_ref[...] = dot(dpre, w2[...], NT).astype(BF16)
-    ffo_ref[...] = dot(u, wd[...]).astype(BF16)
+    both[:, 0:1536] = dot(dpre, w2[...], NT).astype(BF16)
+    both[:, 1536:3072] = dot(u, wd[...]).astype(BF16)
 
 
 def feed_forward(n2, c_all, w2, wd):
@@ -427,8 +427,7 @@
         ffn_kernel,
         grid=(1024 // rows,),
         out_shape=(
-            shape(1024, 1536),
-            shape(1024, 1536),
+            shape(1024, 3072),
             shape(1024, 512),
             shape(1024, 1024),
         ),
@@ -439,8 +438,7 @@
             pl.BlockSpec((512, 1536), lambda i: (0, 0)),
         ],
         out_specs=(
-            pl.BlockSpec((rows, 1536), lambda i: (i, 0)),
-            pl.BlockSpec((rows, 1536), lambda i: (i, 0)),
+            pl.BlockSpec((rows, 3072), lambda i: (i, 0)),
             pl.BlockSpec((rows, 512), lambda i: (i, 0)),
             pl.BlockSpec((rows, 1024), lambda i: (i, 0)),
         ),
@@ -475,21 +473,29 @@
                 ]
 
 
-def split_kernel(ids, r, _after, *outs):
+def split_kernel(ids, r, *outs):
     for k in range(8):
         at = pl.multiple_of(lax.rem(ids[2] + k, 8) * 96, 16)
         outs[k][...] = r[pl.ds(at, 96), :]
 
 
-def out_grad_kernel(o, da, out):
-    t = dot(o[...], da[...], TN)
+def out_grad_kernel(ids, o, *refs):
+    pieces, out, o_s, da_s = refs[:8], refs[8], refs[9], refs[10]
+    for k in range(8):
+        first = ids[2] if k < 4 else ids[2] + 1 - 2 * lax.rem(ids[2], 2)
+        slot = lax.rem(first + 8 - 2 * (k % 4), 8)
+        at = pl.multiple_of(slot * 128, 128)
+        o_s[k * 128 : (k + 1) * 128, :] = o[pl.ds(at, 128), :]
+        da_s[k * 128 : (k + 1) * 128, :] = pieces[k][...]
+    t = dot(o_s[...], da_s[...], TN)
     t = jnp.concatenate([t[0:64], t[64:128] + t[128:192], t[192:256]], 0).astype(BF16)
     for c in range(16):
         cr, cc = divmod(c, 4)
         out[c] = t[cr * 48 : (cr + 1) * 48, cc * 384 : (cc + 1) * 384]
 
 
-def head_grad_kernel(n1, dback, dlog2, out, dproj):
+def head_grad_kernel(n1, dback, dlog2, *refs):
+    out, dproj = refs[-2:]
     for s in range(8):
         d0, d1 = dback[2 * s], dback[2 * s + 1]
         dproj[s * 128 : (s + 1) * 128, :] = jnp.concatenate(
@@ -516,7 +522,7 @@
 
 
 def input_grad_kernel(
-    ids, dproj, dlog2, dl, fpre, w1, gains, n1, gain2, ffo, out
+    ids, dproj, dlog2, dl, fpre, w1, gains, n1, gain2, out
 ):
     fi = ids[2]
     rows = [[], [], []]
@@ -562,7 +568,6 @@
             0,
         )
         out[d, 128:144, :] = jnp.concatenate([top, low], 0).astype(BF16)
-        out[d, 144:272, :] = ffo[d * 128 : (d + 1) * 128, :]
 
 
 def head_sum_kernel(r, go, mine, *refs):
@@ -710,7 +715,7 @@
     wo_all = gather(wo_own, "fsdp")
     w2g = gather(w2p, "ctx").reshape(16, 768, 128)
     recv = swap(send, "ctx")
-    sig2 = call(open_kernel, shape(1024, 256, dtype=F32), "open", (n1, w1, near[3]), ins=[VMEM] * 2 + [ANY])
+    sig2 = call(open_kernel, shape(1024, 256, dtype=F32), "open", (n1, w1, near[2]), ins=[VMEM] * 2 + [ANY])
 
     tri = (offsets[:, None] <= offsets[None, :]).astype(BF16)
     blocks = jnp.arange(32, dtype=jnp.int32)
@@ -722,7 +727,7 @@
     starts = jnp.sum(before[None, :, :] * within[:, None, :, 63], -1)
     decay = (within + starts[:, :, None]).reshape(2, 1, SPAN)
 
-    attn_own, attn, log_total = attend(block_map, ids, recv, decay, [wo_all, *near[1:3]])
+    attn_own, attn, log_total = attend(block_map, ids, recv, decay, [near[1]])
     attn2 = swap(attn_own, "ctx").reshape(8, 2, 128, 128).transpose(0, 2, 1, 3)
     attn2 = attn2.reshape(1024, 256)
     o2 = (attn2.astype(F32) * sig2).astype(BF16)
@@ -741,8 +746,8 @@
         (ids, w2g, *c_parts),
         ins=[SMEM] + [VMEM] * 9,
     )
-    dn2, ffo, u, dpre = feed_forward(n2, c_all, w2, w_down)
-    dn2 = lax.psum_scatter(dn2, "fsdp", scatter_dimension=0, tiled=True)
+    both, u, dpre = feed_forward(n2, c_all, w2, w_down)
+    both = lax.psum_scatter(both, "fsdp", scatter_dimension=0, tiled=True)
 
     fg = call(
         ffn_grad_kernel,
@@ -760,11 +765,14 @@
             shape(1, 1536, dtype=F32),
         ),
         "mid_back",
-        (dn2, h, inv2, c_own, gains, wo_all, fg),
+        (both, h, inv2, c_own, gains, wo_all, fg),
         ins=[VMEM] * 6 + [ANY],
     )
     do2 = swap(do_own, "fsdp").reshape(1024, 256)
-    da = gather(da_own, "fsdp")
+    da_near = [da_own] + [
+        lax.ppermute(da_own, "fsdp", [(f, (f + 2 * k) % 8) for f in range(8)])
+        for k in range(1, 4)
+    ]
     do2 = do2.astype(F32)
     datt2 = (do2 * sig2).astype(BF16)
     dlog2 = (do2 * attn2.astype(F32) * sig2 * (1.0 - sig2)).astype(BF16)
@@ -774,34 +782,44 @@
     fg_rows = lax.psum_scatter(
         fg.reshape(16 * 1152, 128), "ctx", scatter_dimension=0, tiled=True
     )
-    go = call(out_grad_kernel, shape(16, 48, 384), "out_grad", (o2, da))
+    da_near = [after(piece, datt_send) for piece in da_near]
+    da_far = [lax.ppermute(p, "fsdp", [(f, f ^ 1) for f in range(8)]) for p in da_near]
+    go = call(
+        out_grad_kernel,
+        shape(16, 48, 384),
+        "out_grad",
+        (ids, o2, *da_near, *da_far),
+        [pltpu.VMEM((1024, 256), BF16), pltpu.VMEM((1024, 1536), BF16)],
+        [SMEM] + [VMEM] * 9,
+    )
     dheads = attend_back(block_map, ids, recv, datt, attn, log_total, decay, go)
     dback = swap(dheads, "ctx")
+    cols_g = call(
+        split_kernel, (shape(96, 128),) * 8, "split", (ids, fg_rows), ins=[SMEM, VMEM]
+    )
+    cols_g = [cols_g[0]] + [
+        lax.ppermute(cols_g[k], "fsdp", [(f, (f + k) % 8) for f in range(8)]) for k in range(1, 8)
+    ]
     g1, dproj = call(
         head_grad_kernel,
         (shape(16, 8, 80, 128), shape(1024, 576)),
         "head_grad",
-        (n1, dback, dlog2),
+        (n1, dback, dlog2, *cols_g[1:]),
+        ins=[VMEM] * 3 + [ANY] * 7,
         flops=3 * 10**9,
     )
     g1 = swap(g1.reshape(128, 80, 128), BOTH).reshape(16, 8, 80, 128)
 
     dn1 = call(
         input_grad_kernel,
-        shape(8, 272, 1536),
+        shape(8, 144, 1536),
         "input_grad",
-        (ids, dproj, dlog2, dback[:, 128, 0:256], fpre, w1, gains, n1, gain2_part, ffo),
-        ins=[SMEM] + [VMEM] * 9,
+        (ids, dproj, dlog2, dback[:, 128, 0:256], fpre, w1, gains, n1, gain2_part),
+        ins=[SMEM] + [VMEM] * 8,
         flops=3 * 10**9,
     )
-    cols_g = call(
-        split_kernel, (shape(96, 128),) * 8, "split", (ids, fg_rows, dn1), ins=[SMEM, VMEM, ANY]
-    )
-    cols_g = [cols_g[0]] + [
-        lax.ppermute(cols_g[k], "fsdp", [(f, (f + k) % 8) for f in range(8)]) for k in range(1, 8)
-    ]
     dn1 = lax.psum_scatter(
-        dn1.reshape(8 * 272, 1536), "fsdp", scatter_dimension=0, tiled=True
+        dn1.reshape(8 * 144, 1536), "fsdp", scatter_dimension=0, tiled=True
     )
     total = call(
         head_sum_kernel,
@@ -824,7 +842,7 @@
     live = (
         lax.dynamic_slice_in_dim(block_map, 2 * ci, 2)[:, None] * 64 + offsets[None, :]
     ).reshape(128) < lengths[0]
-    mixed = jnp.where(live[:, None], h + dn1[144:272].astype(F32), 0.0).astype(BF16)
+    mixed = jnp.where(live[:, None], h + both[:, 1536:3072].astype(F32), 0.0).astype(BF16)
     query_g, key_g, value_g, outgate_g, output_g, gate_g, up_g, down_g = unpack(ids, total)
     return (
         mixed[None], tokens_grad[None], small[3, 0:192], query_g, key_g, value_g, forget_g,

time: 555 us -> 556 us (level)
  blocking collectives: 73.8 us -> 14.7 us
  waiting for transfers between devices: 232 us -> 283 us
    all_to_all x3 -> x1, blocking collectives: 73.8 us -> 14.7 us  [swap(): return lax.all_to_all(array, axis, 0, 0, tiled=True)]
    all_to_all x6 -> x8, waiting for transfers between devices: 76.3 us -> 131 us  [swap(): return lax.all_to_all(array, axis, 0, 0, tiled=True)]
    reduce_scatter x1, waiting for transfers between devices: 2.22 us -> 35.8 us  [per_device(): lax.psum_scatter(fg.reshape(16 * 1152, 128), 'ctx', scatter_dimension=0,...]
    all_gather x6 -> x5, waiting for transfers between devices: 79.9 us -> 54.9 us  [gather(): return lax.all_gather(array, axis, axis=0, tiled=True)]
    reduce_scatter x2, waiting for transfers between devices: 46.7 us -> 30.7 us  [the longest x1 30.7 us: per_device(): both = lax.psum_scatter(both, 'fsdp', scatter_dimension=0, tiled=True)]
    ppermute x7, starting transfers between devices: 20.9 us -> 8.67 us  [per_device(): lax.ppermute(cols_g[k], 'fsdp', [(f, (f + k) % 8) for f in range(8)])]
    all_to_all x6 -> x8, starting transfers between devices: 38.8 us -> 48.2 us  [swap(): return lax.all_to_all(array, axis, 0, 0, tiled=True)]
    ppermute x0 -> x3, waiting for transfers between devices: none -> 7.85 us  [per_device(): lax.ppermute(da_own, 'fsdp', [(f, (f + 2 * k) % 8) for f in range(8)])]
  transfers between devices with their start and end apart: 29 -> 37, of which waited for: 20 -> 19; matrix products, arithmetic and copies ran while one was open for 3% -> 3% of each run, Pallas kernels for 17% -> 13%
where the time goes in v3:
time: 556 us; the launch traced here: 546 us
  waiting for transfers between devices  283 us (51%)
  Pallas kernels  135 us (24%)
  starting transfers between devices  68.7 us (12%)
  local copies, waits for them, and re-layouts  23.9 us (4%)
  between operations  15.6 us (3%)
  blocking collectives  14.7 us (3%)
    all_to_all x8, waiting for transfers between devices, swap(): return lax.all_to_all(array, axis, 0, 0, tiled=True)  131 us
    pallas_call x15, Pallas kernels, call(): pl.pallas_call(kernel, grid=(1,), out_shape=outs, in_specs=ins or [VMEM]...  103 us
    all_gather x5, waiting for transfers between devices, gather(): return lax.all_gather(array, axis, axis=0, tiled=True)  54.9 us
    all_to_all x8, starting transfers between devices, swap(): return lax.all_to_all(array, axis, 0, 0, tiled=True)  48.2 us
    reduce_scatter x1, waiting for transfers between devices, per_device(): lax.psum_scatter(fg.reshape(16 * 1152, 128), 'ctx', scatter_dimension=0,...  35.8 us
    reduce_scatter x1, waiting for transfers between devices, per_device(): both = lax.psum_scatter(both, 'fsdp', scatter_dimension=0, tiled=True)  30.7 us
    ppermute x3, waiting for transfers between devices, per_device(): lax.ppermute(c_own, 'fsdp', [(f, (f + 2 * k) % 8) for f in range(8)])  16.9 us
    pallas_call x1, Pallas kernels, feed_forward(): pl.pallas_call(ffn_kernel, grid=(1024 // rows,), out_shape=(shape(1024, 3...  15.2 us
  transfers between devices with their start and end apart: 37, of which 19 were waited for; matrix products, arithmetic and copies ran while one was open for 3% of the time, Pallas kernels for 13%

profile of v3, /device:TPU:1, one launch (start us, length us, event | category | flops | bytes accessed | tf_op | source)
XLA Modules:
  0.0 546.5 jit_solution(10532760995166077184)
XLA Ops:
  10.4 6.2 %pack.1 = (bf16[8,208,896]{2,1,0:T(8,128)(2,1)}, bf16[128,1536]{1,0:T(8,128)(2,1)}, bf16[128,1536]{1,0:T(8,128)(2,1)}) custom-call(s32[5]{0:T(128)} %stack.32.ids, s32[32]{0:T(128)} %bm_ref.5, s32[1]{0:T(128)} %copy.81.len_ref, bf16[128,1536]{1,0:T(8,128)(2,1)} %bitcast.65, bf16[128,1536]{1,0:T(8,128)(2,1)} %bitcast.68, bf16[192,1536]{1,0:T(8,128)(2,1)} %wq.1, ...), custom_call_target="tpu_custom_call" | custom-call | flops 1000000000 | bytes 10000000 | tf_op jit(solution)/shard_map/pack/pallas_call | solution.py:36
  16.7 5.8 %all-to-all-start = ((bf16[8,208,896]{2,1,0:T(8,128)(2,1)}), bf16[8,208,896]{2,1,0:T(8,128)(2,1)S(1)}, u32[]{:S(2)}, u32[]{:S(2)}) async-start(bf16[8,208,896]{2,1,0:T(8,128)(2,1)} %get-tuple-element.60), calls=%async_computation | async-start | bytes 5963776 | tf_op jit(solution)/shard_map/all_to_all | solution.py:676
  23.2 47.8 %all-to-all-done.w1r = bf16[8,208,896]{2,1,0:T(8,128)(2,1)S(1)} async-done(((bf16[8,208,896]{2,1,0:T(8,128)(2,1)}), bf16[8,208,896]{2,1,0:T(8,128)(2,1)S(1)}, u32[]{:S(2)}, u32[]{:S(2)}) %all-to-all-start) | async-done | bytes 2981920 | tf_op jit(solution)/shard_map/all_to_all | solution.py:676
  71.0 1.6 copy-done.5
  72.6 7.6 %project.1 = (bf16[1024,1536]{1,0:T(8,128)(2,1)}, bf16[16,144,384]{2,1,0:T(8,128)(2,1)}, f32[8,1024]{1,0:T(8,128)}, f32[8,1536]{1,0:T(8,128)}, bf16[1536,896]{1,...) custom-call(bf16[1024,1536]{1,0:T(8,128)(2,1)} %all-gather.6.cloned.1.call-done.x, ...), custom_call_target="tpu_custom_call" | custom-call | flops 2000000000 | bytes 10000000 | tf_op jit(solution)/shard_map/project/pallas_call | solution.py:132
  80.9 7.8 %all-to-all-start.1 = ((bf16[16,144,384]{2,1,0:T(8,128)(2,1)}), bf16[16,144,384]{2,1,0:T(8,128)(2,1)S(1)}, u32[]{:S(2)}, u32[]{:S(2)}) async-start(bf16[16,144,384]{2,1,0:T(8,128)(2,1)} %get-tuple-element.61), calls=%async_computation.1 | async-start | bytes 3538944 | tf_op jit(solution)/shard_map/all_to_all | solution.py:676
  89.1 24.7 %all-to-all-done.1.r1 = bf16[16,144,384]{2,1,0:T(8,128)(2,1)S(1)} async-done(((bf16[16,144,384]{2,1,0:T(8,128)(2,1)}), bf16[16,144,384]{2,1,0:T(8,128)(2,1)S(1)}, u32[]{:S(2)}, u32[]{:S(2)}) %all-to-all-start.1) | async-done | bytes 1769504 | tf_op jit(solution)/shard_map/all_to_all | solution.py:676
  116.2 13.8 %attend.1 = (bf16[16,128,128]{2,1,0:T(8,128)(2,1)}, f32[2,2048,64]{2,1,0:T(8,128)}, f32[2,1,2048]{2,1,0:T(1,128)}) custom-call(s32[32]{0:T(128)} %bm_ref.5, s32[5]{0:T(128)} %stack.32.ids, bf16[16,144,384]{2,1,0:T(8,128)(2,1)} %copy-done.7, f32[2,1,2048]{2,1,0:T(1,128)} %reshape.116.fr, bf16[128,1536]{1,0:T(8,128)(2,1)} %copy-done.12), custom_call_target="tpu_custom_call" | custom-call | flops 4000000000 | bytes 10000000 | tf_op jit(solution)/shard_map/attend/pallas_call | solution.py:36
  129.9 5.0 all-to-all-start.2
  135.8 10.1 %collective-permute-done.1._a.refs_2_ = bf16[128,1536]{1,0:T(8,128)(2,1)S(1)} collective-permute-done((bf16[128,1536]{1,0:T(8,128)(2,1)S(1)}, bf16[128,1536]{1,0:T(8,128)(2,1)S(1)}, u32[]{:S(2)}, u32[]{:S(2)}) %collective-permute-start.1) | collective-permute-done | bytes 393248 | tf_op jit(solution)/shard_map/ppermute | solution.py:709
  146.6 4.7 open.1
  153.2 14.7 %all_to_all.45.o_r = bf16[8,128,256]{2,1,0:T(8,128)(2,1)} all-to-all(bf16[8,128,256]{2,1,0:T(8,128)(2,1)S(1)} %bitcast.60), channel_id=1, replica_groups=mesh['ctx'=16,'fsdp'=8] {'fsdp'}, dimensions={0} | all-to-all | bytes 1048576 | tf_op jit(solution)/shard_map/all_to_all | solution.py:676
  167.9 5.6 %mid.1 = (f32[128,1536]{1,0:T(8,128)}, bf16[128,1536]{1,0:T(8,128)(2,1)}, f32[128,128]{1,0:T(8,128)}) custom-call(bf16[8,128,256]{2,1,0:T(8,128)(2,1)} %all_to_all.45.o_r, bf16[1536,1536]{1,0:T(8,128)(2,1)} %all-gather.8.cloned.1.call-done.wo, bf16[128,1536]{1,0:T(8,128)(2,1)} %bitcast.66, f32[8,1536]{1,0:T(8,128)} %get-tuple-element.67.gains), custom_call_target="tpu_custom_call" | custom-call | flops 1000000000 | bytes 10000000 | tf_op jit(solution)/shard_map/mid/pallas_call | solution.py:36
  176.4 6.8 %collective-permute-done.2.refs_3_ = bf16[128,1536]{1,0:T(8,128)(2,1)S(1)} collective-permute-done((bf16[128,1536]{1,0:T(8,128)(2,1)S(1)}, bf16[128,1536]{1,0:T(8,128)(2,1)S(1)}, u32[]{:S(2)}, u32[]{:S(2)}) %collective-permute-start.2) | collective-permute-done | bytes 393248 | tf_op jit(solution)/shard_map/ppermute | solution.py:709
  183.2 2.3 collective-permute-start.6
  187.2 6.3 %ready.1 = (bf16[1536,1024]{1,0:T(8,128)(2,1)}, bf16[1024,1536]{1,0:T(8,128)(2,1)}) custom-call(s32[5]{0:T(128)} %stack.32.ids, bf16[16,768,128]{2,1,0:T(8,128)(2,1)} %bitcast.61, bf16[128,1536]{1,0:T(8,128)(2,1)} %get-tuple-element.62.refs_0_.c_ref, bf16[128,1536]{1,0:T(8,128)(2,1)} %copy-done.12, bf16[128,1536]{1,0:T(8,128)(2,1)} %copy-done.9, ...), custom_call_target="tpu_custom_call" | custom-call | flops 1000000000 | bytes 10000000 | tf_op jit(solution)/shard_map/ready/pallas_call | solution.py:36
  193.4 9.5 %all-gather.10.cloned.1.call-done.n2 = bf16[1024,1536]{1,0:T(8,128)(2,1)} async-done(((bf16[128,1536]{1,0:T(8,128)(2,1)}), bf16[1024,1536]{1,0:T(8,128)(2,1)}) %all-gather.10.cloned.1.call-update) | async-done | bytes 3145744 | tf_op jit(solution)/shard_map/all_gather | solution.py:680
  202.9 15.2 %feed_forward.1 = (bf16[1024,3072]{1,0:T(8,128)(2,1)}, bf16[1024,512]{1,0:T(8,128)(2,1)}, bf16[1024,1024]{1,0:T(8,128)(2,1)}) custom-call(bf16[1024,1536]{1,0:T(8,128)(2,1)} %all-gather.10.cloned.1.call-done.n2, bf16[1024,1536]{1,0:T(8,128)(2,1)} %get-tuple-element.71.c, bf16[1536,1024]{1,0:T(8,128)(2,1)} %get-tuple-element.72.w2, bf16[512,1536]{1,0:T(8,128)(2,1)} %wd.1), custom_call_target="tpu_custom_call" | custom-call | flops 10000000000 | bytes 20000000 | tf_op jit(solution)/shard_map/feed_forward/pallas_call | solution.py:426
  218.2 10.9 %ffn_grad.1._after.refs_0_ = bf16[16,1152,128]{2,1,0:T(8,128)(2,1)} custom-call(bf16[1024,1536]{1,0:T(8,128)(2,1)} %all-gather.10.cloned.1.call-done.n2, bf16[1024,1024]{1,0:T(8,128)(2,1)} %get-tuple-element.75.dpre, bf16[1024,512]{1,0:T(8,128)(2,1)} %get-tuple-element.76.u, bf16[1024,1536]{1,0:T(8,128)(2,1)} %get-tuple-element.71.c), custom_call_target="tpu_custom_call" | custom-call | flops 5000000000 | bytes 10000000 | tf_op jit(solution)/shard_map/ffn_grad/pallas_call | solution.py:36
  229.1 30.7 %reduce-scatter.4.cloned.1.call-done.dn2_r = bf16[128,3072]{1,0:T(8,128)(2,1)} async-done(((bf16[1024,3072]{1,0:T(8,128)(2,1)}), bf16[128,3072]{1,0:T(8,128)(2,1)}) %reduce-scatter.4.cloned.1.call-update) | async-done | bytes 786448 | tf_op jit(solution)/shard_map/reduce_scatter | solution.py:750
  259.8 6.0 %mid_back.1 = (f32[128,1536]{1,0:T(8,128)}, bf16[128,1536]{1,0:T(8,128)(2,1)}, bf16[8,128,256]{2,1,0:T(8,128)(2,1)}, f32[1,1536]{1,0:T(1,128)}) custom-call(bf16[128,3072]{1,0:T(8,128)(2,1)} %reduce-scatter.4.cloned.1.call-done.dn2_r, f32[128,1536]{1,0:T(8,128)} %get-tuple-element.68.h_ref, f32[128,128]{1,0:T(8,128)} %get-tuple-element.74.r2_ref, ...), custom_call_target="tpu_custom_call" | custom-call | flops 1000000000 | bytes 10000000 | tf_op jit(solution)/shard_map/mid_back/pallas_call | solution.py:36
  265.8 4.8 all-to-all-start.4
  270.5 2.6 collective-permute-start.9
  274.3 5.8 %all-to-all-done.4 = bf16[8,128,256]{2,1,0:T(8,128)(2,1)S(1)} async-done(((bf16[8,128,256]{2,1,0:T(8,128)(2,1)}), bf16[8,128,256]{2,1,0:T(8,128)(2,1)S(1)}, u32[]{:S(2)}, u32[]{:S(2)}) %all-to-all-start.4) | async-done | bytes 524320 | tf_op jit(solution)/shard_map/all_to_all | solution.py:676
  282.2 6.7 %all-to-all-start.5 = ((bf16[16,128,128]{2,1,0:T(8,128)(2,1)}), bf16[16,128,128]{2,1,0:T(8,128)(2,1)S(1)}, u32[]{:S(2)}, u32[]{:S(2)}) async-start(bf16[16,128,128]{2,1,0:T(8,128)(2,1)} %bitcast.20.refs_1_), calls=%async_computation.6 | async-start | bytes 1048576 | tf_op jit(solution)/shard_map/all_to_all | solution.py:676
  288.9 7.8 %collective-permute-done.7.refs_0_ = bf16[128,1536]{1,0:T(8,128)(2,1)} collective-permute-done((bf16[128,1536]{1,0:T(8,128)(2,1)S(1)}, bf16[128,1536]{1,0:T(8,128)(2,1)}, u32[]{:S(2)}, u32[]{:S(2)}) %collective-permute-start.7) | collective-permute-done | bytes 393248 | tf_op jit(solution)/shard_map/ppermute | solution.py:773
  301.8 3.9 out_grad.1.go
  306.4 18.6 %attend_back.1 = bf16[16,192,384]{2,1,0:T(8,128)(2,1)} custom-call(s32[32]{0:T(128)} %bm_ref.5, s32[5]{0:T(128)} %stack.32.ids, bf16[16,144,384]{2,1,0:T(8,128)(2,1)} %copy-done.7, bf16[16,128,128]{2,1,0:T(8,128)(2,1)} %copy-done.11, f32[2,2048,64]{2,1,0:T(8,128)} %get-tuple-element.78.attn_ref, f32[2,1,2048]{2,1,0:T(1,128)} %get-tuple-element.79.l_ref, ...), custom_call_target="tpu_custom_call" | custom-call | flops 10000000000 | bytes 10000000 | tf_op jit(solution)/shard_map/attend_back/pallas_call | solution.py:36
  325.0 6.8 %all-to-all-start.6 = ((bf16[16,192,384]{2,1,0:T(8,128)(2,1)}), bf16[16,192,384]{2,1,0:T(8,128)(2,1)S(1)}, u32[]{:S(2)}, u32[]{:S(2)}) async-start(bf16[16,192,384]{2,1,0:T(8,128)(2,1)} %attend_back.1), calls=%async_computation.7 | async-start | bytes 4718592 | tf_op jit(solution)/shard_map/all_to_all | solution.py:676
  331.9 35.8 %reduce-scatter.6.cloned.1.call-done.r.mine = bf16[1152,128]{1,0:T(8,128)(2,1)} async-done(((bf16[18432,128]{1,0:T(8,128)(2,1)}), bf16[1152,128]{1,0:T(8,128)(2,1)}) %reduce-scatter.6.cloned.1.call-update) | async-done | bytes 294928 | tf_op jit(solution)/shard_map/reduce_scatter | solution.py:782
  367.7 1.7 split.1
  369.4 2.1 collective-permute-start.14
  371.5 2.4 collective-permute-start.16
  374.8 2.2 collective-permute-start.18
  381.7 8.3 %head_grad.1 = (bf16[16,8,80,128]{3,2,1,0:T(8,128)(2,1)}, bf16[1024,576]{1,0:T(8,128)(2,1)}) custom-call(bf16[1024,1536]{1,0:T(8,128)(2,1)} %get-tuple-element.64.n1, bf16[16,192,384]{2,1,0:T(8,128)(2,1)} %copy-done.2, bf16[1024,256]{1,0:T(8,128)(2,1)} %get-tuple-element.104.dlog2, bf16[96,128]{1,0:T(8,128)(2,1)} %copy-done.25, bf16[96,128]{1,0:T(8,128)(2,1)} %copy-done.26, ...), custom_call_target="tpu_custom_call" | custom-call | flops 3000000000 | bytes 10000000 | tf_op jit(solution)/shard_map/head_grad/pallas_call | solution.py:36
  390.0 9.8 %input_grad.1 = bf16[8,144,1536]{2,1,0:T(8,128)(2,1)} custom-call(s32[5]{0:T(128)} %stack.32.ids, bf16[1024,576]{1,0:T(8,128)(2,1)} %get-tuple-element.90.dproj, bf16[1024,256]{1,0:T(8,128)(2,1)} %get-tuple-element.104.dlog2, bf16[16,256]{1,0:T(8,128)(2,1)} %bitcast.71, f32[8,1024]{1,0:T(8,128)} %get-tuple-element.91.fpre, ...), custom_call_target="tpu_custom_call" | custom-call | flops 3000000000 | bytes 10000000 | tf_op jit(solution)/shard_map/input_grad/pallas_call | solution.py:36
  399.9 7.7 %all-to-all-start.7 = ((bf16[128,80,128]{2,1,0:T(8,128)(2,1)}), bf16[128,80,128]{2,1,0:T(8,128)(2,1)S(1)}, u32[]{:S(2)}, u32[]{:S(2)}) async-start(bf16[128,80,128]{2,1,0:T(8,128)(2,1)} %bitcast.23), calls=%async_computation.9 | async-start | bytes 5242880 | tf_op jit(solution)/shard_map/all_to_all | solution.py:676
  407.6 2.0 slice.47.go
  409.7 48.0 %all-to-all-done.7 = bf16[128,80,128]{2,1,0:T(8,128)(2,1)S(1)} async-done(((bf16[128,80,128]{2,1,0:T(8,128)(2,1)}), bf16[128,80,128]{2,1,0:T(8,128)(2,1)S(1)}, u32[]{:S(2)}, u32[]{:S(2)}) %all-to-all-start.7) | async-done | bytes 2621472 | tf_op jit(solution)/shard_map/all_to_all | solution.py:676
  457.7 1.5 copy-done.6
  459.2 3.3 head_sum.1
  465.0 3.6 all-to-all-start.8
  468.6 1.9 fusion.5
  470.4 2.6 finish.1
  473.0 5.0 all-to-all-done.8.r
  478.8 1.7 small_sum.1
  484.6 45.4 %all-gather.14.cloned.1.call-done = bf16[30976,128]{1,0:T(8,128)(2,1)} async-done(((bf16[1936,128]{1,0:T(8,128)(2,1)}), bf16[30976,128]{1,0:T(8,128)(2,1)}) %all-gather.14.cloned.1.call-update) | async-done | bytes 7929872 | tf_op jit(solution)/shard_map/all_gather | solution.py:680
  530.0 9.2 %unpack.1 = (f32[192,1536]{1,0:T(8,128)}, f32[192,1536]{1,0:T(8,128)}, f32[192,1536]{1,0:T(8,128)}, f32[192,1536]{1,0:T(8,128)}, f32[192,1536]{1,0:T(8,128)}, /*...) custom-call(s32[5]{0:T(128)} %stack.32.ids, bf16[16,1936,128]{2,1,0:T(8,128)(2,1)} %bitcast.75), custom_call_target="tpu_custom_call" | custom-call | flops 60000002048 | bytes 30000000 | tf_op jit(solution)/shard_map/unpack/pallas_call | solution.py:650
  (164 shorter events, 37.0 us)
Async XLA Ops:
  7.2 63.8 %all-gather.6.cloned.1.call-start = ((), (), s32[]{:S(2)}) async-start(), calls=%async_computation.12 | async-start | bytes 3538944 | tf_op jit(solution)/shard_map/all_gather | solution.py:680
  16.7 5.8 %copy-start.32 = (bf16[3]{0:T(256)(128)(2,1)S(1)}, bf16[3]{0:T(256)(128)(2,1)}, u32[]{:S(2)}) copy-start(bf16[3]{0:T(256)(128)(2,1)} %param.25) | copy-start | bytes 22
  16.7 54.3 %all-to-all-start = ((bf16[8,208,896]{2,1,0:T(8,128)(2,1)}), bf16[8,208,896]{2,1,0:T(8,128)(2,1)S(1)}, u32[]{:S(2)}, u32[]{:S(2)}) async-start(bf16[8,208,896]{2,1,0:T(8,128)(2,1)} %get-tuple-element.60), calls=%async_computation | async-start | bytes 5963776 | tf_op jit(solution)/shard_map/all_to_all | solution.py:676
  22.5 145.4 %all-gather.8.cloned.1.call-start = ((), (), s32[]{:S(2)}) async-start(), calls=%async_computation.13 | async-start | bytes 5308416 | tf_op jit(solution)/shard_map/all_gather | solution.py:680
  80.2 8.6 %copy-start.8 = (bf16[128,1536]{1,0:T(8,128)(2,1)S(1)}, bf16[128,1536]{1,0:T(8,128)(2,1)}, u32[]{:S(2)}) copy-start(bf16[128,1536]{1,0:T(8,128)(2,1)} %get-tuple-element.62.refs_0_.c_ref) | copy-start | bytes 1179652
  80.2 33.9 %copy-start.23 = (s32[32]{0:T(128)S(1)}, s32[32]{0:T(128)}, u32[]{:S(2)}) copy-start(s32[32]{0:T(128)} %bm_ref.5) | copy-start | bytes 388
  80.2 106.9 %all-gather.12.cloned.1.call-start = ((), (), s32[]{:S(2)}) async-start(), calls=%async_computation.15 | async-start | bytes 3342336 | tf_op jit(solution)/shard_map/all_gather | solution.py:680
  80.9 32.8 %all-to-all-start.1 = ((bf16[16,144,384]{2,1,0:T(8,128)(2,1)}), bf16[16,144,384]{2,1,0:T(8,128)(2,1)S(1)}, u32[]{:S(2)}, u32[]{:S(2)}) async-start(bf16[16,144,384]{2,1,0:T(8,128)(2,1)} %get-tuple-element.61), calls=%async_computation.1 | async-start | bytes 3538944 | tf_op jit(solution)/shard_map/all_to_all | solution.py:676
  88.7 26.7 %collective-permute-start = (bf16[128,1536]{1,0:T(8,128)(2,1)S(1)}, bf16[128,1536]{1,0:T(8,128)(2,1)S(1)}, u32[]{:S(2)}, u32[]{:S(2)}) collective-permute-start(bf16[128,1536]{1,0:T(8,128)(2,1)S(1)} %copy-done.8), channel_id=1, source_target_pairs={{0,2},{1,3},{2,4},{3,5},{4,6},{5,7},{6,0},{7,1},{8,10},{9,11},{10,... | collective-permute-start | bytes 1179656 | tf_op jit(solution)/shard_map/ppermute | solution.py:709
  129.9 21.4 %all-to-all-start.2 = ((bf16[16,128,128]{2,1,0:T(8,128)(2,1)}), bf16[16,128,128]{2,1,0:T(8,128)(2,1)S(1)}, u32[]{:S(2)}, u32[]{:S(2)}) async-start(bf16[16,128,128]{2,1,0:T(8,128)(2,1)} %get-tuple-element.63), calls=%async_computation.2 | async-start | bytes 1048576 | tf_op jit(solution)/shard_map/all_to_all | solution.py:676
  135.0 67.9 %all-gather.10.cloned.1.call-start = ((), (), s32[]{:S(2)}) async-start(), calls=%async_computation.14 | async-start | bytes 3538944 | tf_op jit(solution)/shard_map/all_gather | solution.py:680
  135.0 10.8 %collective-permute-start.1 = (bf16[128,1536]{1,0:T(8,128)(2,1)S(1)}, bf16[128,1536]{1,0:T(8,128)(2,1)S(1)}, u32[]{:S(2)}, u32[]{:S(2)}) collective-permute-start(bf16[128,1536]{1,0:T(8,128)(2,1)S(1)} %copy-done.8), channel_id=1, source_target_pairs={{0,4},{1,5},{2,6},{3,7},{4,0},{5,1},{6,2},{7,3},{8,12},{9,13},{10,... | collective-permute-start | bytes 1179656 | tf_op jit(solution)/shard_map/ppermute | solution.py:709
  153.2 20.3 %copy-start.1 = (bf16[1024,256]{1,0:T(8,128)(2,1)}, bf16[1024,256]{1,0:T(8,128)(2,1)S(1)}, u32[]{:S(2)}) copy-start(bf16[1024,256]{1,0:T(8,128)(2,1)S(1)} %fusion.4.o) | copy-start | bytes 1572868
  167.9 7.9 %copy-start.13 = (bf16[128,1536]{1,0:T(8,128)(2,1)S(1)}, bf16[128,1536]{1,0:T(8,128)(2,1)}, u32[]{:S(2)}) copy-start(bf16[128,1536]{1,0:T(8,128)(2,1)} %copy-done.12) | copy-start | bytes 1179652
  167.9 7.9 %copy-start.10 = (bf16[128,1536]{1,0:T(8,128)(2,1)S(1)}, bf16[128,1536]{1,0:T(8,128)(2,1)}, u32[]{:S(2)}) copy-start(bf16[128,1536]{1,0:T(8,128)(2,1)} %copy-done.9) | copy-start | bytes 1179652
  173.5 86.3 %reduce-scatter.4.cloned.1.call-start = ((), (), s32[]{:S(2)}) async-start(), calls=%async_computation.16 | async-start | bytes 7077888 | tf_op jit(solution)/shard_map/reduce_scatter | solution.py:750
  173.5 9.6 %collective-permute-start.2 = (bf16[128,1536]{1,0:T(8,128)(2,1)S(1)}, bf16[128,1536]{1,0:T(8,128)(2,1)S(1)}, u32[]{:S(2)}, u32[]{:S(2)}) collective-permute-start(bf16[128,1536]{1,0:T(8,128)(2,1)S(1)} %copy-done.8), channel_id=1, source_target_pairs={{0,6},{1,7},{2,0},{3,1},{4,2},{5,3},{6,4},{7,5},{8,14},{9,15},{10,... | collective-permute-start | bytes 1179656 | tf_op jit(solution)/shard_map/ppermute | solution.py:709
  174.5 11.1 %collective-permute-start.3 = (bf16[128,1536]{1,0:T(8,128)(2,1)S(1)}, bf16[128,1536]{1,0:T(8,128)(2,1)S(1)}, u32[]{:S(2)}, u32[]{:S(2)}) collective-permute-start(bf16[128,1536]{1,0:T(8,128)(2,1)S(1)} %copy-done.8), channel_id=1, source_target_pairs={{0,1},{1,0},{2,3},{3,2},{4,5},{5,4},{6,7},{7,6},{8,9},{9,8},{10,11... | collective-permute-start | bytes 1179656 | tf_op jit(solution)/shard_map/ppermute | solution.py:711
  175.9 9.7 %collective-permute-start.4 = (bf16[128,1536]{1,0:T(8,128)(2,1)S(1)}, bf16[128,1536]{1,0:T(8,128)(2,1)S(1)}, u32[]{:S(2)}, u32[]{:S(2)}) collective-permute-start(bf16[128,1536]{1,0:T(8,128)(2,1)S(1)} %copy-done.13), channel_id=1, source_target_pairs={{0,1},{1,0},{2,3},{3,2},{4,5},{5,4},{6,7},{7,6},{8,9},{9,8},{10,11... | collective-permute-start | bytes 1179656 | tf_op jit(solution)/shard_map/ppermute | solution.py:711
  175.9 9.7 %collective-permute-start.5 = (bf16[128,1536]{1,0:T(8,128)(2,1)S(1)}, bf16[128,1536]{1,0:T(8,128)(2,1)S(1)}, u32[]{:S(2)}, u32[]{:S(2)}) collective-permute-start(bf16[128,1536]{1,0:T(8,128)(2,1)S(1)} %copy-done.10), channel_id=1, source_target_pairs={{0,1},{1,0},{2,3},{3,2},{4,5},{5,4},{6,7},{7,6},{8,9},{9,8},{10,11... | collective-permute-start | bytes 1179656 | tf_op jit(solution)/shard_map/ppermute | solution.py:711
  183.2 4.0 copy-start.14
  183.2 4.0 collective-permute-start.6
  218.1 149.6 %reduce-scatter.6.cloned.1.call-start = ((), (), s32[]{:S(2)}) async-start(), calls=%async_computation.17 | async-start | bytes 5013504 | tf_op jit(solution)/shard_map/reduce_scatter | solution.py:782
  265.7 4.8 copy-start.3
  265.7 14.3 %copy-start = (f32[1024,256]{1,0:T(8,128)S(1)}, f32[1024,256]{1,0:T(8,128)}, u32[]{:S(2)}) copy-start(f32[1024,256]{1,0:T(8,128)} %open.1) | copy-start | bytes 3145732
  265.8 14.3 %all-to-all-start.4 = ((bf16[8,128,256]{2,1,0:T(8,128)(2,1)}), bf16[8,128,256]{2,1,0:T(8,128)(2,1)S(1)}, u32[]{:S(2)}, u32[]{:S(2)}) async-start(bf16[8,128,256]{2,1,0:T(8,128)(2,1)} %get-tuple-element.77), calls=%async_computation.5 | async-start | bytes 1048576 | tf_op jit(solution)/shard_map/all_to_all | solution.py:676
  270.5 18.3 %collective-permute-start.9 = (bf16[128,1536]{1,0:T(8,128)(2,1)S(1)}, bf16[128,1536]{1,0:T(8,128)(2,1)}, u32[]{:S(2)}, u32[]{:S(2)}) collective-permute-start(bf16[128,1536]{1,0:T(8,128)(2,1)S(1)} %copy-done.3), channel_id=1, source_target_pairs={{0,6},{1,7},{2,0},{3,1},{4,2},{5,3},{6,4},{7,5},{8,14},{9,15},{10,... | collective-permute-start | bytes 1179656 | tf_op jit(solution)/shard_map/ppermute | solution.py:773
  273.2 15.7 %collective-permute-start.8 = (bf16[128,1536]{1,0:T(8,128)(2,1)S(1)}, bf16[128,1536]{1,0:T(8,128)(2,1)}, u32[]{:S(2)}, u32[]{:S(2)}) collective-permute-start(bf16[128,1536]{1,0:T(8,128)(2,1)S(1)} %copy-done.3), channel_id=1, source_target_pairs={{0,4},{1,5},{2,6},{3,7},{4,0},{5,1},{6,2},{7,3},{8,12},{9,13},{10,... | collective-permute-start | bytes 1179656 | tf_op jit(solution)/shard_map/ppermute | solution.py:773
  273.7 23.0 %collective-permute-start.7 = (bf16[128,1536]{1,0:T(8,128)(2,1)S(1)}, bf16[128,1536]{1,0:T(8,128)(2,1)}, u32[]{:S(2)}, u32[]{:S(2)}) collective-permute-start(bf16[128,1536]{1,0:T(8,128)(2,1)S(1)} %copy-done.3), channel_id=1, source_target_pairs={{0,2},{1,3},{2,4},{3,5},{4,6},{5,7},{6,0},{7,1},{8,10},{9,11},{10,... | collective-permute-start | bytes 1179656 | tf_op jit(solution)/shard_map/ppermute | solution.py:773
  282.2 23.5 %all-to-all-start.5 = ((bf16[16,128,128]{2,1,0:T(8,128)(2,1)}), bf16[16,128,128]{2,1,0:T(8,128)(2,1)S(1)}, u32[]{:S(2)}, u32[]{:S(2)}) async-start(bf16[16,128,128]{2,1,0:T(8,128)(2,1)} %bitcast.20.refs_1_), calls=%async_computation.6 | async-start | bytes 1048576 | tf_op jit(solution)/shard_map/all_to_all | solution.py:676
  296.7 2.4 collective-permute-start.10
  297.6 2.1 collective-permute-start.11
  297.6 2.7 collective-permute-start.12
  298.1 2.7 collective-permute-start.13
  325.0 53.1 %all-to-all-start.6 = ((bf16[16,192,384]{2,1,0:T(8,128)(2,1)}), bf16[16,192,384]{2,1,0:T(8,128)(2,1)S(1)}, u32[]{:S(2)}, u32[]{:S(2)}) async-start(bf16[16,192,384]{2,1,0:T(8,128)(2,1)} %attend_back.1), calls=%async_computation.7 | async-start | bytes 4718592 | tf_op jit(solution)/shard_map/all_to_all | solution.py:676
  331.9 130.6 %reduce-scatter.8.cloned.1.call-start = ((), (), s32[]{:S(2)}) async-start(), calls=%async_computation.18 | async-start | bytes 3981312 | tf_op jit(solution)/shard_map/reduce_scatter | solution.py:821
  369.4 7.6 %collective-permute-start.14 = (bf16[96,128]{1,0:T(8,128)(2,1)}, bf16[96,128]{1,0:T(8,128)(2,1)S(1)}, u32[]{:S(2)}, u32[]{:S(2)}) collective-permute-start(bf16[96,128]{1,0:T(8,128)(2,1)} %get-tuple-element.81), channel_id=1, source_target_pairs={{0,1},{1,2},{2,3},{3,4},{4,5},{5,6},{6,7},{7,0},{8,9},{9,10},{10,1... | collective-permute-start | bytes 73736 | tf_op jit(solution)/shard_map/ppermute | solution.py:801
  371.5 5.8 %collective-permute-start.15 = (bf16[96,128]{1,0:T(8,128)(2,1)}, bf16[96,128]{1,0:T(8,128)(2,1)S(1)}, u32[]{:S(2)}, u32[]{:S(2)}) collective-permute-start(bf16[96,128]{1,0:T(8,128)(2,1)} %get-tuple-element.82), channel_id=1, source_target_pairs={{0,2},{1,3},{2,4},{3,5},{4,6},{5,7},{6,0},{7,1},{8,10},{9,11},{10,... | collective-permute-start | bytes 73736 | tf_op jit(solution)/shard_map/ppermute | solution.py:801
  371.5 7.3 %collective-permute-start.16 = (bf16[96,128]{1,0:T(8,128)(2,1)}, bf16[96,128]{1,0:T(8,128)(2,1)S(1)}, u32[]{:S(2)}, u32[]{:S(2)}) collective-permute-start(bf16[96,128]{1,0:T(8,128)(2,1)} %get-tuple-element.83), channel_id=1, source_target_pairs={{0,3},{1,4},{2,5},{3,6},{4,7},{5,0},{6,1},{7,2},{8,11},{9,12},{10,... | collective-permute-start | bytes 73736 | tf_op jit(solution)/shard_map/ppermute | solution.py:801
  373.9 4.9 collective-permute-start.17
  374.8 5.0 collective-permute-start.18
  377.0 4.1 copy-start.25
  377.0 3.1 collective-permute-start.19
  377.3 3.8 collective-permute-start.20
  399.9 57.8 %all-to-all-start.7 = ((bf16[128,80,128]{2,1,0:T(8,128)(2,1)}), bf16[128,80,128]{2,1,0:T(8,128)(2,1)S(1)}, u32[]{:S(2)}, u32[]{:S(2)}) async-start(bf16[128,80,128]{2,1,0:T(8,128)(2,1)} %bitcast.23), calls=%async_computation.9 | async-start | bytes 5242880 | tf_op jit(solution)/shard_map/all_to_all | solution.py:676
  407.6 122.4 %all-gather.14.cloned.1.call-start = ((), (), s32[]{:S(2)}) async-start(), calls=%async_computation.19 | async-start | bytes 8425472 | tf_op jit(solution)/shard_map/all_gather | solution.py:680
  459.2 9.4 %copy-start.4 = (f32[128,1536]{1,0:T(8,128)S(1)}, f32[128,1536]{1,0:T(8,128)}, u32[]{:S(2)}) copy-start(f32[128,1536]{1,0:T(8,128)} %get-tuple-element.68.h_ref) | copy-start | bytes 2359300
  465.0 13.0 %all-to-all-start.8 = ((bf16[16,8,1536]{2,1,0:T(8,128)(2,1)}), bf16[16,8,1536]{2,1,0:T(8,128)(2,1)S(1)}, u32[]{:S(2)}, u32[]{:S(2)}) async-start(bf16[16,8,1536]{2,1,0:T(8,128)(2,1)} %broadcast_in_dim.46), calls=%async_computation.11 | async-start | bytes 786432 | tf_op jit(solution)/shard_map/all_to_all | solution.py:676
  (22 other events, 33.2 us)
Sparse Core Ops, SparseCore 0:
  16.8 47.2 all-gather.5
  80.3 41.5 all-gather.7
  124.1 49.3 all-gather.11
  175.6 27.1 all-gather.9
  218.2 41.5 reduce-scatter.3
  265.9 101.8 reduce-scatter.5
  400.0 56.1 reduce-scatter.7
  462.6 67.3 all-gather.13

commit v4 on v3

--- a/solution.py
+++ b/solution.py
@@ -87,7 +87,7 @@
                     out[d, 192:208, b * 128 : (b + 1) * 128] = w[pl.ds(at, 16), pl.ds(col, 128)]
 
 
-def open_kernel(n1, w1, _a, sig):
+def open_kernel(n1, w1, sig):
     sig[...] = jax.nn.sigmoid(dot(n1[...], w1[:, 640:896]))
 
 
@@ -473,7 +473,7 @@
                 ]
 
 
-def split_kernel(ids, r, *outs):
+def split_kernel(ids, r, _after, *outs):
     for k in range(8):
         at = pl.multiple_of(lax.rem(ids[2] + k, 8) * 96, 16)
         outs[k][...] = r[pl.ds(at, 96), :]
@@ -494,8 +494,7 @@
         out[c] = t[cr * 48 : (cr + 1) * 48, cc * 384 : (cc + 1) * 384]
 
 
-def head_grad_kernel(n1, dback, dlog2, *refs):
-    out, dproj = refs[-2:]
+def head_grad_kernel(n1, dback, dlog2, out, dproj):
     for s in range(8):
         d0, d1 = dback[2 * s], dback[2 * s + 1]
         dproj[s * 128 : (s + 1) * 128, :] = jnp.concatenate(
@@ -715,7 +714,7 @@
     wo_all = gather(wo_own, "fsdp")
     w2g = gather(w2p, "ctx").reshape(16, 768, 128)
     recv = swap(send, "ctx")
-    sig2 = call(open_kernel, shape(1024, 256, dtype=F32), "open", (n1, w1, near[2]), ins=[VMEM] * 2 + [ANY])
+    sig2 = call(open_kernel, shape(1024, 256, dtype=F32), "open", (n1, w1))
 
     tri = (offsets[:, None] <= offsets[None, :]).astype(BF16)
     blocks = jnp.arange(32, dtype=jnp.int32)
@@ -794,18 +793,11 @@
     )
     dheads = attend_back(block_map, ids, recv, datt, attn, log_total, decay, go)
     dback = swap(dheads, "ctx")
-    cols_g = call(
-        split_kernel, (shape(96, 128),) * 8, "split", (ids, fg_rows), ins=[SMEM, VMEM]
-    )
-    cols_g = [cols_g[0]] + [
-        lax.ppermute(cols_g[k], "fsdp", [(f, (f + k) % 8) for f in range(8)]) for k in range(1, 8)
-    ]
     g1, dproj = call(
         head_grad_kernel,
         (shape(16, 8, 80, 128), shape(1024, 576)),
         "head_grad",
-        (n1, dback, dlog2, *cols_g[1:]),
-        ins=[VMEM] * 3 + [ANY] * 7,
+        (n1, dback, dlog2),
         flops=3 * 10**9,
     )
     g1 = swap(g1.reshape(128, 80, 128), BOTH).reshape(16, 8, 80, 128)
@@ -818,6 +810,12 @@
         ins=[SMEM] + [VMEM] * 8,
         flops=3 * 10**9,
     )
+    cols_g = call(
+        split_kernel, (shape(96, 128),) * 8, "split", (ids, fg_rows, dn1), ins=[SMEM, VMEM, ANY]
+    )
+    cols_g = [cols_g[0]] + [
+        lax.ppermute(cols_g[k], "fsdp", [(f, (f + k) % 8) for f in range(8)]) for k in range(1, 8)
+    ]
     dn1 = lax.psum_scatter(
         dn1.reshape(8 * 144, 1536), "fsdp", scatter_dimension=0, tiled=True
     )
@@ -826,7 +824,7 @@
         shape(1936, 128),
         "head_sum",
         (g1, dback[:, 144:192], fg_rows, *cols_g),
-        flops=3 * 10**9,
+        flops=int(6 * 10**10),
     )
     total, dn1 = tie(total, dn1)
     total = gather(total, "ctx").reshape(16, 1936, 128)

time: 556 us -> 536 us (0.964)
  waiting for transfers between devices: 283 us -> 222 us
  blocking collectives: 14.7 us -> 56.7 us
    all_to_all x1 -> x2, blocking collectives: 14.7 us -> 56.7 us  [swap(): return lax.all_to_all(array, axis, 0, 0, tiled=True)]
    all_to_all x8 -> x7, waiting for transfers between devices: 131 us -> 91.2 us  [swap(): return lax.all_to_all(array, axis, 0, 0, tiled=True)]
    reduce_scatter x1, waiting for transfers between devices: 35.8 us -> 0.02 us  [per_device(): lax.psum_scatter(fg.reshape(16 * 1152, 128), 'ctx', scatter_dimension=0,...]
    reduce_scatter x1, waiting for transfers between devices: 0.01 us -> 10.8 us  [per_device(): lax.psum_scatter(dn1.reshape(8 * 144, 1536), 'fsdp', scatter_dimension=0,...]
    ppermute x7, waiting for transfers between devices: 2.34 us -> 11.3 us  [per_device(): lax.ppermute(cols_g[k], 'fsdp', [(f, (f + k) % 8) for f in range(8)])]
    all_to_all x8 -> x7, starting transfers between devices: 48.2 us -> 42.2 us  [swap(): return lax.all_to_all(array, axis, 0, 0, tiled=True)]
  transfers between devices with their start and end apart: 37 -> 36, of which waited for: 19 -> 19; matrix products, arithmetic and copies ran while one was open for 3% -> 3% of each run, Pallas kernels for 13% -> 17%
where the time goes in v4:
time: 536 us; the launch traced here: 526 us
  waiting for transfers between devices  222 us (41%)
  Pallas kernels  135 us (25%)
  starting transfers between devices  67.9 us (13%)
  blocking collectives  56.7 us (11%)
  local copies, waits for them, and re-layouts  23.2 us (4%)
  between operations  15.6 us (3%)
    pallas_call x15, Pallas kernels, call(): pl.pallas_call(kernel, grid=(1,), out_shape=outs, in_specs=ins or [VMEM]...  103 us
    all_to_all x7, waiting for transfers between devices, swap(): return lax.all_to_all(array, axis, 0, 0, tiled=True)  91.2 us
    all_to_all x2, blocking collectives, swap(): return lax.all_to_all(array, axis, 0, 0, tiled=True)  56.7 us
    all_gather x5, waiting for transfers between devices, gather(): return lax.all_gather(array, axis, axis=0, tiled=True)  52.6 us
    all_to_all x7, starting transfers between devices, swap(): return lax.all_to_all(array, axis, 0, 0, tiled=True)  42.2 us
    reduce_scatter x1, waiting for transfers between devices, per_device(): both = lax.psum_scatter(both, 'fsdp', scatter_dimension=0, tiled=True)  30.4 us
    pallas_call x1, Pallas kernels, feed_forward(): pl.pallas_call(ffn_kernel, grid=(1024 // rows,), out_shape=(shape(1024, 3...  15.2 us
    ppermute x3, waiting for transfers between devices, per_device(): lax.ppermute(c_own, 'fsdp', [(f, (f + 2 * k) % 8) for f in range(8)])  14.4 us
  transfers between devices with their start and end apart: 36, of which 19 were waited for; matrix products, arithmetic and copies ran while one was open for 3% of the time, Pallas kernels for 17%

profile of v4, /device:TPU:1, one launch (start us, length us, event | category | flops | bytes accessed | tf_op | source)
XLA Modules:
  0.0 526.1 jit_solution(17586247955811574303)
XLA Ops:
  10.4 6.2 %pack.1 = (bf16[8,208,896]{2,1,0:T(8,128)(2,1)}, bf16[128,1536]{1,0:T(8,128)(2,1)}, bf16[128,1536]{1,0:T(8,128)(2,1)}) custom-call(s32[5]{0:T(128)} %stack.32.ids, s32[32]{0:T(128)} %bm_ref.5, s32[1]{0:T(128)} %copy.67.len_ref, bf16[128,1536]{1,0:T(8,128)(2,1)} %bitcast.66, bf16[128,1536]{1,0:T(8,128)(2,1)} %bitcast.69, bf16[192,1536]{1,0:T(8,128)(2,1)} %wq.1, ...), custom_call_target="tpu_custom_call" | custom-call | flops 1000000000 | bytes 10000000 | tf_op jit(solution)/shard_map/pack/pallas_call | solution.py:36
  16.7 5.8 %all-to-all-start = ((bf16[8,208,896]{2,1,0:T(8,128)(2,1)}), bf16[8,208,896]{2,1,0:T(8,128)(2,1)S(1)}, u32[]{:S(2)}, u32[]{:S(2)}) async-start(bf16[8,208,896]{2,1,0:T(8,128)(2,1)} %get-tuple-element.60), calls=%async_computation | async-start | bytes 5963776 | tf_op jit(solution)/shard_map/all_to_all | solution.py:675
  23.2 47.8 %all-to-all-done.w1r = bf16[8,208,896]{2,1,0:T(8,128)(2,1)S(1)} async-done(((bf16[8,208,896]{2,1,0:T(8,128)(2,1)}), bf16[8,208,896]{2,1,0:T(8,128)(2,1)S(1)}, u32[]{:S(2)}, u32[]{:S(2)}) %all-to-all-start) | async-done | bytes 2981920 | tf_op jit(solution)/shard_map/all_to_all | solution.py:675
  72.6 7.6 %project.1 = (bf16[1024,1536]{1,0:T(8,128)(2,1)}, bf16[16,144,384]{2,1,0:T(8,128)(2,1)}, f32[8,1024]{1,0:T(8,128)}, f32[8,1536]{1,0:T(8,128)}, bf16[1536,896]{1,...) custom-call(bf16[1024,1536]{1,0:T(8,128)(2,1)} %all-gather.6.cloned.1.call-done.x, ...), custom_call_target="tpu_custom_call" | custom-call | flops 2000000000 | bytes 10000000 | tf_op jit(solution)/shard_map/project/pallas_call | solution.py:132
  80.9 7.8 %all-to-all-start.1 = ((bf16[16,144,384]{2,1,0:T(8,128)(2,1)}), bf16[16,144,384]{2,1,0:T(8,128)(2,1)S(1)}, u32[]{:S(2)}, u32[]{:S(2)}) async-start(bf16[16,144,384]{2,1,0:T(8,128)(2,1)} %get-tuple-element.61), calls=%async_computation.1 | async-start | bytes 3538944 | tf_op jit(solution)/shard_map/all_to_all | solution.py:675
  89.1 24.7 %all-to-all-done.1.r1 = bf16[16,144,384]{2,1,0:T(8,128)(2,1)S(1)} async-done(((bf16[16,144,384]{2,1,0:T(8,128)(2,1)}), bf16[16,144,384]{2,1,0:T(8,128)(2,1)S(1)}, u32[]{:S(2)}, u32[]{:S(2)}) %all-to-all-start.1) | async-done | bytes 1769504 | tf_op jit(solution)/shard_map/all_to_all | solution.py:675
  116.1 13.8 %attend.1 = (bf16[16,128,128]{2,1,0:T(8,128)(2,1)}, f32[2,2048,64]{2,1,0:T(8,128)}, f32[2,1,2048]{2,1,0:T(1,128)}) custom-call(s32[32]{0:T(128)} %bm_ref.5, s32[5]{0:T(128)} %stack.32.ids, bf16[16,144,384]{2,1,0:T(8,128)(2,1)} %copy-done.6, f32[2,1,2048]{2,1,0:T(1,128)} %reshape.116.fr, bf16[128,1536]{1,0:T(8,128)(2,1)} %copy-done.9), custom_call_target="tpu_custom_call" | custom-call | flops 4000000000 | bytes 10000000 | tf_op jit(solution)/shard_map/attend/pallas_call | solution.py:36
  129.9 5.0 all-to-all-start.2
  135.0 4.7 open.1
  139.7 7.5 %all-to-all-done.2 = bf16[16,128,128]{2,1,0:T(8,128)(2,1)S(1)} async-done(((bf16[16,128,128]{2,1,0:T(8,128)(2,1)}), bf16[16,128,128]{2,1,0:T(8,128)(2,1)S(1)}, u32[]{:S(2)}, u32[]{:S(2)}) %all-to-all-start.2) | async-done | bytes 524320 | tf_op jit(solution)/shard_map/all_to_all | solution.py:675
  149.1 14.3 %all_to_all.45.o_r = bf16[8,128,256]{2,1,0:T(8,128)(2,1)} all-to-all(bf16[8,128,256]{2,1,0:T(8,128)(2,1)S(1)} %bitcast.60), channel_id=1, replica_groups=mesh['ctx'=16,'fsdp'=8] {'fsdp'}, dimensions={0} | all-to-all | bytes 1048576 | tf_op jit(solution)/shard_map/all_to_all | solution.py:675
  163.5 5.5 %mid.1 = (f32[128,1536]{1,0:T(8,128)}, bf16[128,1536]{1,0:T(8,128)(2,1)}, f32[128,128]{1,0:T(8,128)}) custom-call(bf16[8,128,256]{2,1,0:T(8,128)(2,1)} %all_to_all.45.o_r, bf16[1536,1536]{1,0:T(8,128)(2,1)} %all-gather.8.cloned.1.call-done.wo, bf16[128,1536]{1,0:T(8,128)(2,1)} %bitcast.67, f32[8,1536]{1,0:T(8,128)} %get-tuple-element.67.gains), custom_call_target="tpu_custom_call" | custom-call | flops 1000000000 | bytes 10000000 | tf_op jit(solution)/shard_map/mid/pallas_call | solution.py:36
  169.6 2.5 collective-permute-start.2
  173.5 6.8 %collective-permute-done.1.refs_2_ = bf16[128,1536]{1,0:T(8,128)(2,1)S(1)} collective-permute-done((bf16[128,1536]{1,0:T(8,128)(2,1)S(1)}, bf16[128,1536]{1,0:T(8,128)(2,1)S(1)}, u32[]{:S(2)}, u32[]{:S(2)}) %collective-permute-start.1) | collective-permute-done | bytes 393248 | tf_op jit(solution)/shard_map/ppermute | solution.py:708
  180.2 2.0 collective-permute-start.5
  182.2 7.7 %collective-permute-done.2.refs_3_ = bf16[128,1536]{1,0:T(8,128)(2,1)S(1)} collective-permute-done((bf16[128,1536]{1,0:T(8,128)(2,1)S(1)}, bf16[128,1536]{1,0:T(8,128)(2,1)S(1)}, u32[]{:S(2)}, u32[]{:S(2)}) %collective-permute-start.2) | collective-permute-done | bytes 393248 | tf_op jit(solution)/shard_map/ppermute | solution.py:708
  189.8 2.3 collective-permute-start.6
  193.7 6.4 %ready.1 = (bf16[1536,1024]{1,0:T(8,128)(2,1)}, bf16[1024,1536]{1,0:T(8,128)(2,1)}) custom-call(s32[5]{0:T(128)} %stack.32.ids, bf16[16,768,128]{2,1,0:T(8,128)(2,1)} %bitcast.61, bf16[128,1536]{1,0:T(8,128)(2,1)} %get-tuple-element.62.refs_0_.c_ref, bf16[128,1536]{1,0:T(8,128)(2,1)} %copy-done.9, bf16[128,1536]{1,0:T(8,128)(2,1)} %copy-done.11, ...), custom_call_target="tpu_custom_call" | custom-call | flops 1000000000 | bytes 10000000 | tf_op jit(solution)/shard_map/ready/pallas_call | solution.py:36
  200.1 3.0 all-gather.10.cloned.1.call-done.n2
  203.1 15.2 %feed_forward.1 = (bf16[1024,3072]{1,0:T(8,128)(2,1)}, bf16[1024,512]{1,0:T(8,128)(2,1)}, bf16[1024,1024]{1,0:T(8,128)(2,1)}) custom-call(bf16[1024,1536]{1,0:T(8,128)(2,1)} %all-gather.10.cloned.1.call-done.n2, bf16[1024,1536]{1,0:T(8,128)(2,1)} %get-tuple-element.71.c, bf16[1536,1024]{1,0:T(8,128)(2,1)} %get-tuple-element.72.w2, bf16[512,1536]{1,0:T(8,128)(2,1)} %wd.1), custom_call_target="tpu_custom_call" | custom-call | flops 10000000000 | bytes 20000000 | tf_op jit(solution)/shard_map/feed_forward/pallas_call | solution.py:426
  218.4 11.0 %ffn_grad.1._after.refs_0_ = bf16[16,1152,128]{2,1,0:T(8,128)(2,1)} custom-call(bf16[1024,1536]{1,0:T(8,128)(2,1)} %all-gather.10.cloned.1.call-done.n2, bf16[1024,1024]{1,0:T(8,128)(2,1)} %get-tuple-element.75.dpre, bf16[1024,512]{1,0:T(8,128)(2,1)} %get-tuple-element.76.u, bf16[1024,1536]{1,0:T(8,128)(2,1)} %get-tuple-element.71.c), custom_call_target="tpu_custom_call" | custom-call | flops 5000000000 | bytes 10000000 | tf_op jit(solution)/shard_map/ffn_grad/pallas_call | solution.py:36
  229.3 30.4 %reduce-scatter.4.cloned.1.call-done.dn2_r = bf16[128,3072]{1,0:T(8,128)(2,1)} async-done(((bf16[1024,3072]{1,0:T(8,128)(2,1)}), bf16[128,3072]{1,0:T(8,128)(2,1)}) %reduce-scatter.4.cloned.1.call-update) | async-done | bytes 786448 | tf_op jit(solution)/shard_map/reduce_scatter | solution.py:749
  259.7 6.0 %mid_back.1 = (f32[128,1536]{1,0:T(8,128)}, bf16[128,1536]{1,0:T(8,128)(2,1)}, bf16[8,128,256]{2,1,0:T(8,128)(2,1)}, f32[1,1536]{1,0:T(1,128)}) custom-call(bf16[128,3072]{1,0:T(8,128)(2,1)} %reduce-scatter.4.cloned.1.call-done.dn2_r, f32[128,1536]{1,0:T(8,128)} %get-tuple-element.68.h_ref, f32[128,128]{1,0:T(8,128)} %get-tuple-element.74.r2_ref, ...), custom_call_target="tpu_custom_call" | custom-call | flops 1000000000 | bytes 10000000 | tf_op jit(solution)/shard_map/mid_back/pallas_call | solution.py:36
  265.7 4.8 all-to-all-start.4
  270.5 2.6 collective-permute-start.9
  274.3 5.8 %all-to-all-done.4 = bf16[8,128,256]{2,1,0:T(8,128)(2,1)S(1)} async-done(((bf16[8,128,256]{2,1,0:T(8,128)(2,1)}), bf16[8,128,256]{2,1,0:T(8,128)(2,1)S(1)}, u32[]{:S(2)}, u32[]{:S(2)}) %all-to-all-start.4) | async-done | bytes 524320 | tf_op jit(solution)/shard_map/all_to_all | solution.py:675
  282.1 6.7 %all-to-all-start.5 = ((bf16[16,128,128]{2,1,0:T(8,128)(2,1)}), bf16[16,128,128]{2,1,0:T(8,128)(2,1)S(1)}, u32[]{:S(2)}, u32[]{:S(2)}) async-start(bf16[16,128,128]{2,1,0:T(8,128)(2,1)} %bitcast.20.refs_1_), calls=%async_computation.6 | async-start | bytes 1048576 | tf_op jit(solution)/shard_map/all_to_all | solution.py:675
  288.8 7.8 %collective-permute-done.7.refs_0_ = bf16[128,1536]{1,0:T(8,128)(2,1)} collective-permute-done((bf16[128,1536]{1,0:T(8,128)(2,1)S(1)}, bf16[128,1536]{1,0:T(8,128)(2,1)}, u32[]{:S(2)}, u32[]{:S(2)}) %collective-permute-start.7) | collective-permute-done | bytes 393248 | tf_op jit(solution)/shard_map/ppermute | solution.py:772
  301.7 3.9 out_grad.1.go
  306.4 18.6 %attend_back.1 = bf16[16,192,384]{2,1,0:T(8,128)(2,1)} custom-call(s32[32]{0:T(128)} %bm_ref.5, s32[5]{0:T(128)} %stack.32.ids, bf16[16,144,384]{2,1,0:T(8,128)(2,1)} %copy-done.6, bf16[16,128,128]{2,1,0:T(8,128)(2,1)} %copy-done.8, f32[2,2048,64]{2,1,0:T(8,128)} %get-tuple-element.78.attn_ref, f32[2,1,2048]{2,1,0:T(1,128)} %get-tuple-element.79.l_ref, ...), custom_call_target="tpu_custom_call" | custom-call | flops 10000000000 | bytes 10000000 | tf_op jit(solution)/shard_map/attend_back/pallas_call | solution.py:36
  325.0 42.4 %all_to_all.46.dback = bf16[16,192,384]{2,1,0:T(8,128)(2,1)} all-to-all(bf16[16,192,384]{2,1,0:T(8,128)(2,1)} %attend_back.1), channel_id=1, replica_groups=mesh['ctx'=16,'fsdp'=8] {'ctx'}, dimensions={0} | all-to-all | bytes 4718592 | tf_op jit(solution)/shard_map/all_to_all | solution.py:675
  367.4 8.3 %head_grad.1 = (bf16[16,8,80,128]{3,2,1,0:T(8,128)(2,1)}, bf16[1024,576]{1,0:T(8,128)(2,1)}) custom-call(bf16[1024,1536]{1,0:T(8,128)(2,1)} %get-tuple-element.64.n1, bf16[16,192,384]{2,1,0:T(8,128)(2,1)} %all_to_all.46.dback, bf16[1024,256]{1,0:T(8,128)(2,1)} %get-tuple-element.104.dlog2), custom_call_target="tpu_custom_call" | custom-call | flops 3000000000 | bytes 10000000 | tf_op jit(solution)/shard_map/head_grad/pallas_call | solution.py:36
  375.7 5.1 all-to-all-start.7
  382.3 9.8 %input_grad.1._after = bf16[8,144,1536]{2,1,0:T(8,128)(2,1)} custom-call(s32[5]{0:T(128)} %stack.32.ids, bf16[1024,576]{1,0:T(8,128)(2,1)} %get-tuple-element.82.dproj, bf16[1024,256]{1,0:T(8,128)(2,1)} %get-tuple-element.104.dlog2, bf16[16,256]{1,0:T(8,128)(2,1)} %bitcast.72, f32[8,1024]{1,0:T(8,128)} %get-tuple-element.83.fpre, ...), custom_call_target="tpu_custom_call" | custom-call | flops 3000000000 | bytes 10000000 | tf_op jit(solution)/shard_map/input_grad/pallas_call | solution.py:36
  399.0 2.5 collective-permute-start.18
  401.5 9.1 %collective-permute-done.14.refs_1_ = bf16[96,128]{1,0:T(8,128)(2,1)S(1)} collective-permute-done((bf16[96,128]{1,0:T(8,128)(2,1)}, bf16[96,128]{1,0:T(8,128)(2,1)S(1)}, u32[]{:S(2)}, u32[]{:S(2)}) %collective-permute-start.14) | collective-permute-done | bytes 24608 | tf_op jit(solution)/shard_map/ppermute | solution.py:817
  411.5 2.2 collective-permute-done.15.refs_2_
  413.7 2.8 collective-permute-start.20
  416.4 1.9 slice.47.go
  421.5 3.3 head_sum.1
  424.8 10.8 %reduce-scatter.8.cloned.1.call-done.dn1 = bf16[144,1536]{1,0:T(8,128)(2,1)} async-done(((bf16[1152,1536]{1,0:T(8,128)(2,1)}), bf16[144,1536]{1,0:T(8,128)(2,1)}) %reduce-scatter.8.cloned.1.call-update) | async-done | bytes 442384 | tf_op jit(solution)/shard_map/reduce_scatter | solution.py:819
  438.2 6.9 %all-to-all-start.8 = ((bf16[16,8,1536]{2,1,0:T(8,128)(2,1)}), bf16[16,8,1536]{2,1,0:T(8,128)(2,1)S(1)}, u32[]{:S(2)}, u32[]{:S(2)}) async-start(bf16[16,8,1536]{2,1,0:T(8,128)(2,1)} %broadcast_in_dim.46), calls=%async_computation.11 | async-start | bytes 786432 | tf_op jit(solution)/shard_map/all_to_all | solution.py:675
  445.2 1.9 fusion.5
  447.0 2.5 finish.1
  449.5 3.9 all-to-all-done.8.r
  454.1 1.7 small_sum.1
  460.0 49.6 %all-gather.14.cloned.1.call-done = bf16[30976,128]{1,0:T(8,128)(2,1)} async-done(((bf16[1936,128]{1,0:T(8,128)(2,1)}), bf16[30976,128]{1,0:T(8,128)(2,1)}) %all-gather.14.cloned.1.call-update) | async-done | bytes 7929872 | tf_op jit(solution)/shard_map/all_gather | solution.py:679
  509.6 9.2 %unpack.1 = (f32[192,1536]{1,0:T(8,128)}, f32[192,1536]{1,0:T(8,128)}, f32[192,1536]{1,0:T(8,128)}, f32[192,1536]{1,0:T(8,128)}, f32[192,1536]{1,0:T(8,128)}, /*...) custom-call(s32[5]{0:T(128)} %stack.32.ids, bf16[16,1936,128]{2,1,0:T(8,128)(2,1)} %bitcast.76), custom_call_target="tpu_custom_call" | custom-call | flops 60000002048 | bytes 30000000 | tf_op jit(solution)/shard_map/unpack/pallas_call | solution.py:649
  (159 shorter events, 42.5 us)
Async XLA Ops:
  7.2 63.8 %all-gather.6.cloned.1.call-start = ((), (), s32[]{:S(2)}) async-start(), calls=%async_computation.12 | async-start | bytes 3538944 | tf_op jit(solution)/shard_map/all_gather | solution.py:679
  16.7 5.8 %copy-start.30 = (bf16[3]{0:T(256)(128)(2,1)S(1)}, bf16[3]{0:T(256)(128)(2,1)}, u32[]{:S(2)}) copy-start(bf16[3]{0:T(256)(128)(2,1)} %param.25) | copy-start | bytes 22
  16.7 54.3 %all-to-all-start = ((bf16[8,208,896]{2,1,0:T(8,128)(2,1)}), bf16[8,208,896]{2,1,0:T(8,128)(2,1)S(1)}, u32[]{:S(2)}, u32[]{:S(2)}) async-start(bf16[8,208,896]{2,1,0:T(8,128)(2,1)} %get-tuple-element.60), calls=%async_computation | async-start | bytes 5963776 | tf_op jit(solution)/shard_map/all_to_all | solution.py:675
  22.5 141.0 %all-gather.8.cloned.1.call-start = ((), (), s32[]{:S(2)}) async-start(), calls=%async_computation.13 | async-start | bytes 5308416 | tf_op jit(solution)/shard_map/all_gather | solution.py:679
  80.1 8.6 %copy-start.7 = (bf16[128,1536]{1,0:T(8,128)(2,1)S(1)}, bf16[128,1536]{1,0:T(8,128)(2,1)}, u32[]{:S(2)}) copy-start(bf16[128,1536]{1,0:T(8,128)(2,1)} %get-tuple-element.62.refs_0_.c_ref) | copy-start | bytes 1179652
  80.1 33.9 %copy-start.21 = (s32[32]{0:T(128)S(1)}, s32[32]{0:T(128)}, u32[]{:S(2)}) copy-start(s32[32]{0:T(128)} %bm_ref.5) | copy-start | bytes 388
  80.2 113.5 %all-gather.12.cloned.1.call-start = ((), (), s32[]{:S(2)}) async-start(), calls=%async_computation.15 | async-start | bytes 3342336 | tf_op jit(solution)/shard_map/all_gather | solution.py:679
  80.9 32.8 %all-to-all-start.1 = ((bf16[16,144,384]{2,1,0:T(8,128)(2,1)}), bf16[16,144,384]{2,1,0:T(8,128)(2,1)S(1)}, u32[]{:S(2)}, u32[]{:S(2)}) async-start(bf16[16,144,384]{2,1,0:T(8,128)(2,1)} %get-tuple-element.61), calls=%async_computation.1 | async-start | bytes 3538944 | tf_op jit(solution)/shard_map/all_to_all | solution.py:675
  88.7 26.7 %collective-permute-start = (bf16[128,1536]{1,0:T(8,128)(2,1)S(1)}, bf16[128,1536]{1,0:T(8,128)(2,1)S(1)}, u32[]{:S(2)}, u32[]{:S(2)}) collective-permute-start(bf16[128,1536]{1,0:T(8,128)(2,1)S(1)} %copy-done.7), channel_id=1, source_target_pairs={{0,2},{1,3},{2,4},{3,5},{4,6},{5,7},{6,0},{7,1},{8,10},{9,11},{10,... | collective-permute-start | bytes 1179656 | tf_op jit(solution)/shard_map/ppermute | solution.py:708
  129.9 17.3 %all-to-all-start.2 = ((bf16[16,128,128]{2,1,0:T(8,128)(2,1)}), bf16[16,128,128]{2,1,0:T(8,128)(2,1)S(1)}, u32[]{:S(2)}, u32[]{:S(2)}) async-start(bf16[16,128,128]{2,1,0:T(8,128)(2,1)} %get-tuple-element.63), calls=%async_computation.2 | async-start | bytes 1048576 | tf_op jit(solution)/shard_map/all_to_all | solution.py:675
  135.0 68.1 %all-gather.10.cloned.1.call-start = ((), (), s32[]{:S(2)}) async-start(), calls=%async_computation.14 | async-start | bytes 3538944 | tf_op jit(solution)/shard_map/all_gather | solution.py:679
  149.1 19.9 %copy-start.1 = (bf16[1024,256]{1,0:T(8,128)(2,1)}, bf16[1024,256]{1,0:T(8,128)(2,1)S(1)}, u32[]{:S(2)}) copy-start(bf16[1024,256]{1,0:T(8,128)(2,1)S(1)} %fusion.4.o) | copy-start | bytes 1572868
  163.5 10.0 %copy-start.10 = (bf16[128,1536]{1,0:T(8,128)(2,1)S(1)}, bf16[128,1536]{1,0:T(8,128)(2,1)}, u32[]{:S(2)}) copy-start(bf16[128,1536]{1,0:T(8,128)(2,1)} %copy-done.9) | copy-start | bytes 1179652
  169.0 90.7 %reduce-scatter.4.cloned.1.call-start = ((), (), s32[]{:S(2)}) async-start(), calls=%async_computation.16 | async-start | bytes 7077888 | tf_op jit(solution)/shard_map/reduce_scatter | solution.py:749
  169.1 11.2 %collective-permute-start.1 = (bf16[128,1536]{1,0:T(8,128)(2,1)S(1)}, bf16[128,1536]{1,0:T(8,128)(2,1)S(1)}, u32[]{:S(2)}, u32[]{:S(2)}) collective-permute-start(bf16[128,1536]{1,0:T(8,128)(2,1)S(1)} %copy-done.7), channel_id=1, source_target_pairs={{0,4},{1,5},{2,6},{3,7},{4,0},{5,1},{6,2},{7,3},{8,12},{9,13},{10,... | collective-permute-start | bytes 1179656 | tf_op jit(solution)/shard_map/ppermute | solution.py:708
  169.6 20.2 %collective-permute-start.2 = (bf16[128,1536]{1,0:T(8,128)(2,1)S(1)}, bf16[128,1536]{1,0:T(8,128)(2,1)S(1)}, u32[]{:S(2)}, u32[]{:S(2)}) collective-permute-start(bf16[128,1536]{1,0:T(8,128)(2,1)S(1)} %copy-done.7), channel_id=1, source_target_pairs={{0,6},{1,7},{2,0},{3,1},{4,2},{5,3},{6,4},{7,5},{8,14},{9,15},{10,... | collective-permute-start | bytes 1179656 | tf_op jit(solution)/shard_map/ppermute | solution.py:708
  172.2 19.9 %collective-permute-start.3 = (bf16[128,1536]{1,0:T(8,128)(2,1)S(1)}, bf16[128,1536]{1,0:T(8,128)(2,1)S(1)}, u32[]{:S(2)}, u32[]{:S(2)}) collective-permute-start(bf16[128,1536]{1,0:T(8,128)(2,1)S(1)} %copy-done.7), channel_id=1, source_target_pairs={{0,1},{1,0},{2,3},{3,2},{4,5},{5,4},{6,7},{7,6},{8,9},{9,8},{10,11... | collective-permute-start | bytes 1179656 | tf_op jit(solution)/shard_map/ppermute | solution.py:710
  173.5 18.7 %collective-permute-start.4 = (bf16[128,1536]{1,0:T(8,128)(2,1)S(1)}, bf16[128,1536]{1,0:T(8,128)(2,1)S(1)}, u32[]{:S(2)}, u32[]{:S(2)}) collective-permute-start(bf16[128,1536]{1,0:T(8,128)(2,1)S(1)} %copy-done.10), channel_id=1, source_target_pairs={{0,1},{1,0},{2,3},{3,2},{4,5},{5,4},{6,7},{7,6},{8,9},{9,8},{10,11... | collective-permute-start | bytes 1179656 | tf_op jit(solution)/shard_map/ppermute | solution.py:710
  180.2 13.5 %copy-start.11 = (bf16[128,1536]{1,0:T(8,128)(2,1)}, bf16[128,1536]{1,0:T(8,128)(2,1)S(1)}, u32[]{:S(2)}) copy-start(bf16[128,1536]{1,0:T(8,128)(2,1)S(1)} %collective-permute-done.1.refs_2_) | copy-start | bytes 1179652
  180.2 11.9 %collective-permute-start.5 = (bf16[128,1536]{1,0:T(8,128)(2,1)S(1)}, bf16[128,1536]{1,0:T(8,128)(2,1)S(1)}, u32[]{:S(2)}, u32[]{:S(2)}) collective-permute-start(bf16[128,1536]{1,0:T(8,128)(2,1)S(1)} %collective-permute-done.1.refs_2_), channel_id=1, source_target_pairs={{0,1},{1,0},{2,3},{3,2},{4,5},{5,4},{6,7},{7,6},{8,9},{9,8},{10,11... | collective-permute-start | bytes 1179656 | tf_op jit(solution)/shard_map/ppermute | solution.py:710
  189.8 3.8 collective-permute-start.6
  218.3 173.9 %reduce-scatter.6.cloned.1.call-start = ((), (), s32[]{:S(2)}) async-start(), calls=%async_computation.17 | async-start | bytes 5013504 | tf_op jit(solution)/shard_map/reduce_scatter | solution.py:781
  265.7 4.8 copy-start.2
  265.7 14.3 %copy-start = (f32[1024,256]{1,0:T(8,128)S(1)}, f32[1024,256]{1,0:T(8,128)}, u32[]{:S(2)}) copy-start(f32[1024,256]{1,0:T(8,128)} %open.1) | copy-start | bytes 3145732
  265.7 14.3 %all-to-all-start.4 = ((bf16[8,128,256]{2,1,0:T(8,128)(2,1)}), bf16[8,128,256]{2,1,0:T(8,128)(2,1)S(1)}, u32[]{:S(2)}, u32[]{:S(2)}) async-start(bf16[8,128,256]{2,1,0:T(8,128)(2,1)} %get-tuple-element.77), calls=%async_computation.5 | async-start | bytes 1048576 | tf_op jit(solution)/shard_map/all_to_all | solution.py:675
  270.5 18.3 %collective-permute-start.9 = (bf16[128,1536]{1,0:T(8,128)(2,1)S(1)}, bf16[128,1536]{1,0:T(8,128)(2,1)}, u32[]{:S(2)}, u32[]{:S(2)}) collective-permute-start(bf16[128,1536]{1,0:T(8,128)(2,1)S(1)} %copy-done.2), channel_id=1, source_target_pairs={{0,6},{1,7},{2,0},{3,1},{4,2},{5,3},{6,4},{7,5},{8,14},{9,15},{10,... | collective-permute-start | bytes 1179656 | tf_op jit(solution)/shard_map/ppermute | solution.py:772
  273.1 15.7 %collective-permute-start.8 = (bf16[128,1536]{1,0:T(8,128)(2,1)S(1)}, bf16[128,1536]{1,0:T(8,128)(2,1)}, u32[]{:S(2)}, u32[]{:S(2)}) collective-permute-start(bf16[128,1536]{1,0:T(8,128)(2,1)S(1)} %copy-done.2), channel_id=1, source_target_pairs={{0,4},{1,5},{2,6},{3,7},{4,0},{5,1},{6,2},{7,3},{8,12},{9,13},{10,... | collective-permute-start | bytes 1179656 | tf_op jit(solution)/shard_map/ppermute | solution.py:772
  273.7 23.0 %collective-permute-start.7 = (bf16[128,1536]{1,0:T(8,128)(2,1)S(1)}, bf16[128,1536]{1,0:T(8,128)(2,1)}, u32[]{:S(2)}, u32[]{:S(2)}) collective-permute-start(bf16[128,1536]{1,0:T(8,128)(2,1)S(1)} %copy-done.2), channel_id=1, source_target_pairs={{0,2},{1,3},{2,4},{3,5},{4,6},{5,7},{6,0},{7,1},{8,10},{9,11},{10,... | collective-permute-start | bytes 1179656 | tf_op jit(solution)/shard_map/ppermute | solution.py:772
  282.1 23.5 %all-to-all-start.5 = ((bf16[16,128,128]{2,1,0:T(8,128)(2,1)}), bf16[16,128,128]{2,1,0:T(8,128)(2,1)S(1)}, u32[]{:S(2)}, u32[]{:S(2)}) async-start(bf16[16,128,128]{2,1,0:T(8,128)(2,1)} %bitcast.20.refs_1_), calls=%async_computation.6 | async-start | bytes 1048576 | tf_op jit(solution)/shard_map/all_to_all | solution.py:675
  296.7 2.4 collective-permute-start.10
  297.5 2.1 collective-permute-start.11
  297.5 2.7 collective-permute-start.12
  298.0 2.7 collective-permute-start.13
  375.7 44.3 %all-to-all-start.7 = ((bf16[128,80,128]{2,1,0:T(8,128)(2,1)}), bf16[128,80,128]{2,1,0:T(8,128)(2,1)S(1)}, u32[]{:S(2)}, u32[]{:S(2)}) async-start(bf16[128,80,128]{2,1,0:T(8,128)(2,1)} %bitcast.63), calls=%async_computation.8 | async-start | bytes 5242880 | tf_op jit(solution)/shard_map/all_to_all | solution.py:675
  380.8 54.9 %reduce-scatter.8.cloned.1.call-start = ((), (), s32[]{:S(2)}) async-start(), calls=%async_computation.18 | async-start | bytes 3981312 | tf_op jit(solution)/shard_map/reduce_scatter | solution.py:819
  392.2 117.4 %all-gather.14.cloned.1.call-start = ((), (), s32[]{:S(2)}) async-start(), calls=%async_computation.19 | async-start | bytes 8425472 | tf_op jit(solution)/shard_map/all_gather | solution.py:679
  393.9 16.7 %collective-permute-start.14 = (bf16[96,128]{1,0:T(8,128)(2,1)}, bf16[96,128]{1,0:T(8,128)(2,1)S(1)}, u32[]{:S(2)}, u32[]{:S(2)}) collective-permute-start(bf16[96,128]{1,0:T(8,128)(2,1)} %get-tuple-element.86), channel_id=1, source_target_pairs={{0,1},{1,2},{2,3},{3,4},{4,5},{5,6},{6,7},{7,0},{8,9},{9,10},{10,1... | collective-permute-start | bytes 73736 | tf_op jit(solution)/shard_map/ppermute | solution.py:817
  395.6 18.1 %collective-permute-start.15 = (bf16[96,128]{1,0:T(8,128)(2,1)}, bf16[96,128]{1,0:T(8,128)(2,1)S(1)}, u32[]{:S(2)}, u32[]{:S(2)}) collective-permute-start(bf16[96,128]{1,0:T(8,128)(2,1)} %get-tuple-element.87), channel_id=1, source_target_pairs={{0,2},{1,3},{2,4},{3,5},{4,6},{5,7},{6,0},{7,1},{8,10},{9,11},{10,... | collective-permute-start | bytes 73736 | tf_op jit(solution)/shard_map/ppermute | solution.py:817
  396.8 23.2 %collective-permute-start.16 = (bf16[96,128]{1,0:T(8,128)(2,1)}, bf16[96,128]{1,0:T(8,128)(2,1)S(1)}, u32[]{:S(2)}, u32[]{:S(2)}) collective-permute-start(bf16[96,128]{1,0:T(8,128)(2,1)} %get-tuple-element.88), channel_id=1, source_target_pairs={{0,3},{1,4},{2,5},{3,6},{4,7},{5,0},{6,1},{7,2},{8,11},{9,12},{10,... | collective-permute-start | bytes 73736 | tf_op jit(solution)/shard_map/ppermute | solution.py:817
  398.4 21.6 %collective-permute-start.17 = (bf16[96,128]{1,0:T(8,128)(2,1)}, bf16[96,128]{1,0:T(8,128)(2,1)S(1)}, u32[]{:S(2)}, u32[]{:S(2)}) collective-permute-start(bf16[96,128]{1,0:T(8,128)(2,1)} %get-tuple-element.89), channel_id=1, source_target_pairs={{0,4},{1,5},{2,6},{3,7},{4,0},{5,1},{6,2},{7,3},{8,12},{9,13},{10,... | collective-permute-start | bytes 73736 | tf_op jit(solution)/shard_map/ppermute | solution.py:817
  399.0 21.0 %collective-permute-start.18 = (bf16[96,128]{1,0:T(8,128)(2,1)}, bf16[96,128]{1,0:T(8,128)(2,1)S(1)}, u32[]{:S(2)}, u32[]{:S(2)}) collective-permute-start(bf16[96,128]{1,0:T(8,128)(2,1)} %get-tuple-element.90), channel_id=1, source_target_pairs={{0,5},{1,6},{2,7},{3,0},{4,1},{5,2},{6,3},{7,4},{8,13},{9,14},{10,... | collective-permute-start | bytes 73736 | tf_op jit(solution)/shard_map/ppermute | solution.py:817
  410.6 10.1 %copy-start.23 = (bf16[96,128]{1,0:T(8,128)(2,1)}, bf16[96,128]{1,0:T(8,128)(2,1)S(1)}, u32[]{:S(2)}) copy-start(bf16[96,128]{1,0:T(8,128)(2,1)S(1)} %collective-permute-done.14.refs_1_) | copy-start | bytes 73732
  410.6 9.4 %collective-permute-start.19 = (bf16[96,128]{1,0:T(8,128)(2,1)}, bf16[96,128]{1,0:T(8,128)(2,1)S(1)}, u32[]{:S(2)}, u32[]{:S(2)}) collective-permute-start(bf16[96,128]{1,0:T(8,128)(2,1)} %get-tuple-element.91), channel_id=1, source_target_pairs={{0,6},{1,7},{2,0},{3,1},{4,2},{5,3},{6,4},{7,5},{8,14},{9,15},{10,... | collective-permute-start | bytes 73736 | tf_op jit(solution)/shard_map/ppermute | solution.py:817
  413.7 7.1 %copy-start.24 = (bf16[96,128]{1,0:T(8,128)(2,1)}, bf16[96,128]{1,0:T(8,128)(2,1)S(1)}, u32[]{:S(2)}) copy-start(bf16[96,128]{1,0:T(8,128)(2,1)S(1)} %collective-permute-done.15.refs_2_) | copy-start | bytes 73732
  413.7 6.3 %collective-permute-start.20 = (bf16[96,128]{1,0:T(8,128)(2,1)}, bf16[96,128]{1,0:T(8,128)(2,1)S(1)}, u32[]{:S(2)}, u32[]{:S(2)}) collective-permute-start(bf16[96,128]{1,0:T(8,128)(2,1)} %get-tuple-element.92), channel_id=1, source_target_pairs={{0,7},{1,0},{2,1},{3,2},{4,3},{5,4},{6,5},{7,6},{8,15},{9,8},{10,9... | collective-permute-start | bytes 73736 | tf_op jit(solution)/shard_map/ppermute | solution.py:817
  421.5 14.2 %copy-start.22 = (s32[32]{0:T(128)S(1)}, s32[32]{0:T(128)}, u32[]{:S(2)}) copy-start(s32[32]{0:T(128)} %bm_ref.5) | copy-start | bytes 388
  421.5 23.7 %copy-start.3 = (f32[128,1536]{1,0:T(8,128)S(1)}, f32[128,1536]{1,0:T(8,128)}, u32[]{:S(2)}) copy-start(f32[128,1536]{1,0:T(8,128)} %get-tuple-element.68.h_ref) | copy-start | bytes 2359300
  438.2 15.2 %all-to-all-start.8 = ((bf16[16,8,1536]{2,1,0:T(8,128)(2,1)}), bf16[16,8,1536]{2,1,0:T(8,128)(2,1)S(1)}, u32[]{:S(2)}, u32[]{:S(2)}) async-start(bf16[16,8,1536]{2,1,0:T(8,128)(2,1)} %broadcast_in_dim.46), calls=%async_computation.11 | async-start | bytes 786432 | tf_op jit(solution)/shard_map/all_to_all | solution.py:675
  (19 other events, 24.2 us)
Sparse Core Ops, SparseCore 0:
  16.8 47.2 all-gather.5
  80.3 41.5 all-gather.7
  124.0 49.3 all-gather.11
  175.6 27.4 all-gather.9
  218.4 41.2 reduce-scatter.3
  265.8 96.5 reduce-scatter.5
  392.3 43.3 reduce-scatter.7
  438.6 70.9 all-gather.13

commit v5 on v4

--- a/solution.py
+++ b/solution.py
@@ -255,13 +255,11 @@
 
 
 def bwd_kernel(
-    bm_ref, ids, r1, da_r, attn_ref, l_ref, fr, go,
+    bm_ref, ids, r1, da_r, attn_ref, l_ref, fr,
     ds_ref,
     q_s, k_s, v_s, da_s, kt_s, fc_s, dk_s, dv_s, out_s, rs_ref, dl_s,
 ):
     j = ids[3]
-    for c in range(16):
-        ds_ref[c, 144:192, :] = go[c]
     load_heads(bm_ref, r1, q_s, k_s, v_s)
     column_decay(fr, fc_s)
     for blk in range(32):
@@ -333,12 +331,12 @@
     )
 
 
-def attend_back(block_map, ids, r1, upstream, attn, logs, decay, go):
+def attend_back(block_map, ids, r1, upstream, attn, logs, decay):
     return call(
         bwd_kernel,
-        shape(16, 192, 384),
+        shape(16, 144, 384),
         "attend_back",
-        (block_map, ids, r1, upstream, attn, logs, decay, go),
+        (block_map, ids, r1, upstream, attn, logs, decay),
         HEADS
         + [
             pltpu.VMEM((2, SPAN, HD), BF16),
@@ -350,7 +348,7 @@
             pltpu.VMEM((2, 1, SPAN), F32),
             pltpu.VMEM((2, 32, 64), F32),
         ],
-        [SMEM, SMEM] + [VMEM] * 6,
+        [SMEM, SMEM] + [VMEM] * 5,
         flops=10**10,
     )
 
@@ -479,7 +477,7 @@
         outs[k][...] = r[pl.ds(at, 96), :]
 
 
-def out_grad_kernel(ids, o, *refs):
+def out_grad_kernel(ids, _after, o, *refs):
     pieces, out, o_s, da_s = refs[:8], refs[8], refs[9], refs[10]
     for k in range(8):
         first = ids[2] if k < 4 else ids[2] + 1 - 2 * lax.rem(ids[2], 2)
@@ -783,15 +781,7 @@
     )
     da_near = [after(piece, datt_send) for piece in da_near]
     da_far = [lax.ppermute(p, "fsdp", [(f, f ^ 1) for f in range(8)]) for p in da_near]
-    go = call(
-        out_grad_kernel,
-        shape(16, 48, 384),
-        "out_grad",
-        (ids, o2, *da_near, *da_far),
-        [pltpu.VMEM((1024, 256), BF16), pltpu.VMEM((1024, 1536), BF16)],
-        [SMEM] + [VMEM] * 9,
-    )
-    dheads = attend_back(block_map, ids, recv, datt, attn, log_total, decay, go)
+    dheads = attend_back(block_map, ids, recv, datt, attn, log_total, decay)
     dback = swap(dheads, "ctx")
     g1, dproj = call(
         head_grad_kernel,
@@ -816,6 +806,15 @@
     cols_g = [cols_g[0]] + [
         lax.ppermute(cols_g[k], "fsdp", [(f, (f + k) % 8) for f in range(8)]) for k in range(1, 8)
     ]
+    go = call(
+        out_grad_kernel,
+        shape(16, 48, 384),
+        "out_grad",
+        (ids, dn1, o2, *da_near, *da_far),
+        [pltpu.VMEM((1024, 256), BF16), pltpu.VMEM((1024, 1536), BF16)],
+        [SMEM, ANY] + [VMEM] * 9,
+    )
+    go = swap(after(go, g1), "ctx")
     dn1 = lax.psum_scatter(
         dn1.reshape(8 * 144, 1536), "fsdp", scatter_dimension=0, tiled=True
     )
@@ -823,7 +822,7 @@
         head_sum_kernel,
         shape(1936, 128),
         "head_sum",
-        (g1, dback[:, 144:192], fg_rows, *cols_g),
+        (g1, go, fg_rows, *cols_g),
         flops=int(6 * 10**10),
     )
     total, dn1 = tie(total, dn1)

time: 536 us -> 555 us (1.035)
  blocking collectives: 56.7 us -> 74.5 us
    ppermute x3, waiting for transfers between devices: 7.85 us -> 35.8 us  [per_device(): lax.ppermute(da_own, 'fsdp', [(f, (f + 2 * k) % 8) for f in range(8)])]
    all_to_all x2 -> x4, blocking collectives: 56.7 us -> 74.5 us  [swap(): return lax.all_to_all(array, axis, 0, 0, tiled=True)]
    reduce_scatter x1, waiting for transfers between devices: 10.8 us -> 0.01 us  [per_device(): lax.psum_scatter(dn1.reshape(8 * 144, 1536), 'fsdp', scatter_dimension=0,...]
    ppermute x7, waiting for transfers between devices: 11.3 us -> 2.69 us  [per_device(): lax.ppermute(cols_g[k], 'fsdp', [(f, (f + k) % 8) for f in range(8)])]
    all_to_all x7 -> x6, waiting for transfers between devices: 91.2 us -> 87.2 us  [swap(): return lax.all_to_all(array, axis, 0, 0, tiled=True)]
    all_to_all x7 -> x6, starting transfers between devices: 42.2 us -> 42.8 us  [swap(): return lax.all_to_all(array, axis, 0, 0, tiled=True)]
  transfers between devices with their start and end apart: 36 -> 35, of which waited for: 19 -> 18; matrix products, arithmetic and copies ran while one was open for 3% -> 3% of each run, Pallas kernels for 17% -> 17%
where the time goes in v5:
time: 555 us; the launch traced here: 545 us
  waiting for transfers between devices  222 us (40%)
  Pallas kernels  135 us (24%)
  blocking collectives  74.5 us (13%)
  starting transfers between devices  70.9 us (13%)
  local copies, waits for them, and re-layouts  22.8 us (4%)
  between operations  15.6 us (3%)
    pallas_call x15, Pallas kernels, call(): pl.pallas_call(kernel, grid=(1,), out_shape=outs, in_specs=ins or [VMEM]...  103 us
    all_to_all x6, waiting for transfers between devices, swap(): return lax.all_to_all(array, axis, 0, 0, tiled=True)  87.2 us
    all_to_all x4, blocking collectives, swap(): return lax.all_to_all(array, axis, 0, 0, tiled=True)  74.5 us
    all_gather x5, waiting for transfers between devices, gather(): return lax.all_gather(array, axis, axis=0, tiled=True)  47.6 us
    all_to_all x6, starting transfers between devices, swap(): return lax.all_to_all(array, axis, 0, 0, tiled=True)  42.8 us
    ppermute x3, waiting for transfers between devices, per_device(): lax.ppermute(da_own, 'fsdp', [(f, (f + 2 * k) % 8) for f in range(8)])  35.8 us
    reduce_scatter x1, waiting for transfers between devices, per_device(): both = lax.psum_scatter(both, 'fsdp', scatter_dimension=0, tiled=True)  30.4 us
    pallas_call x1, Pallas kernels, feed_forward(): pl.pallas_call(ffn_kernel, grid=(1024 // rows,), out_shape=(shape(1024, 3...  15.2 us
  transfers between devices with their start and end apart: 35, of which 18 were waited for; matrix products, arithmetic and copies ran while one was open for 3% of the time, Pallas kernels for 17%

profile of v5, /device:TPU:1, one launch (start us, length us, event | category | flops | bytes accessed | tf_op | source)
XLA Modules:
  0.0 545.1 jit_solution(14520017384002947462)
XLA Ops:
  10.4 6.2 %pack.1 = (bf16[8,208,896]{2,1,0:T(8,128)(2,1)}, bf16[128,1536]{1,0:T(8,128)(2,1)}, bf16[128,1536]{1,0:T(8,128)(2,1)}) custom-call(s32[5]{0:T(128)} %stack.32.ids, s32[32]{0:T(128)} %bm_ref.5, s32[1]{0:T(128)} %copy.81.len_ref, bf16[128,1536]{1,0:T(8,128)(2,1)} %bitcast.72, bf16[128,1536]{1,0:T(8,128)(2,1)} %bitcast.75, bf16[192,1536]{1,0:T(8,128)(2,1)} %wq.1, ...), custom_call_target="tpu_custom_call" | custom-call | flops 1000000000 | bytes 10000000 | tf_op jit(solution)/shard_map/pack/pallas_call | solution.py:36
  16.7 5.8 %all-to-all-start = ((bf16[8,208,896]{2,1,0:T(8,128)(2,1)}), bf16[8,208,896]{2,1,0:T(8,128)(2,1)S(1)}, u32[]{:S(2)}, u32[]{:S(2)}) async-start(bf16[8,208,896]{2,1,0:T(8,128)(2,1)} %get-tuple-element.60), calls=%async_computation | async-start | bytes 5963776 | tf_op jit(solution)/shard_map/all_to_all | solution.py:673
  23.2 47.8 %all-to-all-done.w1r = bf16[8,208,896]{2,1,0:T(8,128)(2,1)S(1)} async-done(((bf16[8,208,896]{2,1,0:T(8,128)(2,1)}), bf16[8,208,896]{2,1,0:T(8,128)(2,1)S(1)}, u32[]{:S(2)}, u32[]{:S(2)}) %all-to-all-start) | async-done | bytes 2981920 | tf_op jit(solution)/shard_map/all_to_all | solution.py:673
  71.0 1.6 copy-done.6
  72.6 7.6 %project.1 = (bf16[1024,1536]{1,0:T(8,128)(2,1)}, bf16[16,144,384]{2,1,0:T(8,128)(2,1)}, f32[8,1024]{1,0:T(8,128)}, f32[8,1536]{1,0:T(8,128)}, bf16[1536,896]{1,...) custom-call(bf16[1024,1536]{1,0:T(8,128)(2,1)} %all-gather.6.cloned.1.call-done.x, ...), custom_call_target="tpu_custom_call" | custom-call | flops 2000000000 | bytes 10000000 | tf_op jit(solution)/shard_map/project/pallas_call | solution.py:132
  80.9 7.8 %all-to-all-start.1 = ((bf16[16,144,384]{2,1,0:T(8,128)(2,1)}), bf16[16,144,384]{2,1,0:T(8,128)(2,1)S(1)}, u32[]{:S(2)}, u32[]{:S(2)}) async-start(bf16[16,144,384]{2,1,0:T(8,128)(2,1)} %get-tuple-element.61), calls=%async_computation.1 | async-start | bytes 3538944 | tf_op jit(solution)/shard_map/all_to_all | solution.py:673
  89.1 24.7 %all-to-all-done.1.r1 = bf16[16,144,384]{2,1,0:T(8,128)(2,1)S(1)} async-done(((bf16[16,144,384]{2,1,0:T(8,128)(2,1)}), bf16[16,144,384]{2,1,0:T(8,128)(2,1)S(1)}, u32[]{:S(2)}, u32[]{:S(2)}) %all-to-all-start.1) | async-done | bytes 1769504 | tf_op jit(solution)/shard_map/all_to_all | solution.py:673
  116.1 13.8 %attend.1 = (bf16[16,128,128]{2,1,0:T(8,128)(2,1)}, f32[2,2048,64]{2,1,0:T(8,128)}, f32[2,1,2048]{2,1,0:T(1,128)}) custom-call(s32[32]{0:T(128)} %bm_ref.5, s32[5]{0:T(128)} %stack.32.ids, bf16[16,144,384]{2,1,0:T(8,128)(2,1)} %copy-done.7, f32[2,1,2048]{2,1,0:T(1,128)} %reshape.116.fr, bf16[128,1536]{1,0:T(8,128)(2,1)} %copy-done.16), custom_call_target="tpu_custom_call" | custom-call | flops 4000000000 | bytes 10000000 | tf_op jit(solution)/shard_map/attend/pallas_call | solution.py:36
  129.9 5.0 all-to-all-start.2
  135.0 4.7 open.1
  139.7 7.5 %all-to-all-done.2 = bf16[16,128,128]{2,1,0:T(8,128)(2,1)S(1)} async-done(((bf16[16,128,128]{2,1,0:T(8,128)(2,1)}), bf16[16,128,128]{2,1,0:T(8,128)(2,1)S(1)}, u32[]{:S(2)}, u32[]{:S(2)}) %all-to-all-start.2) | async-done | bytes 524320 | tf_op jit(solution)/shard_map/all_to_all | solution.py:673
  149.1 14.3 %all_to_all.50.o_r = bf16[8,128,256]{2,1,0:T(8,128)(2,1)} all-to-all(bf16[8,128,256]{2,1,0:T(8,128)(2,1)S(1)} %bitcast.67), channel_id=1, replica_groups=mesh['ctx'=16,'fsdp'=8] {'fsdp'}, dimensions={0} | all-to-all | bytes 1048576 | tf_op jit(solution)/shard_map/all_to_all | solution.py:673
  163.5 5.5 %mid.1 = (f32[128,1536]{1,0:T(8,128)}, bf16[128,1536]{1,0:T(8,128)(2,1)}, f32[128,128]{1,0:T(8,128)}) custom-call(bf16[8,128,256]{2,1,0:T(8,128)(2,1)} %all_to_all.50.o_r, bf16[1536,1536]{1,0:T(8,128)(2,1)} %all-gather.8.cloned.1.call-done.wo, bf16[128,1536]{1,0:T(8,128)(2,1)} %bitcast.73, f32[8,1536]{1,0:T(8,128)} %get-tuple-element.67.gains), custom_call_target="tpu_custom_call" | custom-call | flops 1000000000 | bytes 10000000 | tf_op jit(solution)/shard_map/mid/pallas_call | solution.py:36
  169.6 2.5 collective-permute-start.2
  173.5 6.8 %collective-permute-done.1.refs_2_ = bf16[128,1536]{1,0:T(8,128)(2,1)S(1)} collective-permute-done((bf16[128,1536]{1,0:T(8,128)(2,1)S(1)}, bf16[128,1536]{1,0:T(8,128)(2,1)S(1)}, u32[]{:S(2)}, u32[]{:S(2)}) %collective-permute-start.1) | collective-permute-done | bytes 393248 | tf_op jit(solution)/shard_map/ppermute | solution.py:706
  180.2 2.0 collective-permute-start.5
  182.2 7.7 %collective-permute-done.2.refs_3_ = bf16[128,1536]{1,0:T(8,128)(2,1)S(1)} collective-permute-done((bf16[128,1536]{1,0:T(8,128)(2,1)S(1)}, bf16[128,1536]{1,0:T(8,128)(2,1)S(1)}, u32[]{:S(2)}, u32[]{:S(2)}) %collective-permute-start.2) | collective-permute-done | bytes 393248 | tf_op jit(solution)/shard_map/ppermute | solution.py:706
  189.9 2.3 collective-permute-start.6
  193.8 6.4 %ready.1 = (bf16[1536,1024]{1,0:T(8,128)(2,1)}, bf16[1024,1536]{1,0:T(8,128)(2,1)}) custom-call(s32[5]{0:T(128)} %stack.32.ids, bf16[16,768,128]{2,1,0:T(8,128)(2,1)} %bitcast.68, bf16[128,1536]{1,0:T(8,128)(2,1)} %get-tuple-element.62.refs_0_.c_ref, bf16[128,1536]{1,0:T(8,128)(2,1)} %copy-done.16, bf16[128,1536]{1,0:T(8,128)(2,1)} %copy-done.18, ...), custom_call_target="tpu_custom_call" | custom-call | flops 1000000000 | bytes 10000000 | tf_op jit(solution)/shard_map/ready/pallas_call | solution.py:36
  200.2 3.0 all-gather.10.cloned.1.call-done.n2
  203.1 15.2 %feed_forward.1 = (bf16[1024,3072]{1,0:T(8,128)(2,1)}, bf16[1024,512]{1,0:T(8,128)(2,1)}, bf16[1024,1024]{1,0:T(8,128)(2,1)}) custom-call(bf16[1024,1536]{1,0:T(8,128)(2,1)} %all-gather.10.cloned.1.call-done.n2, bf16[1024,1536]{1,0:T(8,128)(2,1)} %get-tuple-element.71.c, bf16[1536,1024]{1,0:T(8,128)(2,1)} %get-tuple-element.72.w2, bf16[512,1536]{1,0:T(8,128)(2,1)} %wd.1), custom_call_target="tpu_custom_call" | custom-call | flops 10000000000 | bytes 20000000 | tf_op jit(solution)/shard_map/feed_forward/pallas_call | solution.py:424
  218.4 11.0 %ffn_grad.1._after.refs_0_ = bf16[16,1152,128]{2,1,0:T(8,128)(2,1)} custom-call(bf16[1024,1536]{1,0:T(8,128)(2,1)} %all-gather.10.cloned.1.call-done.n2, bf16[1024,1024]{1,0:T(8,128)(2,1)} %get-tuple-element.75.dpre, bf16[1024,512]{1,0:T(8,128)(2,1)} %get-tuple-element.76.u, bf16[1024,1536]{1,0:T(8,128)(2,1)} %get-tuple-element.71.c), custom_call_target="tpu_custom_call" | custom-call | flops 5000000000 | bytes 10000000 | tf_op jit(solution)/shard_map/ffn_grad/pallas_call | solution.py:36
  229.3 30.4 %reduce-scatter.4.cloned.1.call-done.dn2_r = bf16[128,3072]{1,0:T(8,128)(2,1)} async-done(((bf16[1024,3072]{1,0:T(8,128)(2,1)}), bf16[128,3072]{1,0:T(8,128)(2,1)}) %reduce-scatter.4.cloned.1.call-update) | async-done | bytes 786448 | tf_op jit(solution)/shard_map/reduce_scatter | solution.py:747
  259.7 6.0 %mid_back.1 = (f32[128,1536]{1,0:T(8,128)}, bf16[128,1536]{1,0:T(8,128)(2,1)}, bf16[8,128,256]{2,1,0:T(8,128)(2,1)}, f32[1,1536]{1,0:T(1,128)}) custom-call(bf16[128,3072]{1,0:T(8,128)(2,1)} %reduce-scatter.4.cloned.1.call-done.dn2_r, f32[128,1536]{1,0:T(8,128)} %get-tuple-element.68.h_ref, f32[128,128]{1,0:T(8,128)} %get-tuple-element.74.r2_ref, ...), custom_call_target="tpu_custom_call" | custom-call | flops 1000000000 | bytes 10000000 | tf_op jit(solution)/shard_map/mid_back/pallas_call | solution.py:36
  266.7 13.1 %all_to_all.51 = bf16[8,128,256]{2,1,0:T(8,128)(2,1)S(1)} all-to-all(bf16[8,128,256]{2,1,0:T(8,128)(2,1)S(1)} %copy-done.13), channel_id=1, replica_groups=mesh['ctx'=16,'fsdp'=8] {'fsdp'}, dimensions={0} | all-to-all | bytes 1048576 | tf_op jit(solution)/shard_map/all_to_all | solution.py:673
  281.1 18.4 %all_to_all.52.da_r = bf16[16,128,128]{2,1,0:T(8,128)(2,1)} all-to-all(bf16[16,128,128]{2,1,0:T(8,128)(2,1)S(1)} %bitcast.58), channel_id=1, replica_groups=mesh['ctx'=16,'fsdp'=8] {'ctx'}, dimensions={0} | all-to-all | bytes 1048576 | tf_op jit(solution)/shard_map/all_to_all | solution.py:673
  299.6 18.3 %attend_back.1 = bf16[16,144,384]{2,1,0:T(8,128)(2,1)} custom-call(s32[32]{0:T(128)} %bm_ref.5, s32[5]{0:T(128)} %stack.32.ids, bf16[16,144,384]{2,1,0:T(8,128)(2,1)} %copy-done.7, bf16[16,128,128]{2,1,0:T(8,128)(2,1)} %all_to_all.52.da_r, f32[2,2048,64]{2,1,0:T(8,128)} %get-tuple-element.78.attn_ref, f32[2,1,2048]{2,1,0:T(1,128)} %get-tuple-element.79.l_ref, ...), custom_call_target="tpu_custom_call" | custom-call | flops 10000000000 | bytes 10000000 | tf_op jit(solution)/shard_map/attend_back/pallas_call | solution.py:36
  317.9 28.6 %all_to_all.53.dback = bf16[16,144,384]{2,1,0:T(8,128)(2,1)} all-to-all(bf16[16,144,384]{2,1,0:T(8,128)(2,1)} %attend_back.1), channel_id=1, replica_groups=mesh['ctx'=16,'fsdp'=8] {'ctx'}, dimensions={0} | all-to-all | bytes 3538944 | tf_op jit(solution)/shard_map/all_to_all | solution.py:673
  346.5 8.2 %head_grad.1 = (bf16[16,8,80,128]{3,2,1,0:T(8,128)(2,1)}, bf16[1024,576]{1,0:T(8,128)(2,1)}) custom-call(bf16[1024,1536]{1,0:T(8,128)(2,1)} %get-tuple-element.64.n1, bf16[16,144,384]{2,1,0:T(8,128)(2,1)} %all_to_all.53.dback, bf16[1024,256]{1,0:T(8,128)(2,1)} %get-tuple-element.104.dlog2), custom_call_target="tpu_custom_call" | custom-call | flops 3000000000 | bytes 10000000 | tf_op jit(solution)/shard_map/head_grad/pallas_call | solution.py:36
  354.7 9.7 %all-to-all-start.7 = ((bf16[128,80,128]{2,1,0:T(8,128)(2,1)}), bf16[128,80,128]{2,1,0:T(8,128)(2,1)S(1)}, u32[]{:S(2)}, u32[]{:S(2)}) async-start(bf16[128,80,128]{2,1,0:T(8,128)(2,1)} %bitcast.69), calls=%async_computation.8 | async-start | bytes 5242880 | tf_op jit(solution)/shard_map/all_to_all | solution.py:673
  366.1 9.9 %input_grad.1._after = bf16[8,144,1536]{2,1,0:T(8,128)(2,1)} custom-call(s32[5]{0:T(128)} %stack.32.ids, bf16[1024,576]{1,0:T(8,128)(2,1)} %get-tuple-element.81.dproj, bf16[1024,256]{1,0:T(8,128)(2,1)} %get-tuple-element.104.dlog2, bf16[16,256]{1,0:T(8,128)(2,1)} %bitcast.78, f32[8,1024]{1,0:T(8,128)} %get-tuple-element.82.fpre, ...), custom_call_target="tpu_custom_call" | custom-call | flops 3000000000 | bytes 10000000 | tf_op jit(solution)/shard_map/input_grad/pallas_call | solution.py:36
  377.0 2.7 collective-permute-start.9
  380.7 28.4 %collective-permute-done.9.refs_0_ = bf16[128,1536]{1,0:T(8,128)(2,1)S(1)} collective-permute-done((bf16[128,1536]{1,0:T(8,128)(2,1)S(1)}, bf16[128,1536]{1,0:T(8,128)(2,1)S(1)}, u32[]{:S(2)}, u32[]{:S(2)}) %collective-permute-start.9) | collective-permute-done | bytes 393248 | tf_op jit(solution)/shard_map/ppermute | solution.py:770
  409.1 1.6 collective-permute-done.8.refs_0_
  411.5 5.8 %collective-permute-done.7.refs_0_ = bf16[128,1536]{1,0:T(8,128)(2,1)} collective-permute-done((bf16[128,1536]{1,0:T(8,128)(2,1)S(1)}, bf16[128,1536]{1,0:T(8,128)(2,1)}, u32[]{:S(2)}, u32[]{:S(2)}) %collective-permute-start.7) | collective-permute-done | bytes 393248 | tf_op jit(solution)/shard_map/ppermute | solution.py:770
  422.9 3.9 out_grad.1.refs_0_
  426.8 1.5 copy-done.1
  428.3 7.6 %all-to-all-start.8 = ((bf16[16,48,384]{2,1,0:T(8,128)(2,1)}), bf16[16,48,384]{2,1,0:T(8,128)(2,1)S(1)}, u32[]{:S(2)}, u32[]{:S(2)}) async-start(bf16[16,48,384]{2,1,0:T(8,128)(2,1)} %after.10), calls=%async_computation.9 | async-start | bytes 1179648 | tf_op jit(solution)/shard_map/all_to_all | solution.py:673
  435.9 1.7 split.1
  437.6 6.5 %collective-permute-start.14 = (bf16[96,128]{1,0:T(8,128)(2,1)}, bf16[96,128]{1,0:T(8,128)(2,1)S(1)}, u32[]{:S(2)}, u32[]{:S(2)}) collective-permute-start(bf16[96,128]{1,0:T(8,128)(2,1)} %get-tuple-element.86), channel_id=1, source_target_pairs={{0,1},{1,2},{2,3},{3,4},{4,5},{5,6},{6,7},{7,0},{8,9},{9,10},{10,1... | collective-permute-start | bytes 73736 | tf_op jit(solution)/shard_map/ppermute | solution.py:807
  444.1 2.1 collective-permute-start.16
  453.8 3.3 head_sum.1
  459.7 6.9 %all-to-all-start.9 = ((bf16[16,8,1536]{2,1,0:T(8,128)(2,1)}), bf16[16,8,1536]{2,1,0:T(8,128)(2,1)S(1)}, u32[]{:S(2)}, u32[]{:S(2)}) async-start(bf16[16,8,1536]{2,1,0:T(8,128)(2,1)} %broadcast_in_dim.46), calls=%async_computation.12 | async-start | bytes 786432 | tf_op jit(solution)/shard_map/all_to_all | solution.py:673
  467.5 2.5 finish.1
  470.0 7.3 %all-to-all-done.9.r = bf16[16,8,1536]{2,1,0:T(8,128)(2,1)S(1)} async-done(((bf16[16,8,1536]{2,1,0:T(8,128)(2,1)}), bf16[16,8,1536]{2,1,0:T(8,128)(2,1)S(1)}, u32[]{:S(2)}, u32[]{:S(2)}) %all-to-all-start.9) | async-done | bytes 393248 | tf_op jit(solution)/shard_map/all_to_all | solution.py:673
  478.1 1.7 small_sum.1
  483.9 44.7 %all-gather.14.cloned.1.call-done = bf16[30976,128]{1,0:T(8,128)(2,1)} async-done(((bf16[1936,128]{1,0:T(8,128)(2,1)}), bf16[30976,128]{1,0:T(8,128)(2,1)}) %all-gather.14.cloned.1.call-update) | async-done | bytes 7929872 | tf_op jit(solution)/shard_map/all_gather | solution.py:677
  528.6 9.2 %unpack.1 = (f32[192,1536]{1,0:T(8,128)}, f32[192,1536]{1,0:T(8,128)}, f32[192,1536]{1,0:T(8,128)}, f32[192,1536]{1,0:T(8,128)}, f32[192,1536]{1,0:T(8,128)}, /*...) custom-call(s32[5]{0:T(128)} %stack.32.ids, bf16[16,1936,128]{2,1,0:T(8,128)(2,1)} %bitcast.82), custom_call_target="tpu_custom_call" | custom-call | flops 60000002048 | bytes 30000000 | tf_op jit(solution)/shard_map/unpack/pallas_call | solution.py:647
  (165 shorter events, 40.7 us)
Async XLA Ops:
  7.2 63.8 %all-gather.6.cloned.1.call-start = ((), (), s32[]{:S(2)}) async-start(), calls=%async_computation.13 | async-start | bytes 3538944 | tf_op jit(solution)/shard_map/all_gather | solution.py:677
  16.7 5.8 %copy-start.33 = (bf16[3]{0:T(256)(128)(2,1)S(1)}, bf16[3]{0:T(256)(128)(2,1)}, u32[]{:S(2)}) copy-start(bf16[3]{0:T(256)(128)(2,1)} %param.25) | copy-start | bytes 22
  16.7 54.3 %all-to-all-start = ((bf16[8,208,896]{2,1,0:T(8,128)(2,1)}), bf16[8,208,896]{2,1,0:T(8,128)(2,1)S(1)}, u32[]{:S(2)}, u32[]{:S(2)}) async-start(bf16[8,208,896]{2,1,0:T(8,128)(2,1)} %get-tuple-element.60), calls=%async_computation | async-start | bytes 5963776 | tf_op jit(solution)/shard_map/all_to_all | solution.py:673
  22.5 141.0 %all-gather.8.cloned.1.call-start = ((), (), s32[]{:S(2)}) async-start(), calls=%async_computation.14 | async-start | bytes 5308416 | tf_op jit(solution)/shard_map/all_gather | solution.py:677
  80.1 8.6 %copy-start.9 = (bf16[128,1536]{1,0:T(8,128)(2,1)S(1)}, bf16[128,1536]{1,0:T(8,128)(2,1)}, u32[]{:S(2)}) copy-start(bf16[128,1536]{1,0:T(8,128)(2,1)} %get-tuple-element.62.refs_0_.c_ref) | copy-start | bytes 1179652
  80.1 33.9 %copy-start.24 = (s32[32]{0:T(128)S(1)}, s32[32]{0:T(128)}, u32[]{:S(2)}) copy-start(s32[32]{0:T(128)} %bm_ref.5) | copy-start | bytes 388
  80.2 113.6 %all-gather.12.cloned.1.call-start = ((), (), s32[]{:S(2)}) async-start(), calls=%async_computation.16 | async-start | bytes 3342336 | tf_op jit(solution)/shard_map/all_gather | solution.py:677
  80.9 32.8 %all-to-all-start.1 = ((bf16[16,144,384]{2,1,0:T(8,128)(2,1)}), bf16[16,144,384]{2,1,0:T(8,128)(2,1)S(1)}, u32[]{:S(2)}, u32[]{:S(2)}) async-start(bf16[16,144,384]{2,1,0:T(8,128)(2,1)} %get-tuple-element.61), calls=%async_computation.1 | async-start | bytes 3538944 | tf_op jit(solution)/shard_map/all_to_all | solution.py:673
  88.7 26.7 %collective-permute-start = (bf16[128,1536]{1,0:T(8,128)(2,1)S(1)}, bf16[128,1536]{1,0:T(8,128)(2,1)S(1)}, u32[]{:S(2)}, u32[]{:S(2)}) collective-permute-start(bf16[128,1536]{1,0:T(8,128)(2,1)S(1)} %copy-done.9), channel_id=1, source_target_pairs={{0,2},{1,3},{2,4},{3,5},{4,6},{5,7},{6,0},{7,1},{8,10},{9,11},{10,... | collective-permute-start | bytes 1179656 | tf_op jit(solution)/shard_map/ppermute | solution.py:706
  129.9 17.3 %all-to-all-start.2 = ((bf16[16,128,128]{2,1,0:T(8,128)(2,1)}), bf16[16,128,128]{2,1,0:T(8,128)(2,1)S(1)}, u32[]{:S(2)}, u32[]{:S(2)}) async-start(bf16[16,128,128]{2,1,0:T(8,128)(2,1)} %get-tuple-element.63), calls=%async_computation.2 | async-start | bytes 1048576 | tf_op jit(solution)/shard_map/all_to_all | solution.py:673
  135.0 68.2 %all-gather.10.cloned.1.call-start = ((), (), s32[]{:S(2)}) async-start(), calls=%async_computation.15 | async-start | bytes 3538944 | tf_op jit(solution)/shard_map/all_gather | solution.py:677
  149.1 19.9 %copy-start.3 = (bf16[1024,256]{1,0:T(8,128)(2,1)}, bf16[1024,256]{1,0:T(8,128)(2,1)S(1)}, u32[]{:S(2)}) copy-start(bf16[1024,256]{1,0:T(8,128)(2,1)S(1)} %fusion.4.o) | copy-start | bytes 1572868
  163.5 10.0 %copy-start.17 = (bf16[128,1536]{1,0:T(8,128)(2,1)S(1)}, bf16[128,1536]{1,0:T(8,128)(2,1)}, u32[]{:S(2)}) copy-start(bf16[128,1536]{1,0:T(8,128)(2,1)} %copy-done.16) | copy-start | bytes 1179652
  169.0 90.7 %reduce-scatter.4.cloned.1.call-start = ((), (), s32[]{:S(2)}) async-start(), calls=%async_computation.17 | async-start | bytes 7077888 | tf_op jit(solution)/shard_map/reduce_scatter | solution.py:747
  169.1 11.2 %collective-permute-start.1 = (bf16[128,1536]{1,0:T(8,128)(2,1)S(1)}, bf16[128,1536]{1,0:T(8,128)(2,1)S(1)}, u32[]{:S(2)}, u32[]{:S(2)}) collective-permute-start(bf16[128,1536]{1,0:T(8,128)(2,1)S(1)} %copy-done.9), channel_id=1, source_target_pairs={{0,4},{1,5},{2,6},{3,7},{4,0},{5,1},{6,2},{7,3},{8,12},{9,13},{10,... | collective-permute-start | bytes 1179656 | tf_op jit(solution)/shard_map/ppermute | solution.py:706
  169.6 20.2 %collective-permute-start.2 = (bf16[128,1536]{1,0:T(8,128)(2,1)S(1)}, bf16[128,1536]{1,0:T(8,128)(2,1)S(1)}, u32[]{:S(2)}, u32[]{:S(2)}) collective-permute-start(bf16[128,1536]{1,0:T(8,128)(2,1)S(1)} %copy-done.9), channel_id=1, source_target_pairs={{0,6},{1,7},{2,0},{3,1},{4,2},{5,3},{6,4},{7,5},{8,14},{9,15},{10,... | collective-permute-start | bytes 1179656 | tf_op jit(solution)/shard_map/ppermute | solution.py:706
  172.2 20.0 %collective-permute-start.3 = (bf16[128,1536]{1,0:T(8,128)(2,1)S(1)}, bf16[128,1536]{1,0:T(8,128)(2,1)S(1)}, u32[]{:S(2)}, u32[]{:S(2)}) collective-permute-start(bf16[128,1536]{1,0:T(8,128)(2,1)S(1)} %copy-done.9), channel_id=1, source_target_pairs={{0,1},{1,0},{2,3},{3,2},{4,5},{5,4},{6,7},{7,6},{8,9},{9,8},{10,11... | collective-permute-start | bytes 1179656 | tf_op jit(solution)/shard_map/ppermute | solution.py:708
  173.5 18.7 %collective-permute-start.4 = (bf16[128,1536]{1,0:T(8,128)(2,1)S(1)}, bf16[128,1536]{1,0:T(8,128)(2,1)S(1)}, u32[]{:S(2)}, u32[]{:S(2)}) collective-permute-start(bf16[128,1536]{1,0:T(8,128)(2,1)S(1)} %copy-done.17), channel_id=1, source_target_pairs={{0,1},{1,0},{2,3},{3,2},{4,5},{5,4},{6,7},{7,6},{8,9},{9,8},{10,11... | collective-permute-start | bytes 1179656 | tf_op jit(solution)/shard_map/ppermute | solution.py:708
  180.2 13.5 %copy-start.18 = (bf16[128,1536]{1,0:T(8,128)(2,1)}, bf16[128,1536]{1,0:T(8,128)(2,1)S(1)}, u32[]{:S(2)}) copy-start(bf16[128,1536]{1,0:T(8,128)(2,1)S(1)} %collective-permute-done.1.refs_2_) | copy-start | bytes 1179652
  180.2 12.0 %collective-permute-start.5 = (bf16[128,1536]{1,0:T(8,128)(2,1)S(1)}, bf16[128,1536]{1,0:T(8,128)(2,1)S(1)}, u32[]{:S(2)}, u32[]{:S(2)}) collective-permute-start(bf16[128,1536]{1,0:T(8,128)(2,1)S(1)} %collective-permute-done.1.refs_2_), channel_id=1, source_target_pairs={{0,1},{1,0},{2,3},{3,2},{4,5},{5,4},{6,7},{7,6},{8,9},{9,8},{10,11... | collective-permute-start | bytes 1179656 | tf_op jit(solution)/shard_map/ppermute | solution.py:708
  189.9 3.9 copy-start.19
  189.9 3.9 collective-permute-start.6
  218.3 217.6 %reduce-scatter.6.cloned.1.call-start = ((), (), s32[]{:S(2)}) async-start(), calls=%async_computation.18 | async-start | bytes 5013504 | tf_op jit(solution)/shard_map/reduce_scatter | solution.py:779
  265.7 14.1 %copy-start.2 = (f32[1024,256]{1,0:T(8,128)S(1)}, f32[1024,256]{1,0:T(8,128)}, u32[]{:S(2)}) copy-start(f32[1024,256]{1,0:T(8,128)} %open.1) | copy-start | bytes 3145732
  281.1 36.8 %copy-start = (bf16[8,2,128,128]{3,2,1,0:T(8,128)(2,1)}, bf16[8,2,128,128]{3,2,1,0:T(8,128)(2,1)S(1)}, u32[]{:S(2)}) copy-start(bf16[8,2,128,128]{3,2,1,0:T(8,128)(2,1)S(1)} %copy.62) | copy-start | bytes 1572868
  354.7 72.1 %all-to-all-start.7 = ((bf16[128,80,128]{2,1,0:T(8,128)(2,1)}), bf16[128,80,128]{2,1,0:T(8,128)(2,1)S(1)}, u32[]{:S(2)}, u32[]{:S(2)}) async-start(bf16[128,80,128]{2,1,0:T(8,128)(2,1)} %bitcast.69), calls=%async_computation.8 | async-start | bytes 5242880 | tf_op jit(solution)/shard_map/all_to_all | solution.py:673
  364.4 92.8 %reduce-scatter.8.cloned.1.call-start = ((), (), s32[]{:S(2)}) async-start(), calls=%async_computation.19 | async-start | bytes 3981312 | tf_op jit(solution)/shard_map/reduce_scatter | solution.py:818
  377.0 32.2 %collective-permute-start.9 = (bf16[128,1536]{1,0:T(8,128)(2,1)S(1)}, bf16[128,1536]{1,0:T(8,128)(2,1)S(1)}, u32[]{:S(2)}, u32[]{:S(2)}) collective-permute-start(bf16[128,1536]{1,0:T(8,128)(2,1)S(1)} %copy-done.4), channel_id=1, source_target_pairs={{0,6},{1,7},{2,0},{3,1},{4,2},{5,3},{6,4},{7,5},{8,14},{9,15},{10,... | collective-permute-start | bytes 1179656 | tf_op jit(solution)/shard_map/ppermute | solution.py:770
  379.6 31.1 %collective-permute-start.8 = (bf16[128,1536]{1,0:T(8,128)(2,1)S(1)}, bf16[128,1536]{1,0:T(8,128)(2,1)S(1)}, u32[]{:S(2)}, u32[]{:S(2)}) collective-permute-start(bf16[128,1536]{1,0:T(8,128)(2,1)S(1)} %copy-done.4), channel_id=1, source_target_pairs={{0,4},{1,5},{2,6},{3,7},{4,0},{5,1},{6,2},{7,3},{8,12},{9,13},{10,... | collective-permute-start | bytes 1179656 | tf_op jit(solution)/shard_map/ppermute | solution.py:770
  380.2 37.1 %collective-permute-start.7 = (bf16[128,1536]{1,0:T(8,128)(2,1)S(1)}, bf16[128,1536]{1,0:T(8,128)(2,1)}, u32[]{:S(2)}, u32[]{:S(2)}) collective-permute-start(bf16[128,1536]{1,0:T(8,128)(2,1)S(1)} %copy-done.4), channel_id=1, source_target_pairs={{0,2},{1,3},{2,4},{3,5},{4,6},{5,7},{6,0},{7,1},{8,10},{9,11},{10,... | collective-permute-start | bytes 1179656 | tf_op jit(solution)/shard_map/ppermute | solution.py:770
  409.1 10.0 %copy-start.10 = (bf16[128,1536]{1,0:T(8,128)(2,1)}, bf16[128,1536]{1,0:T(8,128)(2,1)S(1)}, u32[]{:S(2)}) copy-start(bf16[128,1536]{1,0:T(8,128)(2,1)S(1)} %collective-permute-done.9.refs_0_) | copy-start | bytes 1179652
  417.3 3.4 collective-permute-start.10
  418.6 2.3 collective-permute-start.11
  418.6 3.5 collective-permute-start.12
  419.1 3.0 collective-permute-start.13
  428.3 22.2 %all-to-all-start.8 = ((bf16[16,48,384]{2,1,0:T(8,128)(2,1)}), bf16[16,48,384]{2,1,0:T(8,128)(2,1)S(1)}, u32[]{:S(2)}, u32[]{:S(2)}) async-start(bf16[16,48,384]{2,1,0:T(8,128)(2,1)} %after.10), calls=%async_computation.9 | async-start | bytes 1179648 | tf_op jit(solution)/shard_map/all_to_all | solution.py:673
  435.9 92.7 %all-gather.14.cloned.1.call-start = ((), (), s32[]{:S(2)}) async-start(), calls=%async_computation.20 | async-start | bytes 8425472 | tf_op jit(solution)/shard_map/all_gather | solution.py:677
  437.6 10.9 %collective-permute-start.14 = (bf16[96,128]{1,0:T(8,128)(2,1)}, bf16[96,128]{1,0:T(8,128)(2,1)S(1)}, u32[]{:S(2)}, u32[]{:S(2)}) collective-permute-start(bf16[96,128]{1,0:T(8,128)(2,1)} %get-tuple-element.86), channel_id=1, source_target_pairs={{0,1},{1,2},{2,3},{3,4},{4,5},{5,6},{6,7},{7,0},{8,9},{9,10},{10,1... | collective-permute-start | bytes 73736 | tf_op jit(solution)/shard_map/ppermute | solution.py:807
  444.1 5.2 collective-permute-start.15
  444.1 6.4 %collective-permute-start.16 = (bf16[96,128]{1,0:T(8,128)(2,1)}, bf16[96,128]{1,0:T(8,128)(2,1)S(1)}, u32[]{:S(2)}, u32[]{:S(2)}) collective-permute-start(bf16[96,128]{1,0:T(8,128)(2,1)} %get-tuple-element.88), channel_id=1, source_target_pairs={{0,3},{1,4},{2,5},{3,6},{4,7},{5,0},{6,1},{7,2},{8,11},{9,12},{10,... | collective-permute-start | bytes 73736 | tf_op jit(solution)/shard_map/ppermute | solution.py:807
  446.2 4.8 collective-permute-start.17
  447.4 5.0 collective-permute-start.18
  448.5 4.7 copy-start.26
  448.5 3.9 collective-permute-start.19
  449.3 3.8 collective-permute-start.20
  453.8 12.8 %copy-start.5 = (f32[128,1536]{1,0:T(8,128)S(1)}, f32[128,1536]{1,0:T(8,128)}, u32[]{:S(2)}) copy-start(f32[128,1536]{1,0:T(8,128)} %get-tuple-element.68.h_ref) | copy-start | bytes 2359300
  453.8 12.8 %copy-start.8 = (bf16[128,3072]{1,0:T(8,128)(2,1)S(1)}, bf16[128,3072]{1,0:T(8,128)(2,1)}, u32[]{:S(2)}) copy-start(bf16[128,3072]{1,0:T(8,128)(2,1)} %reduce-scatter.4.cloned.1.call-done.dn2_r) | copy-start | bytes 2359300
  459.7 17.6 %all-to-all-start.9 = ((bf16[16,8,1536]{2,1,0:T(8,128)(2,1)}), bf16[16,8,1536]{2,1,0:T(8,128)(2,1)S(1)}, u32[]{:S(2)}, u32[]{:S(2)}) async-start(bf16[16,8,1536]{2,1,0:T(8,128)(2,1)} %broadcast_in_dim.46), calls=%async_computation.12 | async-start | bytes 786432 | tf_op jit(solution)/shard_map/all_to_all | solution.py:673
  (21 other events, 31.5 us)
Sparse Core Ops, SparseCore 0:
  16.8 47.2 all-gather.5
  80.3 41.5 all-gather.7
  124.1 49.3 all-gather.11
  175.6 27.4 all-gather.9
  218.4 41.2 reduce-scatter.3
  265.8 88.8 reduce-scatter.5
  376.1 57.9 reduce-scatter.7
  457.3 71.2 all-gather.13
